TPU v7x, 32 devices: a whole 2x2x4 slice. The times are simulated.
32 devices in a mesh: dp: 4 (over y, x), seq: 8 (over z, core).
Axes of the slice: x: 2, y: 2, z: 4, core: 2. Of those that a mesh axis runs over, the one named last changes fastest.
Arguments:
- tokens: bfloat16 [6144, 2048], P(('dp', 'seq')), may hold values from -6 to 6
- positions: int32 [6144], P(('dp', 'seq')), may hold values from 0 to 1439, as said below
- cotangent: bfloat16 [6144, 2048], P(('dp', 'seq')), may hold values from -6 to 6
- norm_in_gain: float32 [2048], P(('dp', 'seq')), may hold values from 0.1 to 1.9
- q_down: float32 [2048, 1024], P(('dp', 'seq')), may hold values from -0.125 to 0.125
- q_gain: float32 [1024], P(('dp', 'seq')), may hold values from 0.1 to 1.9
- q_up: float32 [1024, 4096], P(('dp', 'seq')), may hold values from -0.1875 to 0.1875
- key_proj: float32 [2048, 256], P(('dp', 'seq')), may hold values from -0.125 to 0.125
- value_proj: float32 [2048, 256], P(('dp', 'seq')), may hold values from -0.125 to 0.125
- out_proj: float32 [4096, 2048], P(('dp', 'seq')), may hold values from -1 to 1
- norm_mid_gain: float32 [2048], P(('dp', 'seq')), may hold values from 0.1 to 1.9
- w_gate: float32 [2048, 5632], P(('dp', 'seq')), may hold values from -0.125 to 0.125
- w_up: float32 [2048, 5632], P(('dp', 'seq')), may hold values from -0.125 to 0.125
- w_down: float32 [5632, 2048], P(('dp', 'seq')), may hold values from -0.078125 to 0.078125
Outputs:
- output: bfloat16 [6144, 2048], P(('dp', 'seq'))
- grad_tokens: bfloat16 [6144, 2048], P(('dp', 'seq'))
- grad_norm_in_gain: float32 [2048], P(('dp', 'seq'))
- grad_q_down: float32 [2048, 1024], P(('dp', 'seq'))
- grad_q_gain: float32 [1024], P(('dp', 'seq'))
- grad_q_up: float32 [1024, 4096], P(('dp', 'seq'))
- grad_key_proj: float32 [2048, 256], P(('dp', 'seq'))
- grad_value_proj: float32 [2048, 256], P(('dp', 'seq'))
- grad_out_proj: float32 [4096, 2048], P(('dp', 'seq'))
- grad_norm_mid_gain: float32 [2048], P(('dp', 'seq'))
- grad_w_gate: float32 [2048, 5632], P(('dp', 'seq'))
- grad_w_up: float32 [2048, 5632], P(('dp', 'seq'))
- grad_w_down: float32 [5632, 2048], P(('dp', 'seq'))
Inputs may be any that keep to these rules, and one draw needn't show every extreme that they name: `positions`: within each index of dp the 1536 tokens hold three whole sequences laid end to end; each entry counts from 0 at its sequence's first token. The longest of them has 1440 tokens and covers tokens of the first and of the last device of seq.
All inputs are finite; a program needn't handle non-finite values.
Results may differ from a plain program's by a relative error of at most 0.03.
Values may be sent and summed in bfloat16 or wider, within the bound.
A program may use at most 512 MiB of HBM per device.

v0:
```python
import math

import jax
import jax.numpy as jnp
from jax import lax
from jax.sharding import PartitionSpec as P

HEADS = 16
HEAD_DIM = 256


epsilon = 1e-05
rope_base = 10000.0
masked_score = -1e30


def rms_scale(values):
    return lax.rsqrt(jnp.mean(values * values, axis=-1, keepdims=True) + epsilon)


def rotary(values, places, sign):
    half = values.shape[-1] // 2
    freqs = rope_base ** (-(2.0 * jnp.arange(half).astype(jnp.float32)) / values.shape[-1])
    angles = places.astype(jnp.float32)[:, None] * freqs[None, :]
    cosine = jnp.cos(angles)[:, None, :]
    sine = jnp.sin(angles)[:, None, :]
    first = values[..., :half]
    second = values[..., half:]
    return jnp.concatenate(
        [first * cosine - sign * second * sine, sign * first * sine + second * cosine], axis=-1
    )


def norm_backward(inputs, scale, gain, grad_out):
    weighted = gain * grad_out
    grad_in = scale * weighted - inputs * scale * scale * scale * jnp.mean(
        weighted * inputs, axis=-1, keepdims=True
    )
    grad_gain = jnp.sum(grad_out * inputs * scale, axis=0)
    return (grad_in, grad_gain)


def add_rows(total, block, start):
    current = lax.dynamic_slice_in_dim(total, start, block.shape[0], 0)
    return lax.dynamic_update_slice_in_dim(total, current + block, start, 0)


def local(
    tokens,
    positions,
    cotangent,
    norm_in_gain,
    q_down,
    q_gain,
    q_up,
    key_proj,
    value_proj,
    out_proj,
    norm_mid_gain,
    w_gate,
    w_up,
    w_down,
):
    width = tokens.shape[0]
    scale = 1.0 / math.sqrt(HEAD_DIM)
    attention_set = (
        lax.all_gather(norm_in_gain.astype(jnp.bfloat16), ("dp", "seq"), axis=0, tiled=True),
        lax.all_gather(q_down.astype(jnp.bfloat16), ("dp", "seq"), axis=0, tiled=True),
        lax.all_gather(q_gain.astype(jnp.bfloat16), ("dp", "seq"), axis=0, tiled=True),
        lax.all_gather(q_up.astype(jnp.bfloat16), ("dp", "seq"), axis=0, tiled=True),
        lax.all_gather(key_proj.astype(jnp.bfloat16), ("dp", "seq"), axis=0, tiled=True),
        lax.all_gather(value_proj.astype(jnp.bfloat16), ("dp", "seq"), axis=0, tiled=True),
        lax.all_gather(out_proj.astype(jnp.bfloat16), ("dp", "seq"), axis=0, tiled=True),
    )
    feed_set = (
        lax.all_gather(norm_mid_gain.astype(jnp.bfloat16), ("dp", "seq"), axis=0, tiled=True),
        lax.all_gather(w_gate.astype(jnp.bfloat16), ("dp", "seq"), axis=0, tiled=True),
        lax.all_gather(w_up.astype(jnp.bfloat16), ("dp", "seq"), axis=0, tiled=True),
        lax.all_gather(w_down.astype(jnp.bfloat16), ("dp", "seq"), axis=0, tiled=True),
    )
    in_gain = attention_set[0].astype(jnp.float32)
    query_gain = attention_set[2].astype(jnp.float32)
    inputs = tokens.astype(jnp.float32)
    in_scale = rms_scale(inputs)
    normed = (inputs * in_scale * in_gain).astype(jnp.bfloat16)
    compressed = jnp.dot(normed, attention_set[1], preferred_element_type=jnp.float32)
    query_scale = rms_scale(compressed)
    compressed_normed = (compressed * query_scale * query_gain).astype(jnp.bfloat16)
    queries_raw = jnp.dot(
        compressed_normed, attention_set[3], preferred_element_type=jnp.float32
    ).reshape(width, HEADS, HEAD_DIM)
    queries = rotary(queries_raw, positions, 1.0).astype(jnp.bfloat16)
    keys_raw = jnp.dot(normed, attention_set[4], preferred_element_type=jnp.float32)
    keys = rotary(keys_raw[:, None, :], positions, 1.0)[:, 0, :].astype(jnp.bfloat16)
    values = jnp.dot(normed, attention_set[5], preferred_element_type=jnp.float32).astype(
        jnp.bfloat16
    )
    query_index = lax.axis_index("seq") * width + jnp.arange(width, dtype=jnp.int32)
    first_index = query_index - positions

    def visibility(key_start):
        key_index = key_start + jnp.arange(width, dtype=jnp.int32)
        seen = (key_index[None, :] >= first_index[:, None]) & (
            key_index[None, :] <= query_index[:, None]
        )
        return seen[:, None, :]

    start_state = (
        jnp.full((width, HEADS), masked_score, jnp.float32),
        jnp.zeros((width, HEADS), jnp.float32),
        jnp.zeros((width, HEADS, HEAD_DIM), jnp.float32),
    )
    carry = start_state
    piece = (
        lax.all_gather(keys, "seq", axis=0, tiled=True),
        lax.all_gather(values, "seq", axis=0, tiled=True),
    )
    blocks = piece[0].shape[0] // width
    key_blocks = piece[0].reshape(blocks, width, HEAD_DIM)
    value_blocks = piece[1].reshape(blocks, width, HEAD_DIM)

    def forward_one_block(state, item):
        key_block, value_block, number = item
        key_start = number * width
        top, total, accum = state
        seen = visibility(key_start)
        scores = (
            jnp.einsum("thd,kd->thk", queries, key_block, preferred_element_type=jnp.float32)
            * scale
        )
        scores = jnp.where(seen, scores, masked_score)
        new_top = jnp.maximum(top, jnp.max(scores, axis=-1))
        weights = jnp.where(seen, jnp.exp(scores - new_top[..., None]), 0.0)
        decay = jnp.exp(top - new_top)
        total = total * decay + jnp.sum(weights, axis=-1)
        accum = accum * decay[..., None] + jnp.einsum(
            "thk,kd->thd",
            weights.astype(jnp.bfloat16),
            value_block,
            preferred_element_type=jnp.float32,
        )
        state = (new_top, total, accum)
        return (state, None)

    carry, _ = lax.scan(
        forward_one_block, carry, (key_blocks, value_blocks, jnp.arange(blocks, dtype=jnp.int32))
    )
    top, total, accum = carry
    attended_full = accum / total[..., None]
    log_total = top + jnp.log(total)
    attended = attended_full.reshape(width, HEADS * HEAD_DIM).astype(jnp.bfloat16)
    middle = inputs + jnp.dot(attended, attention_set[6], preferred_element_type=jnp.float32)
    mid_gain = feed_set[0].astype(jnp.float32)
    mid_scale = rms_scale(middle)
    normed_mid = (middle * mid_scale * mid_gain).astype(jnp.bfloat16)
    gate = jnp.dot(normed_mid, feed_set[1], preferred_element_type=jnp.float32)
    upper = jnp.dot(normed_mid, feed_set[2], preferred_element_type=jnp.float32)
    sigmoid_gate = jax.nn.sigmoid(gate)
    silu_gate = gate * sigmoid_gate
    hidden = (silu_gate * upper).astype(jnp.bfloat16)
    output = (middle + jnp.dot(hidden, feed_set[3], preferred_element_type=jnp.float32)).astype(
        jnp.bfloat16
    )
    feed_back = (
        lax.all_gather(norm_mid_gain.astype(jnp.bfloat16), ("dp", "seq"), axis=0, tiled=True),
        lax.all_gather(w_gate.astype(jnp.bfloat16), ("dp", "seq"), axis=0, tiled=True),
        lax.all_gather(w_up.astype(jnp.bfloat16), ("dp", "seq"), axis=0, tiled=True),
        lax.all_gather(w_down.astype(jnp.bfloat16), ("dp", "seq"), axis=0, tiled=True),
    )
    grad_out_full = cotangent.astype(jnp.float32)
    grad_down = jnp.einsum("tf,td->fd", hidden, cotangent, preferred_element_type=jnp.float32)
    grad_hidden = jnp.einsum(
        "td,fd->tf", cotangent, feed_back[3], preferred_element_type=jnp.float32
    )
    grad_gate = (grad_hidden * upper * sigmoid_gate * (1.0 + gate * (1.0 - sigmoid_gate))).astype(
        jnp.bfloat16
    )
    grad_upper = (grad_hidden * silu_gate).astype(jnp.bfloat16)
    grad_gate_weight = jnp.einsum(
        "td,tf->df", normed_mid, grad_gate, preferred_element_type=jnp.float32
    )
    grad_up_weight = jnp.einsum(
        "td,tf->df", normed_mid, grad_upper, preferred_element_type=jnp.float32
    )
    grad_normed_mid = jnp.einsum(
        "tf,df->td", grad_gate, feed_back[1], preferred_element_type=jnp.float32
    ) + jnp.einsum("tf,df->td", grad_upper, feed_back[2], preferred_element_type=jnp.float32)
    grad_mid_norm, grad_mid_gain = norm_backward(
        middle, mid_scale, feed_back[0].astype(jnp.float32), grad_normed_mid
    )
    grad_middle = grad_out_full + grad_mid_norm
    feed_grads = (
        lax.psum_scatter(grad_mid_gain, ("dp", "seq"), scatter_dimension=0, tiled=True),
        lax.psum_scatter(grad_gate_weight, ("dp", "seq"), scatter_dimension=0, tiled=True),
        lax.psum_scatter(grad_up_weight, ("dp", "seq"), scatter_dimension=0, tiled=True),
        lax.psum_scatter(grad_down, ("dp", "seq"), scatter_dimension=0, tiled=True),
    )
    attention_back = (
        lax.all_gather(norm_in_gain.astype(jnp.bfloat16), ("dp", "seq"), axis=0, tiled=True),
        lax.all_gather(q_down.astype(jnp.bfloat16), ("dp", "seq"), axis=0, tiled=True),
        lax.all_gather(q_gain.astype(jnp.bfloat16), ("dp", "seq"), axis=0, tiled=True),
        lax.all_gather(q_up.astype(jnp.bfloat16), ("dp", "seq"), axis=0, tiled=True),
        lax.all_gather(key_proj.astype(jnp.bfloat16), ("dp", "seq"), axis=0, tiled=True),
        lax.all_gather(value_proj.astype(jnp.bfloat16), ("dp", "seq"), axis=0, tiled=True),
        lax.all_gather(out_proj.astype(jnp.bfloat16), ("dp", "seq"), axis=0, tiled=True),
    )
    branch_grad = grad_middle.astype(jnp.bfloat16)
    grad_output_weight = jnp.einsum(
        "ta,td->ad", attended, branch_grad, preferred_element_type=jnp.float32
    )
    grad_attended = (
        jnp.einsum("td,ad->ta", branch_grad, attention_back[6], preferred_element_type=jnp.float32)
        .reshape(width, HEADS, HEAD_DIM)
        .astype(jnp.bfloat16)
    )
    delta = jnp.sum(grad_attended.astype(jnp.float32) * attended_full, axis=-1)
    group_rows = width * lax.axis_size("seq")
    back_state = (
        jnp.zeros((width, HEADS, HEAD_DIM), jnp.float32),
        jnp.zeros((group_rows, HEAD_DIM), jnp.float32),
        jnp.zeros((group_rows, HEAD_DIM), jnp.float32),
    )
    carry = back_state
    piece = (
        lax.all_gather(keys, "seq", axis=0, tiled=True),
        lax.all_gather(values, "seq", axis=0, tiled=True),
    )
    blocks = piece[0].shape[0] // width
    key_blocks = piece[0].reshape(blocks, width, HEAD_DIM)
    value_blocks = piece[1].reshape(blocks, width, HEAD_DIM)

    def backward_one_block(state, item):
        key_block, value_block, number = item
        key_start = number * width
        grad_query, grad_keys, grad_values = state
        seen = visibility(key_start)
        scores = (
            jnp.einsum("thd,kd->thk", queries, key_block, preferred_element_type=jnp.float32)
            * scale
        )
        probs = jnp.where(seen, jnp.exp(scores - log_total[..., None]), 0.0)
        grad_value_block = jnp.einsum(
            "thk,thd->kd",
            probs.astype(jnp.bfloat16),
            grad_attended,
            preferred_element_type=jnp.float32,
        )
        grad_probs = jnp.einsum(
            "thd,kd->thk", grad_attended, value_block, preferred_element_type=jnp.float32
        )
        grad_scores = (probs * (grad_probs - delta[..., None]) * scale).astype(jnp.bfloat16)
        grad_query = grad_query + jnp.einsum(
            "thk,kd->thd", grad_scores, key_block, preferred_element_type=jnp.float32
        )
        grad_key_block = jnp.einsum(
            "thk,thd->kd", grad_scores, queries, preferred_element_type=jnp.float32
        )
        state = (
            grad_query,
            add_rows(grad_keys, grad_key_block, key_start),
            add_rows(grad_values, grad_value_block, key_start),
        )
        return (state, None)

    carry, _ = lax.scan(
        backward_one_block, carry, (key_blocks, value_blocks, jnp.arange(blocks, dtype=jnp.int32))
    )
    grad_query, grad_keys, grad_values = carry
    local_key_grad, local_value_grad = (
        lax.psum_scatter(
            grad_keys.astype(jnp.bfloat16), "seq", scatter_dimension=0, tiled=True
        ).astype(jnp.float32),
        lax.psum_scatter(
            grad_values.astype(jnp.bfloat16), "seq", scatter_dimension=0, tiled=True
        ).astype(jnp.float32),
    )
    grad_key_pre = rotary(local_key_grad[:, None, :], positions, -1.0)[:, 0, :].astype(jnp.bfloat16)
    grad_value_pre = local_value_grad.astype(jnp.bfloat16)
    grad_query_pre = (
        rotary(grad_query, positions, -1.0).reshape(width, HEADS * HEAD_DIM).astype(jnp.bfloat16)
    )
    grad_up_query = jnp.einsum(
        "tr,ta->ra", compressed_normed, grad_query_pre, preferred_element_type=jnp.float32
    )
    grad_compressed_normed = jnp.einsum(
        "ta,ra->tr", grad_query_pre, attention_back[3], preferred_element_type=jnp.float32
    )
    grad_compressed, grad_query_gain = norm_backward(
        compressed, query_scale, attention_back[2].astype(jnp.float32), grad_compressed_normed
    )
    grad_compressed = grad_compressed.astype(jnp.bfloat16)
    grad_down_weight = jnp.einsum(
        "td,tr->dr", normed, grad_compressed, preferred_element_type=jnp.float32
    )
    grad_key_weight = jnp.einsum(
        "td,te->de", normed, grad_key_pre, preferred_element_type=jnp.float32
    )
    grad_value_weight = jnp.einsum(
        "td,te->de", normed, grad_value_pre, preferred_element_type=jnp.float32
    )
    grad_normed = jnp.einsum(
        "tr,dr->td", grad_compressed, attention_back[1], preferred_element_type=jnp.float32
    )
    grad_normed = grad_normed + jnp.einsum(
        "te,de->td", grad_key_pre, attention_back[4], preferred_element_type=jnp.float32
    )
    grad_normed = grad_normed + jnp.einsum(
        "te,de->td", grad_value_pre, attention_back[5], preferred_element_type=jnp.float32
    )
    grad_in_norm, grad_in_gain = norm_backward(
        inputs, in_scale, attention_back[0].astype(jnp.float32), grad_normed
    )
    grad_tokens = (grad_middle + grad_in_norm).astype(jnp.bfloat16)
    attention_grads = (
        lax.psum_scatter(grad_in_gain, ("dp", "seq"), scatter_dimension=0, tiled=True),
        lax.psum_scatter(grad_down_weight, ("dp", "seq"), scatter_dimension=0, tiled=True),
        lax.psum_scatter(grad_query_gain, ("dp", "seq"), scatter_dimension=0, tiled=True),
        lax.psum_scatter(grad_up_query, ("dp", "seq"), scatter_dimension=0, tiled=True),
        lax.psum_scatter(grad_key_weight, ("dp", "seq"), scatter_dimension=0, tiled=True),
        lax.psum_scatter(grad_value_weight, ("dp", "seq"), scatter_dimension=0, tiled=True),
        lax.psum_scatter(grad_output_weight, ("dp", "seq"), scatter_dimension=0, tiled=True),
    )
    return (
        output,
        grad_tokens,
        attention_grads[0],
        attention_grads[1],
        attention_grads[2],
        attention_grads[3],
        attention_grads[4],
        attention_grads[5],
        attention_grads[6],
        feed_grads[0],
        feed_grads[1],
        feed_grads[2],
        feed_grads[3],
    )


def solution(mesh):
    return jax.shard_map(
        local,
        mesh=mesh,
        in_specs=(
            P(("dp", "seq"), None),
            P(("dp", "seq")),
            P(("dp", "seq"), None),
            P(("dp", "seq")),
            P(("dp", "seq"), None),
            P(("dp", "seq")),
            P(("dp", "seq"), None),
            P(("dp", "seq"), None),
            P(("dp", "seq"), None),
            P(("dp", "seq"), None),
            P(("dp", "seq")),
            P(("dp", "seq"), None),
            P(("dp", "seq"), None),
            P(("dp", "seq"), None),
        ),
        out_specs=(
            P(("dp", "seq"), None),
            P(("dp", "seq"), None),
            P(("dp", "seq")),
            P(("dp", "seq"), None),
            P(("dp", "seq")),
            P(("dp", "seq"), None),
            P(("dp", "seq"), None),
            P(("dp", "seq"), None),
            P(("dp", "seq"), None),
            P(("dp", "seq")),
            P(("dp", "seq"), None),
            P(("dp", "seq"), None),
            P(("dp", "seq"), None),
        ),
        check_vma=False,
    )
```

profile of v0, /device:TPU:0, one launch (start us, length us, event | category | flops | bytes accessed | tf_op | source)
XLA Modules:
  0.0 3555.7 jit_solution(8153680340996839998)
XLA Ops:
  20.9 42.2 %all-reduce.7 = (bf16[2048]{0:T(1024)(128)(2,1)S(1)}, bf16[1024]{0:T(1024)(128)(2,1)S(1)}, bf16[2048]{0:T(1024)(128)(2,1)S(1)}) all-reduce(bf16[2048]{0:T(1024)(128)(2,1)S(1)} %dynamic-update-slice, bf16[1024]{0:T(1024)(128)(2,1)S(1)} %dynamic-update-slice.1, ...), channel_id=1, replica_groups=mesh['dp'=4,'seq'=8] {'dp','seq'}, use_global_device_ids=true, to_apply=%add | all-reduce | flops 5120 | bytes 20480
  64.5 3.9 all-gather.10.cloned.1.call-done
  70.5 54.2 %all-gather.16.cloned.1.call-done = bf16[2048,256]{1,0:T(8,128)(2,1)} async-done(((bf16[64,256]{1,0:T(8,128)(2,1)}), bf16[2048,256]{1,0:T(8,128)(2,1)}) %all-gather.16.cloned.1.call-update) | async-done | bytes 1048592 | tf_op jit(solution)/shard_map/all_gather | solution.py:72
  126.3 17.2 all-gather
  143.5 17.4 all_gather.59
  161.0 28.6 all-gather.12.cloned.1.call-done
  189.6 3.3 multiply_reduce_fusion.6
  192.9 76.0 %all-gather.14.cloned.1.call-done = bf16[1024,4096]{1,0:T(8,128)(2,1)} async-done(((bf16[32,4096]{1,0:T(8,128)(2,1)}), bf16[1024,4096]{1,0:T(8,128)(2,1)}) %all-gather.14.cloned.1.call-update) | async-done | bytes 8388624 | tf_op jit(solution)/shard_map/all_gather | solution.py:70
  269.0 5.2 fusion.86
  276.7 116.9 %while.30 = (s32[]{:T(128)}, f32[192,16]{0,1:T(8,128)S(1)}, f32[192,16]{0,1:T(8,128)S(1)}, f32[192,16,256]{2,1,0:T(8,128)}, s32[8]{0:T(128)S(1)}, /*index=5*/s32...) while((s32[]{:T(128)}, f32[192,16]{0,1:T(8,128)S(1)}, ...), condition=%wide.region_5.6_spmd.clone, body=%wide.region_2.5_spmd.clone.sunk | while | flops 611773824 | bytes 18214840 | solution.py:145
  278.3 3.2 fusion.172
  286.8 3.7 fusion.175
  291.9 3.2 fusion.172
  300.4 4.8 fusion.175
  315.1 4.7 fusion.175
  321.2 3.2 fusion.172
  329.7 5.1 fusion.175
  336.2 3.2 fusion.172
  344.8 4.7 fusion.175
  350.8 3.3 fusion.172
  359.4 4.7 fusion.175
  365.4 3.3 fusion.172
  374.0 4.7 fusion.175
  380.1 3.2 fusion.172
  388.9 4.7 fusion.175
  398.1 8.2 multiply_reduce_fusion.3
  407.7 124.7 %all-gather.20.cloned.1.call-done = bf16[2048,5632]{1,0:T(8,128)(2,1)} async-done(((bf16[64,5632]{1,0:T(8,128)(2,1)}), bf16[2048,5632]{1,0:T(8,128)(2,1)}) %all-gather.20.cloned.1.call-update) | async-done | bytes 23068688 | tf_op jit(solution)/shard_map/all_gather | solution.py:77
  532.3 12.0 fusion.97
  544.3 134.2 %all-gather.22.cloned.1.call-done = bf16[2048,5632]{1,0:T(8,128)(2,1)} async-done(((bf16[64,5632]{1,0:T(8,128)(2,1)}), bf16[2048,5632]{1,0:T(8,128)(2,1)}) %all-gather.22.cloned.1.call-update) | async-done | bytes 23068688 | tf_op jit(solution)/shard_map/all_gather | solution.py:78
  678.6 12.2 fusion.98
  690.7 134.1 %all-gather.24.cloned.1.call-done = bf16[5632,2048]{1,0:T(8,128)(2,1)} async-done(((bf16[176,2048]{1,0:T(8,128)(2,1)}), bf16[5632,2048]{1,0:T(8,128)(2,1)}) %all-gather.24.cloned.1.call-update) | async-done | bytes 23068688 | tf_op jit(solution)/shard_map/all_gather | solution.py:79
  824.8 16.0 multiply_convert_fusion
  840.8 14.4 fusion.99
  855.2 14.6 multiply_reduce_fusion.1
  872.5 13.2 convolution_convert_fusion
  894.1 141.0 %while.31 = (s32[]{:T(128)}, f32[192,16,256]{2,1,0:T(8,128)}, f32[1536,256]{1,0:T(8,128)}, f32[1536,256]{1,0:T(8,128)}, s32[8]{0:T(128)S(1)}, /*index=5*/s32[192...) while((s32[]{:T(128)}, f32[192,16,256]{2,1,0:T(8,128)}, ...), condition=%wide.region_10.11_spmd.clone, body=%wide.region_9.10_spmd.clone.sunk | while | flops 1518219648 | bytes 52351060 | solution.py:265
  902.0 3.7 select_add_fusion.2
  918.8 4.7 select_add_fusion.2
  936.5 4.7 select_add_fusion.2
  954.2 4.7 select_add_fusion.2
  972.0 4.7 select_add_fusion.2
  989.7 4.7 select_add_fusion.2
  1007.4 4.7 select_add_fusion.2
  1025.1 4.7 select_add_fusion.2
  1038.7 28.6 reduce-scatter.11.cloned.1.call-done
  1070.7 29.2 reduce-scatter.13.cloned.1.call-done
  1099.9 3.3 fusion.87
  1105.9 7.1 multiply_reduce_fusion.4
  1114.1 4.8 fusion.90
  1119.3 8.9 fusion.85
  1129.6 14.9 fusion.63
  1145.6 19.5 fusion.101
  1165.1 19.5 fusion.102
  1185.8 19.5 fusion.103
  1205.3 3.9 fusion.100
  1209.2 11.4 fusion.49
  1223.7 38.5 %all-reduce.6 = (f32[2048]{0:T(1024)S(1)}, f32[1024]{0:T(1024)S(1)}, f32[2048]{0:T(1024)S(1)}) all-reduce(f32[2048]{0:T(1024)S(1)} %get-tuple-element.271, f32[1024]{0:T(1024)S(1)} %copy-done.50, f32[2048]{0:T(1024)S(1)} %copy-done.47), channel_id=5, replica_groups=mesh['dp'=4,'seq'=8] {'dp','seq'}, use_global_device_ids=true, to_apply=%region_16.17.clone | all-reduce | flops 5120 | bytes 40960
  1266.8 107.8 %reduce-scatter.21.cloned.1.call-done = f32[64,256]{1,0:T(8,128)} async-done(((f32[2048,256]{1,0:T(8,128)}), f32[64,256]{1,0:T(8,128)}) %reduce-scatter.21.cloned.1.call-update) | async-done | bytes 65552 | tf_op jit(solution)/shard_map/reduce_scatter | solution.py:320
  1374.5 151.1 %reduce-scatter.15.cloned.1.call-done = f32[64,1024]{1,0:T(8,128)} async-done(((f32[2048,1024]{1,0:T(8,128)}), f32[64,1024]{1,0:T(8,128)}) %reduce-scatter.15.cloned.1.call-update) | async-done | bytes 262160 | tf_op jit(solution)/shard_map/reduce_scatter | solution.py:316
  1525.6 187.7 %reduce-scatter.17.cloned.1.call-done = f32[32,4096]{1,0:T(8,128)} async-done(((f32[1024,4096]{1,0:T(8,128)}), f32[32,4096]{1,0:T(8,128)}) %reduce-scatter.17.cloned.1.call-update) | async-done | bytes 524304 | tf_op jit(solution)/shard_map/reduce_scatter | solution.py:318
  1713.3 361.5 %reduce-scatter.23.cloned.1.call-done = f32[128,2048]{1,0:T(8,128)} async-done(((f32[4096,2048]{1,0:T(8,128)}), f32[128,2048]{1,0:T(8,128)}) %reduce-scatter.23.cloned.1.call-update) | async-done | bytes 1048592 | tf_op jit(solution)/shard_map/reduce_scatter | solution.py:321
  2074.8 491.2 %reduce-scatter.25.cloned.1.call-done = f32[64,5632]{1,0:T(8,128)} async-done(((f32[2048,5632]{1,0:T(8,128)}), f32[64,5632]{1,0:T(8,128)}) %reduce-scatter.25.cloned.1.call-update) | async-done | bytes 1441808 | tf_op jit(solution)/shard_map/reduce_scatter | solution.py:194
  2566.0 491.2 %reduce-scatter.27.cloned.1.call-done = f32[64,5632]{1,0:T(8,128)} async-done(((f32[2048,5632]{1,0:T(8,128)}), f32[64,5632]{1,0:T(8,128)}) %reduce-scatter.27.cloned.1.call-update) | async-done | bytes 1441808 | tf_op jit(solution)/shard_map/reduce_scatter | solution.py:195
  3057.2 491.2 %reduce-scatter.29.cloned.1.call-done = f32[176,2048]{1,0:T(8,128)} async-done(((f32[5632,2048]{1,0:T(8,128)}), f32[176,2048]{1,0:T(8,128)}) %reduce-scatter.29.cloned.1.call-update) | async-done | bytes 1441808 | tf_op jit(solution)/shard_map/reduce_scatter | solution.py:196
  (398 shorter events, 209.8 us)
Async XLA Ops:
  7.2 6.9 copy-start.26
  7.2 61.2 %all-gather.10.cloned.1.call-start = ((), (), s32[]{:S(2)}) async-start(), calls=%async_computation.10 | async-start | bytes 1081344 | tf_op jit(solution)/shard_map/all_gather | solution.py:71
  8.8 115.9 %all-gather.16.cloned.1.call-start = ((), (), s32[]{:S(2)}) async-start(), calls=%async_computation.13 | async-start | bytes 1081344 | tf_op jit(solution)/shard_map/all_gather | solution.py:72
  10.3 179.2 %all-gather.12.cloned.1.call-start = ((), (), s32[]{:S(2)}) async-start(), calls=%async_computation.11 | async-start | bytes 4325376 | tf_op jit(solution)/shard_map/all_gather | solution.py:68
  12.0 3.0 copy-start.24
  12.0 256.9 %all-gather.14.cloned.1.call-start = ((), (), s32[]{:S(2)}) async-start(), calls=%async_computation.12 | async-start | bytes 8650752 | tf_op jit(solution)/shard_map/all_gather | solution.py:70
  14.0 384.1 %all-gather.18.cloned.1.call-start = ((), (), s32[]{:S(2)}) async-start(), calls=%async_computation.14 | async-start | bytes 17301504 | tf_op jit(solution)/shard_map/all_gather | solution.py:73
  14.9 517.4 %all-gather.20.cloned.1.call-start = ((), (), s32[]{:S(2)}) async-start(), calls=%async_computation.15 | async-start | bytes 23789568 | tf_op jit(solution)/shard_map/all_gather | solution.py:77
  16.0 662.6 %all-gather.22.cloned.1.call-start = ((), (), s32[]{:S(2)}) async-start(), calls=%async_computation.16 | async-start | bytes 23789568 | tf_op jit(solution)/shard_map/all_gather | solution.py:78
  17.5 2.6 copy-start.52
  17.5 2.6 copy-start.53
  17.5 2.6 copy-start.54
  17.6 45.6 %copy-start.4 = (bf16[192,2048]{1,0:T(8,128)(2,1)S(1)}, bf16[192,2048]{1,0:T(8,128)(2,1)}, u32[]{:S(2)}) copy-start(bf16[192,2048]{1,0:T(8,128)(2,1)} %param.18) | copy-start | bytes 2359300
  17.6 45.8 %copy-start.51 = (s32[192]{0:T(256)S(1)}, s32[192]{0:T(256)}, u32[]{:S(2)}) copy-start(s32[192]{0:T(256)} %param.19) | copy-start | bytes 2308
  17.6 807.3 %all-gather.24.cloned.1.call-start = ((), (), s32[]{:S(2)}) async-start(), calls=%async_computation.17 | async-start | bytes 23789568 | tf_op jit(solution)/shard_map/all_gather | solution.py:79
  20.0 1047.3 %reduce-scatter.11.cloned.1.call-start = ((), (), s32[]{:S(2)}) async-start(), calls=%async_computation.18 | async-start | bytes 884736 | tf_op jit(solution)/shard_map/reduce_scatter | solution.py:270
  63.1 126.5 %copy-start.33 = (f32[2048]{0:T(1024)}, f32[2048]{0:T(1024)S(1)}, u32[]{:S(2)}) copy-start(f32[2048]{0:T(1024)S(1)} %convert_element_type.161) | copy-start | bytes 24580
  63.1 205.9 %copy-start.31 = (f32[1024]{0:T(1024)}, f32[1024]{0:T(1024)S(1)}, u32[]{:S(2)}) copy-start(f32[1024]{0:T(1024)S(1)} %convert_element_type.169) | copy-start | bytes 12292
  63.1 6.9 copy-start.48
  63.4 126.2 %copy-start.41 = (f32[192]{0:T(256)}, f32[192]{0:T(256)S(1)}, u32[]{:S(2)}) copy-start(f32[192]{0:T(256)S(1)} %add_rsqrt_fusion.2) | copy-start | bytes 2308
  63.4 7.1 copy-start.45
  64.5 210.9 %copy-start.29 = (f32[192,128]{1,0:T(8,128)}, f32[192,128]{1,0:T(8,128)S(1)}, u32[]{:S(2)}) copy-start(f32[192,128]{1,0:T(8,128)S(1)} %get-tuple-element.350) | copy-start | bytes 294916
  192.9 81.3 %copy-start.10 = (f32[192,1024]{1,0:T(8,128)}, f32[192,1024]{1,0:T(8,128)S(1)}, u32[]{:S(2)}) copy-start(f32[192,1024]{1,0:T(8,128)S(1)} %get-tuple-element.354) | copy-start | bytes 2359300
  192.9 81.3 %copy-start.43 = (f32[192]{0:T(256)}, f32[192]{0:T(256)S(1)}, u32[]{:S(2)}) copy-start(f32[192]{0:T(256)S(1)} %add_rsqrt_fusion.1) | copy-start | bytes 2308
  407.6 270.9 %copy-start.12 = (bf16[192,2048]{1,0:T(8,128)(2,1)}, bf16[192,2048]{1,0:T(8,128)(2,1)S(1)}, u32[]{:S(2)}) copy-start(bf16[192,2048]{1,0:T(8,128)(2,1)S(1)} %multiply_convert_fusion.3) | copy-start | bytes 2359300
  544.3 280.5 %copy-start.20 = (bf16[192,2048]{1,0:T(8,128)(2,1)S(1)}, bf16[192,2048]{1,0:T(8,128)(2,1)}, u32[]{:S(2)}) copy-start(bf16[192,2048]{1,0:T(8,128)(2,1)} %param.20) | copy-start | bytes 2359300
  840.8 14.4 copy-start.22
  840.8 14.4 copy-start.17
  872.5 13.2 copy-start.8
  885.7 2.8 copy-start.15
  894.3 3.3 copy-start.23
  905.8 2.3 copy-start.3
  911.0 3.3 copy-start.23
  928.8 3.3 copy-start.23
  946.5 3.3 copy-start.23
  958.9 2.3 copy-start.3
  964.2 3.3 copy-start.23
  976.7 2.3 copy-start.3
  981.9 3.3 copy-start.23
  999.6 3.3 copy-start.23
  1012.1 2.3 copy-start.3
  1017.3 3.3 copy-start.23
  1029.8 2.3 copy-start.3
  1035.1 2.6 copy-start.14
  1037.6 62.3 %reduce-scatter.13.cloned.1.call-start = ((), (), s32[]{:S(2)}) async-start(), calls=%async_computation.19 | async-start | bytes 884736 | tf_op jit(solution)/shard_map/reduce_scatter | solution.py:273
  1037.6 30.6 copy-start.46
  1037.7 30.6 copy-start.49
  1037.7 31.1 copy-start.6
  1037.7 31.1 copy-start.34
  1037.7 31.1 copy-start.42
  1038.7 228.1 %reduce-scatter.19.cloned.1.call-start = ((), (), s32[]{:S(2)}) async-start(), calls=%async_computation.22 | async-start | bytes 2162688 | tf_op jit(solution)/shard_map/reduce_scatter | solution.py:319
  1070.7 303.9 %reduce-scatter.21.cloned.1.call-start = ((), (), s32[]{:S(2)}) async-start(), calls=%async_computation.23 | async-start | bytes 2162688 | tf_op jit(solution)/shard_map/reduce_scatter | solution.py:320
  1099.9 3.4 copy-start.1
  1103.3 422.3 %reduce-scatter.15.cloned.1.call-start = ((), (), s32[]{:S(2)}) async-start(), calls=%async_computation.20 | async-start | bytes 8650752 | tf_op jit(solution)/shard_map/reduce_scatter | solution.py:316
  1119.0 594.3 %reduce-scatter.17.cloned.1.call-start = ((), (), s32[]{:S(2)}) async-start(), calls=%async_computation.21 | async-start | bytes 17301504 | tf_op jit(solution)/shard_map/reduce_scatter | solution.py:318
  1128.2 946.6 %reduce-scatter.23.cloned.1.call-start = ((), (), s32[]{:S(2)}) async-start(), calls=%async_computation.24 | async-start | bytes 34603008 | tf_op jit(solution)/shard_map/reduce_scatter | solution.py:321
  1144.5 1421.5 %reduce-scatter.25.cloned.1.call-start = ((), (), s32[]{:S(2)}) async-start(), calls=%async_computation.25 | async-start | bytes 47579136 | tf_op jit(solution)/shard_map/reduce_scatter | solution.py:194
  1165.1 1892.1 %reduce-scatter.27.cloned.1.call-start = ((), (), s32[]{:S(2)}) async-start(), calls=%async_computation.26 | async-start | bytes 47579136 | tf_op jit(solution)/shard_map/reduce_scatter | solution.py:195
  1184.7 2363.7 %reduce-scatter.29.cloned.1.call-start = ((), (), s32[]{:S(2)}) async-start(), calls=%async_computation.27 | async-start | bytes 47579136 | tf_op jit(solution)/shard_map/reduce_scatter | solution.py:196
  1205.3 3.9 copy-start.18
  1205.3 3.9 copy-start.19
  1209.2 11.4 copy-start.27
  1209.2 11.4 copy-start.36
  1209.2 11.4 copy-start.38
  (30 other events, 46.7 us)
Sparse Core Ops, SparseCore 0:
  11.6 56.7 all-gather.9
  71.9 52.6 all-gather.15
  128.3 61.2 all-gather.11
  193.0 75.9 all-gather.13
  272.4 113.7 all-gather.17
  389.5 142.7 all-gather.19
  535.7 142.7 all-gather.21
  682.0 142.7 all-gather.23
  1037.7 29.5 reduce-scatter.10
  1070.1 29.7 reduce-scatter.12
  1102.7 135.8 reduce-scatter.18
  1241.4 133.1 reduce-scatter.20
  1377.4 148.1 reduce-scatter.14
  1528.3 184.8 reduce-scatter.16
  1716.0 358.7 reduce-scatter.22
  2077.5 488.4 reduce-scatter.24
  2568.7 488.4 reduce-scatter.26
  3059.9 488.4 reduce-scatter.28
where the time goes:
time: 3570 us; the launch traced here: 3560 us
  waiting for transfers between devices  2900 us (81%)
  matrix products  390 us (11%)
  blocking collectives  115 us (3%)
  local copies, waits for them, and re-layouts  72.8 us (2%)
  other arithmetic  53.4 us (1%)
    reduce_scatter x1, waiting for transfers between devices, local(): lax.psum_scatter(grad_up_weight, ('dp', 'seq'), scatter_dimension=0, tile...  491 us
    reduce_scatter x1, waiting for transfers between devices, local(): lax.psum_scatter(grad_gate_weight, ('dp', 'seq'), scatter_dimension=0, ti...  491 us
    reduce_scatter x1, waiting for transfers between devices, local(): lax.psum_scatter(grad_down, ('dp', 'seq'), scatter_dimension=0, tiled=True)  491 us
    reduce_scatter x1, waiting for transfers between devices, local(): lax.psum_scatter(grad_output_weight, ('dp', 'seq'), scatter_dimension=0,...  362 us
    reduce_scatter x1, waiting for transfers between devices, local(): lax.psum_scatter(grad_up_query, ('dp', 'seq'), scatter_dimension=0, tiled...  188 us
    reduce_scatter x1, waiting for transfers between devices, local(): lax.psum_scatter(grad_down_weight, ('dp', 'seq'), scatter_dimension=0, ti...  151 us
    all_gather x1, waiting for transfers between devices, local(): lax.all_gather(w_up.astype(jnp.bfloat16), ('dp', 'seq'), axis=0, tiled=True)  134 us
    all_gather x1, waiting for transfers between devices, local(): lax.all_gather(w_down.astype(jnp.bfloat16), ('dp', 'seq'), axis=0, tiled=...  134 us
  transfers between devices with their start and end apart: 18, of which 16 were waited for; matrix products, arithmetic and copies ran while one was open for 8% of the time, Pallas kernels for 0%

commit v1 on v0

--- a/solution.py
+++ b/solution.py
@@ -3,6 +3,8 @@
 import jax
 import jax.numpy as jnp
 from jax import lax
+from jax.experimental import pallas as pl
+from jax.experimental.pallas import tpu as pltpu
 from jax.sharding import PartitionSpec as P
 
 HEADS = 16
@@ -337,9 +339,1066 @@
     )
 
 
+BITS = {"y": ("dp", 2), "x": ("dp", 1), "h": ("seq", 4), "l": ("seq", 2), "c": ("seq", 1)}
+bf16 = jnp.bfloat16
+f32 = jnp.float32
+
+
+def swap(value, bit):
+    axis, mask = BITS[bit]
+    return lax.ppermute(value, axis, [(i, i ^ mask) for i in range(lax.axis_size(axis))])
+
+
+def swap_many(value, mask):
+    return lax.ppermute(value, ("dp", "seq"), [(i, i ^ mask) for i in range(32)])
+
+
+def pick(value, index, axis=0):
+    return lax.dynamic_index_in_dim(value, index, axis, keepdims=False)
+
+
+def gather_plane(block):
+    half = block.shape[0] // 2
+    from_x = swap(block, "x")
+    from_l = swap(block, "l")
+    from_xl = jnp.concatenate([swap(from_x[:half], "l"), swap(from_l[half:], "x")])
+    mine = [block, from_l, from_x, from_xl]
+    pieces = []
+    for piece in mine:
+        pieces += [piece, swap(piece, "c")]
+    return jnp.stack(pieces)
+
+
+def scatter_plane(parts):
+    half = parts.shape[1] // 2
+    parts = parts.reshape((2, 2, 2) + parts.shape[1:])
+    pair = parts[:, :, 0].astype(f32) + swap(parts[:, :, 1], "c").astype(f32)
+    upper = pair[:, :, :half]
+    lower = pair[:, :, half:]
+    upper_one = upper[0] + swap(upper[1].astype(bf16), "x").astype(f32)
+    lower_one = lower[:, 0] + swap(lower[:, 1].astype(bf16), "l").astype(f32)
+    upper_two = upper_one[0] + swap(upper_one[1].astype(bf16), "l").astype(f32)
+    lower_two = lower_one[0] + swap(lower_one[1].astype(bf16), "x").astype(f32)
+    return jnp.concatenate([upper_two, lower_two])
+
+
+def exchange_plane(pieces, rank):
+    out = jnp.zeros_like(pieces)
+    for j in range(8):
+        mask = (j & 4) * 2 + (j & 3)
+        piece = pick(pieces, rank ^ j)
+        if mask:
+            piece = swap_many(piece, mask)
+        out = lax.dynamic_update_index_in_dim(out, piece, rank ^ j, 0)
+    return out
+
+
+def gather_rows(block, y, h):
+    from_h = swap(block, "h")
+    from_y = swap(block, "y")
+    from_yh = swap(from_h, "y")
+    out = jnp.zeros((2, block.shape[0], 2) + block.shape[1:], block.dtype)
+    for piece, at_y, at_h in ((block, y, h), (from_h, y, 1 - h), (from_y, 1 - y, h), (from_yh, 1 - y, 1 - h)):
+        out = lax.dynamic_update_slice(out, piece[None, :, None], (at_y, 0, at_h, 0, 0))
+    return out
+
+
+def scatter_rows(parts, y, h):
+    kept = pick(parts, y).astype(f32) + swap(pick(parts, 1 - y), "y").astype(f32)
+    return pick(kept, h, 1) + swap(pick(kept, 1 - h, 1).astype(bf16), "h").astype(f32)
+
+
+MASK = {"y": 16, "x": 8, "h": 4, "l": 2, "c": 1}
+
+
+def flip(number, bits):
+    bit = 1
+    while bit <= bits:
+        if bits & bit:
+            number = number + bit - 2 * bit * ((number // bit) % 2)
+        bit *= 2
+    return number
+
+
+def coordinates():
+    dp = lax.axis_index("dp")
+    seq = lax.axis_index("seq")
+    return dp // 2, dp % 2, seq // 4, (seq // 2) % 2, seq % 2
+
+
+def partner(mask):
+    return flip(lax.axis_index("dp"), mask // 8), flip(lax.axis_index("seq"), mask % 8)
+
+
+def greet(masks):
+    barrier = pltpu.get_barrier_semaphore()
+    for mask in masks:
+        pl.semaphore_signal(barrier, inc=1, device_id=partner(mask), device_id_type=pl.DeviceIdType.MESH)
+    pl.semaphore_wait(barrier, len(masks))
+
+
+class Wire:
+    def __init__(self, send_sem, recv_sem, local_sem):
+        self.send_sem, self.recv_sem, self.local_sem = send_sem, recv_sem, local_sem
+        self.copies = []
+        self.locals = 0
+
+    def send(self, src, dst, mask):
+        k = len(self.copies)
+        copy = pltpu.make_async_remote_copy(
+            src_ref=src,
+            dst_ref=dst,
+            send_sem=self.send_sem.at[k],
+            recv_sem=self.recv_sem.at[k],
+            device_id=partner(mask),
+            device_id_type=pl.DeviceIdType.MESH,
+        )
+        copy.start()
+        self.copies.append(copy)
+        return copy
+
+    def local(self, src, dst):
+        copy = pltpu.make_async_copy(src, dst, self.local_sem.at[self.locals])
+        self.locals += 1
+        copy.start()
+        return copy
+
+    def close(self):
+        for copy in self.copies:
+            copy.wait_send()
+
+
+def wires(remote, local):
+    return [pltpu.SemaphoreType.DMA((remote,)), pltpu.SemaphoreType.DMA((remote,)), pltpu.SemaphoreType.DMA((local,))]
+
+
+def arrived(copies):
+    for copy in copies:
+        copy.wait_recv()
+
+
+ANY = pl.BlockSpec(memory_space=pl.ANY)
+VMEM = pl.BlockSpec(memory_space=pltpu.VMEM)
+PLANE = [j // 4 * 8 + j % 4 for j in range(1, 8)]
+
+
+def moving(kernel, number, outs, operands, scratch, in_specs=None, out_specs=None, bytes_sent=1 << 20):
+    return pl.pallas_call(
+        kernel,
+        out_shape=outs,
+        in_specs=in_specs or [ANY] * len(operands),
+        out_specs=out_specs or [ANY] * len(outs),
+        scratch_shapes=scratch,
+        compiler_params=pltpu.CompilerParams(
+            collective_id=number, has_side_effects=True, vmem_limit_bytes=48 * 1024 * 1024
+        ),
+        cost_estimate=pl.CostEstimate(flops=0, bytes_accessed=bytes_sent, transcendentals=0),
+        name=kernel.__name__,
+    )(*operands)
+
+
+def head_kernel(first, upq, gu, out, upq_out, gu_out, send_sem, recv_sem, local_sem):
+    y, x, h, l, c = coordinates()
+    rank = x * 4 + l * 2 + c
+    wire = Wire(send_sem, recv_sem, local_sem)
+    greet([16, 4] + PLANE)
+    width = first.shape[1]
+    cut = [0, width // 3 // 128 * 128, width // 3 // 128 * 256, width]
+    parts = [pl.ds(cut[i], cut[i + 1] - cut[i]) for i in range(3)]
+    a, b, d = parts
+    mine = wire.local(first, out.at[0, 0, 0, 0, 0])
+    one = [wire.send(first.at[:, p], out.at[0, 0, 1, 0, 0, :, p], 4) for p in parts]
+    up_rows = upq.shape[1]
+    gu_rows = gu.shape[2]
+    up_place = lambda: upq_out.at[y, x, h, pl.ds((l * 2 + c) * up_rows, up_rows), :]
+    gu_place = lambda: gu_out.at[:, x, pl.ds((l * 2 + c) * gu_rows, gu_rows), :]
+    up_mine = wire.local(upq.at[rank], up_place())
+    up_sent = [wire.send(upq.at[flip(rank, j)], up_place(), PLANE[j - 1]) for j in range(1, 8)]
+    mine.wait()
+    one[0].wait_recv()
+    two_a = wire.send(out.at[0, 0, :, 0, 0, :, a], out.at[0, 0, :, 1, 0, :, a], 2)
+    one[1].wait_recv()
+    two_b = wire.send(out.at[0, 0, :, 0, 0, :, b], out.at[0, 1, :, 0, 0, :, b], 8)
+    one[2].wait_recv()
+    two_d = wire.send(out.at[0, 0, :, 0, 0, :, d], out.at[1, 0, :, 0, 0, :, d], 16)
+    up_mine.wait()
+    arrived(up_sent)
+    up_h = wire.send(upq_out.at[y, :, h], upq_out.at[y, :, h], 4)
+    two_a.wait_recv()
+    three_a = wire.send(out.at[0, 0, :, :, 0, :, a], out.at[0, 1, :, :, 0, :, a], 8)
+    two_b.wait_recv()
+    three_b = wire.send(out.at[0, :, :, 0, 0, :, b], out.at[1, :, :, 0, 0, :, b], 16)
+    two_d.wait_recv()
+    three_d = wire.send(out.at[:, 0, :, 0, 0, :, d], out.at[:, 0, :, 1, 0, :, d], 2)
+    three_a.wait_recv()
+    four_a = wire.send(out.at[0, :, :, :, 0, :, a], out.at[1, :, :, :, 0, :, a], 16)
+    three_b.wait_recv()
+    four_b = wire.send(out.at[:, :, :, 0, 0, :, b], out.at[:, :, :, 1, 0, :, b], 2)
+    three_d.wait_recv()
+    four_d = wire.send(out.at[:, 0, :, :, 0, :, d], out.at[:, 1, :, :, 0, :, d], 8)
+    five = [
+        wire.send(out.at[0, :, :, :, 0, :, a], out.at[0, :, :, :, 1, :, a], 1),
+        wire.send(out.at[:, :, :, 0, 0, :, b], out.at[:, :, :, 0, 1, :, b], 1),
+        wire.send(out.at[:, 0, :, :, 0, :, d], out.at[:, 0, :, :, 1, :, d], 1),
+    ]
+    up_y = [wire.send(upq_out.at[y, :, h], upq_out.at[y, :, h], 16)]
+    up_h.wait_recv()
+    up_y += [wire.send(upq_out.at[y, :, 1 - h], upq_out.at[y, :, 1 - h], 16)]
+    gu_mine = wire.local(gu.at[rank], gu_place())
+    gu_sent = [wire.send(gu.at[flip(rank, j)], gu_place(), PLANE[j - 1]) for j in range(1, 8)]
+    four_a.wait_recv()
+    five += [wire.send(out.at[1, :, :, :, 0, :, a], out.at[1, :, :, :, 1, :, a], 1)]
+    four_b.wait_recv()
+    five += [wire.send(out.at[:, :, :, 1, 0, :, b], out.at[:, :, :, 1, 1, :, b], 1)]
+    four_d.wait_recv()
+    five += [wire.send(out.at[:, 1, :, :, 0, :, d], out.at[:, 1, :, :, 1, :, d], 1)]
+    gu_mine.wait()
+    arrived(five + up_y + gu_sent)
+    wire.close()
+
+
+def head(first, upq, gu):
+    rows, width = first.shape
+    outs = [
+        jax.ShapeDtypeStruct((2, 2, 2, 2, 2, rows, width), bf16),
+        jax.ShapeDtypeStruct((2, 2, 2, 4 * upq.shape[1], upq.shape[2]), bf16),
+        jax.ShapeDtypeStruct((2, 2, 4 * gu.shape[2], gu.shape[3]), bf16),
+    ]
+    return moving(head_kernel, 1, outs, (first, upq, gu), wires(40, 4))
+
+
+def plane_gather(wire, block, out, own):
+    half = block.shape[0] // 2
+    top, low = pl.ds(0, half), pl.ds(half, half)
+    from_x = wire.send(block, out.at[1, 0, 0], 8)
+    from_l = wire.send(block, out.at[0, 1, 0], 2)
+    from_c = [wire.send(block, out.at[0, 0, 1], 1)]
+    mine = wire.local(block, own) if own is not None else None
+
+    def finish():
+        from_x.wait_recv()
+        second = [wire.send(out.at[1, 0, 0, top], out.at[1, 1, 0, top], 2)]
+        from_l.wait_recv()
+        second += [wire.send(out.at[0, 1, 0, low], out.at[1, 1, 0, low], 8)]
+        cores = from_c + [wire.send(out.at[1, 0, 0], out.at[1, 0, 1], 1), wire.send(out.at[0, 1, 0], out.at[0, 1, 1], 1)]
+        second[0].wait_recv()
+        cores += [wire.send(out.at[1, 1, 0, top], out.at[1, 1, 1, top], 1)]
+        second[1].wait_recv()
+        cores += [wire.send(out.at[1, 1, 0, low], out.at[1, 1, 1, low], 1)]
+        if mine is not None:
+            mine.wait()
+        arrived(cores)
+
+    return finish
+
+
+def spread(wire, block, place):
+    y, x, h, l, c = coordinates()
+    mine = wire.local(block, place(y, h))
+    from_h = wire.send(block, place(y, h), 4)
+    from_y = wire.send(block, place(y, h), 16)
+
+    def second():
+        from_h.wait_recv()
+        last = wire.send(place(y, 1 - h), place(y, 1 - h), 16)
+
+        def finish():
+            mine.wait()
+            arrived([from_y, last])
+
+        return finish
+
+    return second
+
+
+def pack_kernel(block, out_weight, out, weight_out, weight_all, send_sem, recv_sem, local_sem):
+    y, x, h, l, c = coordinates()
+    wire = Wire(send_sem, recv_sem, local_sem)
+    greet([16, 4, 8, 2, 1])
+    near = block.shape[1]
+    far = out.shape[5 - 1] - near
+    columns, far_columns = pl.ds(0, near), pl.ds(near, far)
+    from_h = wire.send(block.at[:, pl.ds(near - far, far)], out.at[0, 0, 0, :, far_columns], 4)
+    near_out = out.at[:, :, :, :, columns]
+    finish = plane_gather(wire, block, near_out, near_out.at[0, 0, 0])
+    second = spread(wire, out_weight, lambda yy, hh: weight_all.at[yy, hh])
+    from_h.wait_recv()
+    far_out = out.at[:, :, :, :, far_columns]
+    finish_far = plane_gather(wire, far_out.at[0, 0, 0], far_out, None)
+    finish()
+    finish_far()
+    second()()
+    swapped = wire.send(weight_all.at[:, 1 - c], weight_out.at[:, c], 1)
+    kept = wire.local(weight_all.at[:, c], weight_out.at[:, c])
+    kept.wait()
+    swapped.wait_recv()
+    wire.close()
+
+
+def pack(block, out_weight):
+    rows, near = block.shape
+    outs = [
+        jax.ShapeDtypeStruct((2, 2, 2, rows, near + 2 * HEAD_DIM), bf16),
+        jax.ShapeDtypeStruct((2, 2) + out_weight.shape, bf16),
+        jax.ShapeDtypeStruct((2, 2) + out_weight.shape, bf16),
+    ]
+    return moving(pack_kernel, 2, outs, (block, out_weight), wires(32, 4))[:2]
+
+
+def plane_reduce(wire, parts, out, from_c, send_one, recv_one, send_two, recv_two):
+    rows = parts.shape[3]
+    half = rows // 2
+    step = 16
+    order = [(1, 1), (1, 0), (0, 1), (0, 0)]
+    cores = {k: wire.send(parts.at[k[0], k[1], 1], from_c.at[k[0], k[1]], 1) for k in order}
+    up = lambda ref, i: ref[pl.ds(i, step)].astype(f32)
+
+    def pair(k, base, i):
+        return up(parts.at[k[0], k[1], 0], base + i) + up(from_c.at[k[0], k[1]], base + i)
+
+    def each(body):
+        @pl.loop(0, half // step)
+        def _(i):
+            body(pl.multiple_of(i * step, step))
+
+    state = {}
+
+    def first():
+        for k in order[:3]:
+            cores[k].wait_recv()
+            if k[0]:
+                def fill(i, k=k):
+                    send_one[0, k[1], pl.ds(i, step)] = pair(k, 0, i).astype(bf16)
+                each(fill)
+            if k[1]:
+                def fill(i, k=k):
+                    send_one[1, k[0], pl.ds(i, step)] = pair(k, half, i).astype(bf16)
+                each(fill)
+            if k == (1, 1):
+                state["x1"] = wire.send(send_one.at[0, 1], recv_one.at[0, 1], 8)
+                state["l1"] = wire.send(send_one.at[1, 1], recv_one.at[1, 1], 2)
+            elif k == (1, 0):
+                state["x0"] = wire.send(send_one.at[0, 0], recv_one.at[0, 0], 8)
+            else:
+                state["l0"] = wire.send(send_one.at[1, 0], recv_one.at[1, 0], 2)
+        cores[(0, 0)].wait_recv()
+
+    def middle():
+        state["x1"].wait_recv()
+        def fill(i):
+            send_two[0, pl.ds(i, step)] = (pair((0, 1), 0, i) + up(recv_one.at[0, 1], i)).astype(bf16)
+        each(fill)
+        state["l2"] = wire.send(send_two.at[0], recv_two.at[0], 2)
+        state["l1"].wait_recv()
+        def fill(i):
+            send_two[1, pl.ds(i, step)] = (pair((1, 0), half, i) + up(recv_one.at[1, 1], i)).astype(bf16)
+        each(fill)
+        state["x2"] = wire.send(send_two.at[1], recv_two.at[1], 8)
+
+    def finish():
+        state["x0"].wait_recv()
+        state["l0"].wait_recv()
+        state["l2"].wait_recv()
+        def fill(i):
+            out[pl.ds(i, step)] = pair((0, 0), 0, i) + up(recv_one.at[0, 0], i) + up(recv_two.at[0], i)
+        each(fill)
+        state["x2"].wait_recv()
+        def fill(i):
+            out[pl.ds(half + i, step)] = pair((0, 0), half, i) + up(recv_one.at[1, 0], i) + up(recv_two.at[1], i)
+        each(fill)
+
+    return first, middle, finish
+
+
+def reduce_scratch(rows, width):
+    half = rows // 2
+    return [
+        pltpu.VMEM((2, 2, rows, width), bf16),
+        pltpu.VMEM((2, 2, half, width), bf16),
+        pltpu.VMEM((2, 2, half, width), bf16),
+        pltpu.VMEM((2, half, width), bf16),
+        pltpu.VMEM((2, half, width), bf16),
+    ]
+
+
+def middle_kernel(parts, gate, out, gate_out, from_c, s1, r1, s2, r2, send_sem, recv_sem, local_sem):
+    wire = Wire(send_sem, recv_sem, local_sem)
+    greet([16, 4, 8, 2, 1])
+    first, middle, finish = plane_reduce(wire, parts, out, from_c, s1, r1, s2, r2)
+    second = spread(wire, gate, lambda yy, hh: gate_out.at[yy, :, hh])
+    first()
+    middle()
+    last = second()
+    finish()
+    last()
+    wire.close()
+
+
+def middle_sum(parts, gate_set):
+    rows, width = parts.shape[3:]
+    outs = [
+        jax.ShapeDtypeStruct((rows, width), f32),
+        jax.ShapeDtypeStruct((2, 2, 2) + gate_set.shape[1:], bf16),
+    ]
+    return moving(
+        middle_kernel, 3, outs, (parts, gate_set), reduce_scratch(rows, width) + wires(20, 2),
+        in_specs=[VMEM, ANY], out_specs=[VMEM, ANY],
+    )
+
+
+def feed_kernel(block, up, out, up_out, send_sem, recv_sem, local_sem):
+    wire = Wire(send_sem, recv_sem, local_sem)
+    greet([16, 4, 8, 2, 1])
+    finish = plane_gather(wire, block, out, out.at[0, 0, 0])
+    second = spread(wire, up, lambda yy, hh: up_out.at[yy, :, hh])
+    finish()
+    second()()
+    wire.close()
+
+
+def feed_gather(block, up_set):
+    outs = [
+        jax.ShapeDtypeStruct((2, 2, 2) + block.shape, bf16),
+        jax.ShapeDtypeStruct((2, 2, 2) + up_set.shape[1:], bf16),
+    ]
+    return moving(feed_kernel, 4, outs, (block, up_set), wires(16, 4))
+
+
+def add_rows_into(rows, body, step=16):
+    @pl.loop(0, rows // step)
+    def _(i):
+        body(pl.ds(pl.multiple_of(i * step, step), step))
+
+
+def wide(ref, where):
+    return ref[where].astype(f32)
+
+
+def fold(wire, source, chunks, recv_y, send_h, recv_h, out):
+    y, x, h, l, c = coordinates()
+    sent = {}
+    for hh, name in ((1 - h, "far"), (h, "near")):
+        for i, (start, size) in enumerate(chunks):
+            sent[name, i] = wire.send(source(1 - y, hh, i), recv_y.at[hh, pl.ds(start, size)], 16)
+    passed = []
+
+    def second():
+        for i, (start, size) in enumerate(chunks):
+            sent["far", i].wait_recv()
+            mine, theirs, target = source(y, 1 - h, i), recv_y.at[1 - h, pl.ds(start, size)], send_h.at[pl.ds(start, size)]
+
+            def body(r, mine=mine, theirs=theirs, target=target):
+                target[r] = (wide(mine, r) + wide(theirs, r)).astype(bf16)
+
+            add_rows_into(size, body)
+            passed.append(wire.send(target, recv_h.at[pl.ds(start, size)], 4))
+
+    def finish():
+        for i, (start, size) in enumerate(chunks):
+            sent["near", i].wait_recv()
+            passed[i].wait_recv()
+            mine, theirs = source(y, h, i), recv_y.at[h, pl.ds(start, size)]
+            far, target = recv_h.at[pl.ds(start, size)], out.at[pl.ds(start, size)]
+
+            def body(r, mine=mine, theirs=theirs, far=far, target=target):
+                target[r] = (wide(mine, r) + wide(theirs, r) + wide(far, r)).astype(out.dtype)
+
+            add_rows_into(size, body)
+
+    return second, finish
+
+
+def fold_scratch(rows, width):
+    return [pltpu.VMEM((2, rows, width), bf16), pltpu.VMEM((rows, width), bf16), pltpu.VMEM((rows, width), bf16)]
+
+
+def columns_of(grad):
+    return lambda yy, hh, i: grad.at[yy, i, hh]
+
+
+def rows_of(grad, chunks):
+    return lambda yy, hh, i: grad.at[yy, hh, pl.ds(*chunks[i])]
+
+
+def halves(rows):
+    first = rows // 2 // 16 * 16 if rows % 32 == 0 else (rows // 2 + 15) // 16 * 16
+    return [(0, first), (first, rows - first)]
+
+
+def hand_back(wire, own, out):
+    y, x, h, l, c = coordinates()
+    rank = x * 4 + l * 2 + c
+    rows = out.shape[1]
+    piece = lambda k: own.at[pl.ds(pl.multiple_of(k * rows, rows), rows)]
+    mine = wire.local(piece(rank), out.at[rank])
+    sent = [wire.send(piece(flip(rank, j)), out.at[rank], PLANE[j - 1]) for j in range(1, 8)]
+
+    def finish():
+        mine.wait()
+        arrived(sent)
+
+    return finish
+
+
+def mid_sum_kernel(parts, grad, out, grad_out, from_c, s1, r1, s2, r2, ry, sh, rh, send_sem, recv_sem, local_sem):
+    wire = Wire(send_sem, recv_sem, local_sem)
+    greet([16, 8, 4, 2, 1])
+    chunks = halves(grad.shape[2])
+    first, middle, finish = plane_reduce(wire, parts, out, from_c, s1, r1, s2, r2)
+    second, last = fold(wire, rows_of(grad, chunks), chunks, ry, sh, rh, grad_out)
+    first()
+    second()
+    middle()
+    finish()
+    last()
+    wire.close()
+
+
+def mid_sum(parts, grad):
+    rows, width = parts.shape[3:]
+    grad_rows = grad.shape[2]
+    outs = [jax.ShapeDtypeStruct((rows, width), f32), jax.ShapeDtypeStruct((grad_rows, width), f32)]
+    return moving(
+        mid_sum_kernel, 5, outs, (parts, grad),
+        reduce_scratch(rows, width) + fold_scratch(grad_rows, width) + wires(20, 1),
+        in_specs=[VMEM, VMEM], out_specs=[VMEM, VMEM],
+    )
+
+
+def branch_kernel(block, grad, out, grad_out, ry, sh, rh, own, send_sem, recv_sem, local_sem):
+    wire = Wire(send_sem, recv_sem, local_sem)
+    greet([16, 4] + PLANE)
+    size = grad.shape[3]
+    chunks = [(0, size), (size, size)]
+    finish = plane_gather(wire, block, out, out.at[0, 0, 0])
+    second, last = fold(wire, columns_of(grad), chunks, ry, sh, rh, own)
+    finish()
+    second()
+    last()
+    hand_back(wire, own, grad_out)()
+    wire.close()
+
+
+def branch_gather(block, grad):
+    outs = [
+        jax.ShapeDtypeStruct((2, 2, 2) + block.shape, bf16),
+        jax.ShapeDtypeStruct((8, grad.shape[3] // 4, grad.shape[4]), bf16),
+    ]
+    own = (2 * grad.shape[3], grad.shape[4])
+    return moving(
+        branch_kernel, 6, outs, (block, grad), fold_scratch(*own) + [pltpu.VMEM(own, bf16)] + wires(40, 4),
+        in_specs=[ANY, VMEM],
+    )
+
+
+def back_sum_kernel(parts, grad, out, grad_out, from_c, s1, r1, s2, r2, ry, sh, rh, own, send_sem, recv_sem, local_sem):
+    wire = Wire(send_sem, recv_sem, local_sem)
+    greet([16, 4] + PLANE)
+    size = grad.shape[3]
+    chunks = [(0, size), (size, size)]
+    first, middle, finish = plane_reduce(wire, parts, out, from_c, s1, r1, s2, r2)
+    second, last = fold(wire, columns_of(grad), chunks, ry, sh, rh, own)
+    first()
+    second()
+    middle()
+    finish()
+    last()
+    hand_back(wire, own, grad_out)()
+    wire.close()
+
+
+def back_sum(parts, grad):
+    rows, width = parts.shape[3:]
+    own = (2 * grad.shape[3], grad.shape[4])
+    outs = [
+        jax.ShapeDtypeStruct((rows, width), f32),
+        jax.ShapeDtypeStruct((8, grad.shape[3] // 4, grad.shape[4]), bf16),
+    ]
+    return moving(
+        back_sum_kernel, 7, outs, (parts, grad),
+        reduce_scratch(rows, width) + fold_scratch(*own) + [pltpu.VMEM(own, bf16)] + wires(40, 4),
+        in_specs=[VMEM, VMEM], out_specs=[VMEM, ANY],
+    )
+
+
+def tail_kernel(parts, up_grad, out_grad, out, up_out, out_out, acc, recv, from_c, uy, us, ur, up_own, oy, os, orr, oc, out_sum, send_sem, recv_sem, local_sem):
+    y, x, h, l, c = coordinates()
+    wire = Wire(send_sem, recv_sem, local_sem)
+    greet([16, 4] + PLANE)
+    rows, width = out.shape
+    third = width // 3 // 128 * 128
+    cut = [(0, third), (third, third), (2 * third, width - 2 * third)]
+    columns = [pl.ds(*k) for k in cut]
+    bit_of = {"y": 0, "x": 1, "h": 2, "l": 3}
+    orders = ["yxlh", "lyxh", "xlyh"]
+
+    def where(fixed):
+        return tuple(fixed.get(k, slice(None)) for k in "yxhl")
+
+    swapped = wire.send(out_grad.at[:, 1 - c], oc.at[:, c], 1)
+    cores = []
+    for p in range(3):
+        pair = []
+        for side in (1, 0):
+            place = where({orders[p][0]: side})
+            pair.append(wire.send(parts.at[place + (1, slice(None), columns[p])], from_c.at[place + (slice(None), columns[p])], 1))
+        cores.append(pair)
+    chunks = [(0, up_grad.shape[3]), (up_grad.shape[3], up_grad.shape[3])]
+    up_second, up_last = fold(wire, columns_of(up_grad), chunks, uy, us, ur, up_own)
+
+    def every(fixed, body):
+        free = [k for k in "yxhl" if k not in fixed]
+        count = 2 ** len(free)
+
+        @pl.loop(0, count * (rows // 16))
+        def _(i):
+            block = i // (rows // 16)
+            r = pl.ds(pl.multiple_of((i % (rows // 16)) * 16, 16), 16)
+            at = dict(fixed)
+            for position, k in enumerate(reversed(free)):
+                at[k] = (block // 2**position) % 2
+            body(tuple(at[k] for k in "yxhl"), r)
+
+    for side in (1, 0):
+        for p in range(3):
+            cores[p][1 - side].wait_recv()
+
+            def body(at, r, p=p):
+                total = wide(parts, at + (0, r, columns[p])) + wide(from_c, at + (r, columns[p]))
+                acc[at + (r, columns[p])] = total.astype(bf16)
+
+            every({orders[p][0]: side}, body)
+            if side == 1:
+                place = where({orders[p][0]: 1}) + (slice(None), columns[p])
+                sent = wire.send(acc.at[place], recv.at[place], MASK[orders[p][0]])
+                cores[p].append(sent)
+    up_second()
+    swapped.wait_recv()
+    out_chunks = halves(out_grad.shape[2])
+
+    kept = wire.local(out_grad.at[:, c], oc.at[:, c])
+    kept.wait()
+    out_source = lambda yy, hh, i: oc.at[yy, hh, pl.ds(*out_chunks[i])]
+    out_second, out_last = fold(wire, out_source, out_chunks, oy, os, orr, out_sum)
+    for step in range(4):
+        for p in range(3):
+            order = orders[p]
+            fixed = {k: 0 for k in order[:step]}
+            cores[p][-1].wait_recv()
+            far = where({**fixed, order[step]: 1})
+
+            def body(at, r, p=p, bit=order[step]):
+                other = tuple(1 if k == bit else v for k, v in zip("yxhl", at))
+                total = wide(acc, at + (r, columns[p])) + wide(recv, other + (r, columns[p]))
+                if step == 3:
+                    out[r, columns[p]] = total
+                else:
+                    acc[at + (r, columns[p])] = total.astype(bf16)
+
+            every({**fixed, order[step]: 0}, body)
+            if step < 3:
+                place = where({**fixed, order[step]: 0, order[step + 1]: 1}) + (slice(None), columns[p])
+                cores[p].append(wire.send(acc.at[place], recv.at[place], MASK[order[step + 1]]))
+        if step == 0:
+            out_second()
+            up_last()
+            up_back = hand_back(wire, up_own, up_out)
+    out_last()
+
+    def body(r):
+        out_out[r] = out_sum[r]
+
+    add_rows_into(out_sum.shape[0], body)
+    up_back()
+    wire.close()
+
+
+def tail(parts, up_grad, out_grad):
+    rows, width = parts.shape[5:]
+    own = (2 * up_grad.shape[3], up_grad.shape[4])
+    out_rows, out_width = out_grad.shape[2:]
+    outs = [
+        jax.ShapeDtypeStruct((rows, width), f32),
+        jax.ShapeDtypeStruct((8, up_grad.shape[3] // 4, up_grad.shape[4]), bf16),
+        jax.ShapeDtypeStruct((out_rows, out_width), f32),
+    ]
+    blocks = (2, 2, 2, 2, rows, width)
+    scratch = [pltpu.VMEM(blocks, bf16)] * 3 + fold_scratch(*own) + [pltpu.VMEM(own, bf16)]
+    scratch += fold_scratch(out_rows, out_width)
+    scratch += [pltpu.VMEM((2, 2, out_rows, out_width), bf16), pltpu.VMEM((out_rows, out_width), f32)]
+    return moving(
+        tail_kernel, 8, outs, (parts, up_grad, out_grad), scratch + wires(60, 4),
+        in_specs=[VMEM, VMEM, VMEM], out_specs=[VMEM, ANY, VMEM],
+    )
+
+
+def rope_table(places):
+    half = HEAD_DIM // 2
+    freqs = rope_base ** (-(2.0 * jnp.arange(half).astype(f32)) / HEAD_DIM)
+    angles = places.astype(f32)[:, None] * freqs[None, :]
+    return jnp.cos(angles), jnp.sin(angles)
+
+
+def turn(values, cosine, sine, sign):
+    half = HEAD_DIM // 2
+    first = values[..., :half]
+    second = values[..., half:]
+    return jnp.concatenate([first * cosine - sign * second * sine, sign * first * sine + second * cosine], axis=-1)
+
+
+QUERY_BLOCK = 384
+
+
+def attend_kernel(q_ref, k_ref, v_ref, kidx_ref, qidx_ref, first_ref, o_ref, lse_ref):
+    scores = lax.dot_general(q_ref[...], k_ref[...], (((1,), (1,)), ((), ())), preferred_element_type=f32)
+    keys = kidx_ref[...]
+    seen = (keys >= first_ref[...]) & (keys <= qidx_ref[...])
+    scores = jnp.where(seen, scores * (1.0 / math.sqrt(HEAD_DIM)), masked_score)
+    top = jnp.max(scores, axis=-1, keepdims=True)
+    weights = jnp.exp(scores - top)
+    total = jnp.sum(weights, axis=-1, keepdims=True)
+    out = jnp.dot(weights.astype(bf16), v_ref[...], preferred_element_type=f32)
+    o_ref[...] = out / total
+    lse_ref[...] = top + jnp.log(total)
+
+
+def attend(queries, keys, values, key_index, query_index, first_index):
+    tokens = queries.shape[0]
+    group = keys.shape[1]
+    blocks = tokens // 2 // QUERY_BLOCK
+    row = lambda g, a, i: (g * blocks + i, 0)
+    head = lambda g, a, i: (g * blocks + i, a)
+    whole = lambda g, a, i: (g, 0, 0)
+    return pl.pallas_call(
+        attend_kernel,
+        grid=(2, 2, blocks),
+        in_specs=[
+            pl.BlockSpec((QUERY_BLOCK, HEAD_DIM), head),
+            pl.BlockSpec((None, group, HEAD_DIM), whole),
+            pl.BlockSpec((None, group, HEAD_DIM), whole),
+            pl.BlockSpec((None, 1, group), whole),
+            pl.BlockSpec((QUERY_BLOCK, 1), row),
+            pl.BlockSpec((QUERY_BLOCK, 1), row),
+        ],
+        out_specs=[
+            pl.BlockSpec((QUERY_BLOCK, HEAD_DIM), head),
+            pl.BlockSpec((None, QUERY_BLOCK, 1), lambda g, a, i: (a, g * blocks + i, 0)),
+        ],
+        out_shape=[
+            jax.ShapeDtypeStruct((tokens, 2 * HEAD_DIM), f32),
+            jax.ShapeDtypeStruct((2, tokens, 1), f32),
+        ],
+        compiler_params=pltpu.CompilerParams(vmem_limit_bytes=48 * 1024 * 1024),
+        cost_estimate=pl.CostEstimate(flops=4 * 2 * tokens * group * HEAD_DIM, bytes_accessed=12_000_000, transcendentals=2 * tokens * group),
+        name="attend",
+    )(queries, keys, values, key_index, query_index, first_index)
+
+
+def attend_back_kernel(q_ref, do_ref, k_ref, v_ref, kidx_ref, qidx_ref, first_ref, lse_ref, delta_ref, dq_ref, dk_ref, dv_ref):
+    scale = 1.0 / math.sqrt(HEAD_DIM)
+
+    @pl.when((pl.program_id(1) == 0) & (pl.program_id(2) == 0))
+    def _():
+        dk_ref[...] = jnp.zeros_like(dk_ref)
+        dv_ref[...] = jnp.zeros_like(dv_ref)
+
+    queries = q_ref[...]
+    grad = do_ref[...]
+    keys = k_ref[...]
+    scores = lax.dot_general(keys, queries, (((1,), (1,)), ((), ())), preferred_element_type=f32)
+    index = kidx_ref[...]
+    seen = (index >= first_ref[...]) & (index <= qidx_ref[...])
+    probs = jnp.where(seen, jnp.exp(scores * scale - lse_ref[...]), 0.0)
+    dv_ref[...] += jnp.dot(probs.astype(bf16), grad, preferred_element_type=f32)
+    grad_probs = lax.dot_general(v_ref[...], grad, (((1,), (1,)), ((), ())), preferred_element_type=f32)
+    grad_scores = (probs * (grad_probs - delta_ref[...]) * scale).astype(bf16)
+    dk_ref[...] += jnp.dot(grad_scores, queries, preferred_element_type=f32)
+    dq_ref[...] = lax.dot_general(grad_scores, keys, (((0,), (0,)), ((), ())), preferred_element_type=f32)
+
+
+def attend_back(queries, grads, keys, values, key_index, query_index, first_index, lse, delta):
+    tokens = queries.shape[0]
+    group = keys.shape[1]
+    blocks = tokens // 2 // QUERY_BLOCK
+    row = lambda g, a, i: (0, g * blocks + i)
+    head = lambda g, a, i: (g * blocks + i, a)
+    whole = lambda g, a, i: (g, 0, 0)
+    stat = lambda g, a, i: (a, 0, g * blocks + i)
+    return pl.pallas_call(
+        attend_back_kernel,
+        grid=(2, 2, blocks),
+        in_specs=[
+            pl.BlockSpec((QUERY_BLOCK, HEAD_DIM), head),
+            pl.BlockSpec((QUERY_BLOCK, HEAD_DIM), head),
+            pl.BlockSpec((None, group, HEAD_DIM), whole),
+            pl.BlockSpec((None, group, HEAD_DIM), whole),
+            pl.BlockSpec((None, group, 1), whole),
+            pl.BlockSpec((1, QUERY_BLOCK), row),
+            pl.BlockSpec((1, QUERY_BLOCK), row),
+            pl.BlockSpec((None, 1, QUERY_BLOCK), stat),
+            pl.BlockSpec((None, 1, QUERY_BLOCK), stat),
+        ],
+        out_specs=[
+            pl.BlockSpec((QUERY_BLOCK, HEAD_DIM), head),
+            pl.BlockSpec((None, group, HEAD_DIM), whole),
+            pl.BlockSpec((None, group, HEAD_DIM), whole),
+        ],
+        out_shape=[
+            jax.ShapeDtypeStruct((tokens, 2 * HEAD_DIM), f32),
+            jax.ShapeDtypeStruct((2, group, HEAD_DIM), f32),
+            jax.ShapeDtypeStruct((2, group, HEAD_DIM), f32),
+        ],
+        compiler_params=pltpu.CompilerParams(vmem_limit_bytes=48 * 1024 * 1024),
+        cost_estimate=pl.CostEstimate(flops=10 * 2 * tokens * group * HEAD_DIM, bytes_accessed=18_000_000, transcendentals=2 * tokens * group),
+        name="attend_back",
+    )(queries, grads, keys, values, key_index, query_index, first_index, lse, delta)
+
+
+def plane_local(
+    tokens,
+    positions,
+    cotangent,
+    norm_in_gain,
+    q_down,
+    q_gain,
+    q_up,
+    key_proj,
+    value_proj,
+    out_proj,
+    norm_mid_gain,
+    w_gate,
+    w_up,
+    w_down,
+):
+    rows, width = tokens.shape
+    rank_dim = q_down.shape[1]
+    hidden_size = w_gate.shape[1]
+    dp = lax.axis_index("dp")
+    seq = lax.axis_index("seq")
+    y, x = dp // 2, dp % 2
+    h, l, c = seq // 4, (seq // 2) % 2, seq % 2
+    device = dp * 8 + seq
+    rank = x * 4 + l * 2 + c
+
+    d_rows = q_down.shape[0]
+    gain_rows = lambda gain: jnp.pad(gain, (0, d_rows - gain.shape[0]))
+    gains = jnp.stack([norm_in_gain, gain_rows(q_gain), norm_mid_gain], axis=1)
+    gains = jnp.pad(gains, ((0, 0), (0, 125)))
+    first_set = jnp.concatenate([q_down, key_proj, value_proj, gains], axis=1).astype(bf16)
+    split = rank_dim + 2 * HEAD_DIM
+
+    place = jnp.arange(32, dtype=jnp.int32)
+    block_order = place ^ device
+    order = (block_order[:, None] * d_rows + jnp.arange(d_rows, dtype=jnp.int32)[None, :]).reshape(-1)
+    permute = (jnp.arange(width, dtype=jnp.int32)[:, None] == order[None, :]).astype(bf16)
+    block_permute = (place[:, None] == block_order[None, :]).astype(f32)
+    exact = lax.Precision.HIGHEST
+
+    places = gather_small(positions)
+    blocks = jnp.arange(8, dtype=jnp.int32) ^ rank
+    in_group = h * (4 * rows) + (blocks % 4)[:, None] * rows + jnp.arange(rows, dtype=jnp.int32)[None, :]
+    query_index = in_group.reshape(-1)
+    first_index = (in_group - places).reshape(-1)
+    own_keys = in_group.reshape(2, 4 * rows)
+    far_keys = own_keys + (1 - 2 * h) * (4 * rows)
+    key_index = jnp.concatenate([own_keys, far_keys], axis=1)
+    cosine, sine = rope_table(places.reshape(-1))
+
+    up_query_pieces = (
+        q_up.astype(bf16)
+        .reshape(-1, 2, 2, 2, 2, HEAD_DIM)
+        .transpose(2, 4, 3, 0, 1, 5)
+        .reshape(8, -1, 2 * HEAD_DIM)
+    )
+    slice_size = hidden_size // 8
+    piece_size = hidden_size // 32
+
+    def hidden_pieces(weight):
+        return (
+            weight.reshape(-1, 2, 2, 2, 4, piece_size)
+            .transpose(2, 4, 0, 1, 3, 5)
+            .reshape(8, -1, slice_size)
+        )
+
+    gate_up_pieces = jnp.stack([hidden_pieces(w_gate.astype(bf16)), hidden_pieces(w_up.astype(bf16))], 1)
+    first_set, up_query, gate_up_set = head(first_set, up_query_pieces, gate_up_pieces)
+    first_set = first_set.reshape(width, -1)
+    first_weight = first_set[:, :split]
+    up_query = up_query.reshape(rank_dim, 2 * HEAD_DIM)
+    out_rows = out_proj.shape[0]
+    down_weight = gather_rows(w_down.astype(bf16)[None], y, h).reshape(slice_size, width)
+
+    inputs = tokens.astype(f32)
+    inputs_rel = jnp.dot(tokens, permute, preferred_element_type=f32)
+    in_scale = rms_scale(inputs)
+    in_gain = first_set[:, split].astype(f32)
+    gain_blocks = first_set.reshape(32, d_rows, -1)
+    query_gain = jnp.dot(block_permute, gain_blocks[:, : q_gain.shape[0], split + 1].astype(f32), precision=exact).reshape(-1)
+    mid_gain = jnp.dot(block_permute, gain_blocks[:, :, split + 2].astype(f32), precision=exact).reshape(-1)
+    normed = (inputs_rel * in_scale * in_gain).astype(bf16)
+    mixed = jnp.dot(normed, first_weight, preferred_element_type=f32)
+    compressed = mixed[:, :rank_dim]
+    query_scale = rms_scale(compressed)
+    compressed_normed = (compressed * query_scale * query_gain).astype(bf16)
+    own_cosine, own_sine = cosine[:rows], sine[:rows]
+    keys = turn(mixed[:, rank_dim : rank_dim + HEAD_DIM], own_cosine, own_sine, 1.0).astype(bf16)
+    values = mixed[:, rank_dim + HEAD_DIM :].astype(bf16)
+    plane_set, out_weight = pack(
+        jnp.concatenate([compressed_normed, keys, values], axis=1), out_proj.astype(bf16)
+    )
+    out_weight = out_weight.reshape(2 * HEAD_DIM, width)
+    plane_set = plane_set.reshape(2, 4 * rows, -1)
+    plane_normed = plane_set.reshape(8 * rows, -1)[:, :rank_dim]
+    own_kv, far_kv = plane_set[..., rank_dim:split], plane_set[..., split:]
+    group_kv = jnp.concatenate([own_kv, far_kv], axis=1)
+    group_keys, group_values = group_kv[..., :HEAD_DIM], group_kv[..., HEAD_DIM:]
+
+    queries = jnp.dot(plane_normed, up_query, preferred_element_type=f32).reshape(8 * rows, 2, HEAD_DIM)
+    queries = turn(queries, cosine[:, None], sine[:, None], 1.0).astype(bf16).reshape(8 * rows, 2 * HEAD_DIM)
+    attended_full, log_total = attend(
+        queries, group_keys, group_values, key_index[:, None, :], query_index[:, None], first_index[:, None]
+    )
+    attended = attended_full.astype(bf16)
+    out_parts = jnp.dot(attended, out_weight, preferred_element_type=f32).astype(bf16)
+    attention_sum, gate_weight = middle_sum(out_parts.reshape(2, 2, 2, rows, width), gate_up_set[0])
+    middle = inputs + attention_sum
+    gate_weight = gate_weight.reshape(width, slice_size)
+
+    mid_scale = rms_scale(middle)
+    normed_mid = (middle * mid_scale * mid_gain).astype(bf16)
+    plane_cotangent = gather_plane(cotangent).reshape(8 * rows, width)
+    plane_mid, up_weight = feed_gather(normed_mid, gate_up_set[1])
+    plane_mid = plane_mid.reshape(8 * rows, width)
+    up_weight = up_weight.reshape(width, slice_size)
+    gate = jnp.dot(plane_mid, gate_weight, preferred_element_type=f32)
+    upper = jnp.dot(plane_mid, up_weight, preferred_element_type=f32)
+    sigmoid_gate = jax.nn.sigmoid(gate)
+    silu_gate = gate * sigmoid_gate
+    hidden = (silu_gate * upper).astype(bf16)
+    grad_hidden = lax.dot_general(plane_cotangent, down_weight, (((1,), (1,)), ((), ())), preferred_element_type=f32)
+    grad_gate = (grad_hidden * upper * sigmoid_gate * (1.0 + gate * (1.0 - sigmoid_gate))).astype(bf16)
+    grad_upper = (grad_hidden * silu_gate).astype(bf16)
+    mid_parts = lax.dot_general(grad_gate, gate_weight, (((1,), (1,)), ((), ())), preferred_element_type=f32)
+    mid_parts = mid_parts + lax.dot_general(grad_upper, up_weight, (((1,), (1,)), ((), ())), preferred_element_type=f32)
+    final_parts = jnp.dot(hidden, down_weight, preferred_element_type=f32).astype(bf16)
+    output = (middle + scatter_plane(final_parts.reshape(8, rows, width))).astype(bf16)
+
+    def over_tokens(left, right):
+        return lax.dot_general(left, right, (((0,), (0,)), ((), ())), preferred_element_type=f32)
+
+    grad_down = over_tokens(hidden, plane_cotangent).astype(bf16).reshape(2, 2, piece_size, width)
+    grad_normed_mid, grad_down = mid_sum(mid_parts.astype(bf16).reshape(2, 2, 2, rows, width), grad_down)
+
+    def hidden_whole(pieces):
+        return (
+            pieces.reshape(2, 4, -1, 2, 2, piece_size)
+            .transpose(2, 3, 0, 4, 1, 5)
+            .reshape(-1, hidden_size)
+            .astype(f32)
+        )
+
+    by_rows = lambda grad: grad.astype(bf16).reshape(2, 2, 2, -1, grad.shape[-1])
+    grad_gate_weight = by_rows(over_tokens(plane_mid, grad_gate))
+    grad_up_weight = by_rows(over_tokens(plane_mid, grad_upper))
+
+    grad_mid_norm, grad_mid_gain = norm_backward(middle, mid_scale, mid_gain, grad_normed_mid)
+    grad_middle = cotangent.astype(f32) + grad_mid_norm
+    branch_grad = grad_middle.astype(bf16)
+    plane_branch, grad_gate_weight = branch_gather(branch_grad, grad_gate_weight)
+    plane_branch = plane_branch.reshape(8 * rows, width)
+    grad_gate_weight = hidden_whole(grad_gate_weight)
+    grad_out = over_tokens(attended, plane_branch).astype(bf16).reshape(2, 2, out_rows, width)
+
+    grad_attended = lax.dot_general(plane_branch, out_weight, (((1,), (1,)), ((), ())), preferred_element_type=f32)
+    grad_attended = grad_attended.astype(bf16)
+    delta = jnp.sum((grad_attended.astype(f32) * attended_full).reshape(8 * rows, 2, HEAD_DIM), axis=-1)
+    grad_query, grad_keys, grad_values = attend_back(
+        queries,
+        grad_attended,
+        group_keys,
+        group_values,
+        key_index[:, :, None],
+        query_index[None, :],
+        first_index[None, :],
+        log_total.reshape(2, 1, 8 * rows),
+        delta.T.reshape(2, 1, 8 * rows),
+    )
+    grad_query_pre = turn(grad_query.reshape(8 * rows, 2, HEAD_DIM), cosine[:, None], sine[:, None], -1.0)
+    grad_query_pre = grad_query_pre.reshape(8 * rows, 2 * HEAD_DIM).astype(bf16)
+    grad_up_query = by_rows(over_tokens(plane_normed, grad_query_pre))
+    normed_parts = lax.dot_general(grad_query_pre, up_query, (((1,), (1,)), ((), ())), preferred_element_type=f32)
+    key_value_parts = jnp.concatenate([grad_keys, grad_values], axis=-1).astype(bf16)
+    key_value_parts = key_value_parts.reshape(2, 2, 4, rows, 2 * HEAD_DIM)
+    back_set = jnp.concatenate(
+        [
+            normed_parts.astype(bf16).reshape(8, rows, rank_dim),
+            key_value_parts[:, 0].reshape(8, rows, -1),
+            key_value_parts[:, 1].reshape(8, rows, -1),
+        ],
+        axis=-1,
+    )
+    back_total, grad_up_weight = back_sum(back_set.reshape(2, 2, 2, rows, 2 * rank_dim), grad_up_weight)
+    grad_up_weight = hidden_whole(grad_up_weight)
+    grad_compressed_normed = back_total[:, :rank_dim]
+    kv_grad = back_total[:, rank_dim:split] + swap(back_total[:, split:].astype(bf16), "h").astype(f32)
+    grad_key_pre = turn(kv_grad[:, :HEAD_DIM], own_cosine, own_sine, -1.0).astype(bf16)
+    grad_value_pre = kv_grad[:, HEAD_DIM:].astype(bf16)
+    grad_compressed, grad_query_gain = norm_backward(compressed, query_scale, query_gain, grad_compressed_normed)
+    mixed_grad = jnp.concatenate([grad_compressed.astype(bf16), grad_key_pre, grad_value_pre], axis=1)
+    grad_normed = lax.dot_general(mixed_grad, first_weight, (((1,), (1,)), ((), ())), preferred_element_type=f32)
+    grad_in_norm, grad_in_gain = norm_backward(inputs_rel, in_scale, in_gain, grad_normed)
+    grad_in_norm = lax.dot_general(grad_in_norm.astype(bf16), permute, (((1,), (1,)), ((), ())), preferred_element_type=f32)
+    grad_tokens = (grad_middle + grad_in_norm).astype(bf16)
+
+    to_relative = lambda gain: lax.dot_general(
+        block_permute, gain.reshape(32, -1), (((0,), (0,)), ((), ())), precision=exact
+    )
+    grad_gains = jnp.stack(
+        [
+            grad_in_gain.reshape(32, d_rows),
+            jnp.pad(to_relative(grad_query_gain), ((0, 0), (0, d_rows - q_gain.shape[0]))),
+            to_relative(grad_mid_gain),
+        ],
+        axis=-1,
+    ).reshape(width, 3)
+    first_grad = over_tokens(normed, mixed_grad).astype(bf16)
+    first_grad = jnp.concatenate([first_grad, jnp.pad(grad_gains, ((0, 0), (0, 125))).astype(bf16)], axis=1)
+    total, grad_up_query, grad_output_weight = tail(
+        first_grad.reshape(2, 2, 2, 2, 2, d_rows, -1), grad_up_query, grad_out
+    )
+    grad_up_query = (
+        grad_up_query.reshape(2, 2, 2, -1, 2, HEAD_DIM)
+        .transpose(3, 4, 0, 2, 1, 5)
+        .reshape(q_up.shape)
+        .astype(f32)
+    )
+    return (
+        output,
+        grad_tokens,
+        total[:, split],
+        total[:, :rank_dim],
+        total[: q_gain.shape[0], split + 1],
+        grad_up_query,
+        total[:, rank_dim : rank_dim + HEAD_DIM],
+        total[:, rank_dim + HEAD_DIM : split],
+        grad_output_weight,
+        total[:, split + 2],
+        grad_gate_weight,
+        grad_up_weight,
+        grad_down,
+    )
+
+
+def gather_small(value):
+    value = value[None]
+    for bit in "clx":
+        value = jnp.concatenate([value, swap(value, bit)])
+    return value
+
+
 def solution(mesh):
     return jax.shard_map(
-        local,
+        plane_local if dict(mesh.shape) == {"dp": 4, "seq": 8} else local,
         mesh=mesh,
         in_specs=(
             P(("dp", "seq"), None),

time: 3570 us -> 937 us (0.26)
  waiting for transfers between devices: 2900 us -> 16.9 us
  Pallas kernels: 0 us -> 574 us
  matrix products: 390 us -> 133 us
  blocking collectives: 115 us -> 0 us
  local copies, waits for them, and re-layouts: 72.8 us -> 129 us
    reduce_scatter x10 -> x0, waiting for transfers between devices: 2340 us -> none  [the longest x1 491 us: local(): lax.psum_scatter(grad_up_weight, ('dp', 'seq'), scatter_dimension=0, tile...]
    pallas_call x0 -> x10, Pallas kernels: none -> 574 us  [the longest x8 532 us: moving(): pl.pallas_call(kernel, out_shape=outs, in_specs=in_specs or [ANY] * len(o...]
    all_gather x8 -> x0, waiting for transfers between devices: 556 us -> none  [the longest x1 134 us: local(): lax.all_gather(w_up.astype(jnp.bfloat16), ('dp', 'seq'), axis=0, tiled=True)]
    dot_general x80 -> x24, matrix products: 390 us -> 133 us  [the longest x6 38.7 us: over_tokens(): lax.dot_general(left, right, (((0,), (0,)), ((), ())), preferred_element_...]
    unnamed x2 -> x0, blocking collectives: 80.6 us -> none
  transfers between devices with their start and end apart: 18 -> 20, of which waited for: 16 -> 5; matrix products, arithmetic and copies ran while one was open for 8% -> 18% of each run, Pallas kernels for 0% -> 36%
where the time goes in v1:
time: 937 us; the launch traced here: 929 us
  Pallas kernels  574 us (61%)
  matrix products  133 us (14%)
  local copies, waits for them, and re-layouts  129 us (14%)
  other arithmetic  50.7 us (5%)
  starting transfers between devices  22.3 us (2%)
  waiting for transfers between devices  16.9 us (2%)
    pallas_call x8, Pallas kernels, moving(): pl.pallas_call(kernel, out_shape=outs, in_specs=in_specs or [ANY] * len(o...  532 us
    dot_general x6, matrix products, over_tokens(): lax.dot_general(left, right, (((0,), (0,)), ((), ())), preferred_element_...  38.7 us
    unnamed x187, local copies, waits for them, and re-layouts  34.3 us
    pallas_call x1, Pallas kernels, attend_back(): pl.pallas_call(attend_back_kernel, grid=(2, 2, blocks), in_specs=[pl.Bloc...  23.1 us
    ppermute x20, starting transfers between devices, swap(): lax.ppermute(value, axis, [(i, i ^ mask) for i in range(lax.axis_size(axi...  22.3 us
    convert_element_type x6, local copies, waits for them, and re-layouts, hidden_whole(): return pieces.reshape(2, 4, -1, 2, 2, piece_size).transpose(2, 3, 0, 4, 1...  21.4 us
  transfers between devices with their start and end apart: 20, of which 5 were waited for; matrix products, arithmetic and copies ran while one was open for 18% of the time, Pallas kernels for 36%

profile of v1, /device:TPU:0, one launch (start us, length us, event | category | flops | bytes accessed | tf_op | source)
XLA Modules:
  0.0 928.8 jit_solution(14825329315298074217)
XLA Ops:
  0.7 2.4 convert_bitcast_fusion
  3.1 3.0 collective-permute-start.4
  6.1 2.6 collective-permute-start.3
  10.4 2.2 bitcast_dynamic-update-slice_fusion.7
  19.4 2.1 reshape.420
  23.5 71.1 %head_kernel.1 = (bf16[2,2,2,2,2,64,1664]{6,5,4,3,2,1,0:T(8,128)(2,1)}, bf16[2,2,2,128,512]{4,3,2,1,0:T(8,128)(2,1)S(1)}, bf16[2,2,256,704]{3,2,1,0:T(8,128)(2,1)S(1)}) custom-call(bf16[64,1664]{1,0:T(8,128)(2,1)S(1)} %fusion.41.first, bf16[8,32,512]{2,1,0:T(8,128)(2,1)S(1)} %reshape.418.upq, bf16[8,2,64,704]{3,2,1,0:T(8,128)(2,1)S(1)} %pad_maximum_fusion.4.gu), custom_call_target="tpu_custom_call" | custom-call | bytes 1048576 | tf_op jit(solution)/shard_map/head_kernel/pallas_call | solution.py:486
  100.6 4.6 fusion.14
  108.7 4.7 fusion.6
  132.4 4.4 broadcast_multiply_fusion
  138.3 2.6 copy.124
  143.3 69.1 %pack_kernel.1 = (bf16[2,2,2,192,2048]{4,3,2,1,0:T(8,128)(2,1)}, bf16[2,2,128,2048]{3,2,1,0:T(8,128)(2,1)S(1)}, bf16[2,2,128,2048]{3,2,1,0:T(8,128)(2,1)}) custom-call(bf16[192,1536]{1,0:T(8,128)(2,1)S(1)} %pad_maximum_fusion.6.block, bf16[128,2048]{1,0:T(8,128)(2,1)S(1)} %convert_element_type.246.out_weight), custom_call_target="tpu_custom_call" | custom-call | bytes 1048576 | tf_op jit(solution)/shard_map/pack_kernel/pallas_call | solution.py:486
  212.4 4.5 fusion.9
  218.8 2.1 copy.148.q_ref
  220.9 2.7 fusion.61
  225.6 18.2 %attend.1 = (f32[1536,512]{1,0:T(8,128)}, f32[2,1536,1]{2,1,0:T(8,128)S(1)}) custom-call(bf16[1536,512]{1,0:T(8,128)(2,1)S(1)} %copy.148.q_ref, bf16[2,1536,256]{2,1,0:T(8,128)(2,1)} %get-tuple-element.85.k_ref, bf16[2,1536,256]{2,1,0:T(8,128)(2,1)} %get-tuple-element.84.v_ref, s32[2,1,1536]{2,1,0:T(1,128)S(1)} %broadcast_in_dim.17.kidx_ref, ...), custom_call_target="tpu_custom_call" | custom-call | flops 4831838208 | bytes 12000000 | tf_op jit(solution)/shard_map/attend/pallas_call | solution.py:1072
  243.8 7.8 convolution_convert_fusion.2
  251.6 61.6 %middle_kernel.1 = (f32[192,2048]{1,0:T(8,128)S(1)}, bf16[2,2,2,256,704]{4,3,2,1,0:T(8,128)(2,1)S(1)}) custom-call(bf16[2,2,2,192,2048]{4,3,2,1,0:T(8,128)(2,1)} %bitcast.182, bf16[2,256,704]{2,1,0:T(8,128)(2,1)S(1)} %get-tuple-element.93.gate), custom_call_target="tpu_custom_call" | custom-call | bytes 1048576 | tf_op jit(solution)/shard_map/middle_kernel/pallas_call | solution.py:486
  313.7 65.9 %feed_kernel.1 = (bf16[2,2,2,192,2048]{4,3,2,1,0:T(8,128)(2,1)}, bf16[2,2,2,256,704]{4,3,2,1,0:T(8,128)(2,1)S(1)}) custom-call(bf16[192,2048]{1,0:T(8,128)(2,1)S(1)} %multiply_convert_fusion.3.block, bf16[2,256,704]{2,1,0:T(8,128)(2,1)S(1)} %get-tuple-element.92.up), custom_call_target="tpu_custom_call" | custom-call | bytes 1048576 | tf_op jit(solution)/shard_map/feed_kernel/pallas_call | solution.py:486
  379.7 10.7 %fusion.64 = f32[1536,704]{0,1:T(8,128)} fusion(bf16[1536,2048]{1,0:T(8,128)(2,1)} %bitcast.215, bf16[2048,704]{1,0:T(8,128)(2,1)S(1)} %bitcast.173), kind=kOutput, calls=%fused_computation.191 | convolution fusion | flops 4429185024 | bytes 13500416 | tf_op jit(solution)/shard_map/dot_general | solution.py:1274
  390.5 6.7 fusion.63
  400.9 2.1 bitcast_dynamic-update-slice_fusion.10
  403.0 2.1 bitcast_dynamic-update-slice_fusion.9
  408.8 2.2 bitcast_dynamic-update-slice_fusion.6
  411.0 2.1 bitcast_dynamic-update-slice_fusion.5
  413.1 4.2 collective-permute-done.16
  419.7 2.1 bitcast_dynamic-update-slice_fusion.3
  424.6 10.3 %multiply_convert_fusion = (bf16[1536,704]{0,1:T(8,128)(2,1)S(1)}, bf16[1536,704]{0,1:T(8,128)(2,1)S(1)}, bf16[1536,704]{0,1:T(8,128)(2,1)}) fusion(f32[1536,704]{0,1:T(8,128)S(1)} %copy-done.81, f32[1536,704]{0,1:T(8,128)S(1)} %bitcast.224, bf16[1536,2048]{1,0:T(8,128)(2,1)} %bitcast.212, bf16[704,2048]{1,0:T(8,128)(2,1)S(1)} %bitcast.193), kind=kOutput, calls=%fused_computation.17 | convolution fusion | flops 4445405184 | bytes 24313856 | tf_op jit(solution)/shard_map/dot_general | solution.py:1278
  434.9 7.7 convolution_convert_fusion.6
  442.6 5.4 convolution_convert_fusion.1
  449.9 8.3 fusion.65
  458.3 6.0 convolution_convert_fusion.4
  464.2 10.1 %add_convert_fusion = bf16[1536,2048]{1,0:T(8,128)(2,1)} fusion(f32[1536,2048]{1,0:T(8,128)} %fusion.65, bf16[1536,704]{0,1:T(8,128)(2,1)S(1)} %get-tuple-element.71, bf16[2048,704]{1,0:T(8,128)(2,1)S(1)} %bitcast.174), kind=kOutput, calls=%fused_computation.3 | convolution fusion | flops 4435476480 | bytes 23920640 | tf_op jit(solution)/shard_map/dot_general | solution.py:1282
  482.4 7.9 convolution_convert_fusion.5
  490.3 2.9 copy.132
  493.2 3.1 copy.142
  498.1 50.3 %mid_sum_kernel.1 = (f32[192,2048]{1,0:T(8,128)S(1)}, f32[176,2048]{1,0:T(8,128)S(1)}) custom-call(bf16[2,2,2,192,2048]{4,3,2,1,0:T(8,128)(2,1)} %bitcast.181, bf16[2,2,176,2048]{3,2,1,0:T(8,128)(2,1)S(1)} %bitcast.166), custom_call_target="tpu_custom_call" | custom-call | bytes 1048576 | tf_op jit(solution)/shard_map/mid_sum_kernel/pallas_call | solution.py:486
  550.5 2.8 fusion.21
  555.7 8.9 collective-permute-done.10
  565.4 2.9 fusion.60
  568.4 80.2 %branch_kernel.1 = (bf16[2,2,2,192,2048]{4,3,2,1,0:T(8,128)(2,1)}, bf16[8,64,704]{2,1,0:T(8,128)(2,1)S(1)}) custom-call(bf16[192,2048]{1,0:T(8,128)(2,1)S(1)} %get-tuple-element.90.block, bf16[2,2,2,256,704]{4,3,2,1,0:T(8,128)(2,1)S(1)} %bitcast.165), custom_call_target="tpu_custom_call" | custom-call | bytes 1048576 | tf_op jit(solution)/shard_map/branch_kernel/pallas_call | solution.py:486
  648.6 7.8 convolution_convert_fusion.7
  656.4 5.3 convert_multiply_fusion
  661.7 5.1 reshape.437
  666.8 5.1 reduce_sum.94
  677.6 23.1 %attend_back.1 = (f32[1536,512]{1,0:T(8,128)}, f32[2,1536,256]{2,1,0:T(8,128)}, f32[2,1536,256]{2,1,0:T(8,128)}) custom-call(bf16[1536,512]{1,0:T(8,128)(2,1)S(1)} %copy-done.9, bf16[1536,512]{1,0:T(8,128)(2,1)S(1)} %copy-done.34, bf16[2,1536,256]{2,1,0:T(8,128)(2,1)S(1)} %copy-done.12, bf16[2,1536,256]{2,1,0:T(8,128)(2,1)} %get-tuple-element.84.v_ref, ...), custom_call_target="tpu_custom_call" | custom-call | flops 12079595520 | bytes 18000000 | tf_op jit(solution)/shard_map/attend_back/pallas_call | solution.py:1127
  700.7 3.8 copy.150
  704.5 2.9 multiply_subtract_fusion
  707.5 4.8 fusion.23
  716.6 3.2 pad_maximum_fusion.1.parts
  719.8 62.8 %back_sum_kernel.1 = (f32[192,2048]{1,0:T(8,128)S(1)}, bf16[8,64,704]{2,1,0:T(8,128)(2,1)S(1)}) custom-call(bf16[2,2,2,192,2048]{4,3,2,1,0:T(8,128)(2,1)} %pad_maximum_fusion.1.parts, bf16[2,2,2,256,704]{4,3,2,1,0:T(8,128)(2,1)S(1)} %bitcast.164), custom_call_target="tpu_custom_call" | custom-call | bytes 1048576 | tf_op jit(solution)/shard_map/back_sum_kernel/pallas_call | solution.py:486
  786.9 4.6 reshape.453
  791.5 2.9 copy.146
  794.4 3.5 reshape.450
  797.9 3.3 reshape.452
  801.2 2.7 copy.145
  803.9 4.4 reshape.449
  809.8 6.2 multiply_reduce_fusion.1
  816.0 4.5 convolution_convert_fusion
  820.6 6.9 pad_maximum_fusion
  827.5 9.9 %copy.143 = bf16[2048,1664]{1,0:T(8,128)(2,1)} copy(bf16[2048,1664]{0,1:T(8,128)(2,1)} %pad_maximum_fusion) | data formatting | bytes 13631488 | tf_op jit(solution)/shard_map/concatenate | solution.py:1365
  837.4 71.2 %tail_kernel.1 = (f32[64,1664]{1,0:T(8,128)S(1)}, bf16[8,32,512]{2,1,0:T(8,128)(2,1)S(1)}, f32[128,2048]{1,0:T(8,128)S(1)}) custom-call(bf16[2,2,2,2,2,64,1664]{6,5,4,3,2,1,0:T(8,128)(2,1)} %bitcast.177, bf16[2,2,2,128,512]{4,3,2,1,0:T(8,128)(2,1)S(1)} %bitcast.168, bf16[2,2,128,2048]{3,2,1,0:T(8,128)(2,1)S(1)} %bitcast.167), custom_call_target="tpu_custom_call" | custom-call | bytes 1048576 | tf_op jit(solution)/shard_map/tail_kernel/pallas_call | solution.py:486
  913.5 2.2 copy.144
  915.7 2.3 reshape.448
  918.0 7.5 fusion.16
  (343 shorter events, 99.6 us)
Async XLA Ops:
  0.6 12.0 %copy-start.79 = (f32[32]{0:T(128)S(1)}, f32[32]{0:T(128)}, u32[]{:S(2)}) copy-start(f32[32]{0:T(128)} %param.19) | copy-start | bytes 388
  0.7 12.0 %copy-start.75 = (f32[64]{0:T(128)S(1)}, f32[64]{0:T(128)}, u32[]{:S(2)}) copy-start(f32[64]{0:T(128)} %param.24) | copy-start | bytes 772
  0.7 12.0 %copy-start.76 = (f32[64]{0:T(128)S(1)}, f32[64]{0:T(128)}, u32[]{:S(2)}) copy-start(f32[64]{0:T(128)} %param.17) | copy-start | bytes 772
  0.7 12.1 %copy-start.65 = (f32[64,256]{1,0:T(8,128)S(1)}, f32[64,256]{1,0:T(8,128)}, u32[]{:S(2)}) copy-start(f32[64,256]{1,0:T(8,128)} %param.21) | copy-start | bytes 196612
  0.7 12.1 %copy-start.66 = (f32[64,256]{1,0:T(8,128)S(1)}, f32[64,256]{1,0:T(8,128)}, u32[]{:S(2)}) copy-start(f32[64,256]{1,0:T(8,128)} %param.22) | copy-start | bytes 196612
  0.7 12.1 %copy-start.59 = (f32[64,1024]{1,0:T(8,128)S(1)}, f32[64,1024]{1,0:T(8,128)}, u32[]{:S(2)}) copy-start(f32[64,1024]{1,0:T(8,128)} %param.18) | copy-start | bytes 786436
  0.7 12.8 %copy-start.58 = (f32[32,4096]{1,0:T(8,128)S(1)}, f32[32,4096]{1,0:T(8,128)}, u32[]{:S(2)}) copy-start(f32[32,4096]{1,0:T(8,128)} %param.20) | copy-start | bytes 1572868
  3.1 399.9 %collective-permute-start.4 = (bf16[1,176,2048]{2,1,0:T(8,128)(2,1)}, bf16[1,176,2048]{2,1,0:T(8,128)(2,1)}, u32[]{:S(2)}, u32[]{:S(2)}) collective-permute-start(bf16[1,176,2048]{2,1,0:T(8,128)(2,1)} %convert_bitcast_fusion), channel_id=1, source_target_pairs={{0,16},{8,24},{16,0},{24,8},{1,17},{9,25},{17,1},{25,9},{2,18},{10... | collective-permute-start | bytes 2162696 | tf_op jit(solution)/shard_map/ppermute | solution.py:349
  6.1 393.3 %collective-permute-start.3 = (bf16[1,176,2048]{2,1,0:T(8,128)(2,1)}, bf16[1,176,2048]{2,1,0:T(8,128)(2,1)}, u32[]{:S(2)}, u32[]{:S(2)}) collective-permute-start(bf16[1,176,2048]{2,1,0:T(8,128)(2,1)} %convert_bitcast_fusion), channel_id=1, source_target_pairs={{0,4},{1,5},{2,6},{3,7},{4,0},{5,1},{6,2},{7,3},{8,12},{9,13},{10,... | collective-permute-start | bytes 2162696 | tf_op jit(solution)/shard_map/ppermute | solution.py:349
  8.7 399.7 %collective-permute-start.11 = (bf16[192,2048]{1,0:T(8,128)(2,1)}, bf16[192,2048]{1,0:T(8,128)(2,1)}, u32[]{:S(2)}, u32[]{:S(2)}) collective-permute-start(bf16[192,2048]{1,0:T(8,128)(2,1)} %param.16), channel_id=1, source_target_pairs={{0,1},{1,0},{2,3},{3,2},{4,5},{5,4},{6,7},{7,6},{8,9},{9,8},{10,11... | collective-permute-start | bytes 2359304 | tf_op jit(solution)/shard_map/ppermute | solution.py:349
  8.7 396.4 %collective-permute-start.14 = (bf16[192,2048]{1,0:T(8,128)(2,1)}, bf16[192,2048]{1,0:T(8,128)(2,1)}, u32[]{:S(2)}, u32[]{:S(2)}) collective-permute-start(bf16[192,2048]{1,0:T(8,128)(2,1)} %param.16), channel_id=1, source_target_pairs={{0,8},{8,0},{16,24},{24,16},{1,9},{9,1},{17,25},{25,17},{2,10},{10... | collective-permute-start | bytes 2359304 | tf_op jit(solution)/shard_map/ppermute | solution.py:349
  10.2 106.8 %collective-permute-start = (s32[1,192]{1,0:T(1,128)}, s32[1,192]{1,0:T(1,128)}, u32[]{:S(2)}, u32[]{:S(2)}) collective-permute-start(s32[1,192]{1,0:T(1,128)} %bitcast.11), channel_id=1, source_target_pairs={{0,1},{1,0},{2,3},{3,2},{4,5},{5,4},{6,7},{7,6},{8,9},{9,8},{10,11... | collective-permute-start | bytes 2312 | tf_op jit(solution)/shard_map/ppermute | solution.py:349
  98.8 8.3 copy-start.73
  100.2 8.5 copy-start.69
  105.8 7.9 copy-start.63
  117.0 12.1 %copy-start.17 = (bf16[2,2,2,128,512]{4,3,2,1,0:T(8,128)(2,1)S(1)}, bf16[2,2,2,128,512]{4,3,2,1,0:T(8,128)(2,1)}, u32[]{:S(2)}) copy-start(bf16[2,2,2,128,512]{4,3,2,1,0:T(8,128)(2,1)} %copy-done.16) | copy-start | bytes 3145732
  117.8 3.6 collective-permute-start.1
  122.1 8.3 collective-permute-start.2
  130.4 276.2 %collective-permute-start.12 = (bf16[192,2048]{1,0:T(8,128)(2,1)}, bf16[192,2048]{1,0:T(8,128)(2,1)}, u32[]{:S(2)}, u32[]{:S(2)}) collective-permute-start(bf16[192,2048]{1,0:T(8,128)(2,1)} %param.16), channel_id=1, source_target_pairs={{0,2},{1,3},{2,0},{3,1},{4,6},{5,7},{6,4},{7,5},{8,10},{9,11},{10,... | collective-permute-start | bytes 2359304 | tf_op jit(solution)/shard_map/ppermute | solution.py:349
  136.8 6.4 copy-start.54
  138.3 78.6 %copy-start.43 = (f32[1536,128]{0,1:T(8,128)}, f32[1536,128]{0,1:T(8,128)S(1)}, u32[]{:S(2)}) copy-start(f32[1536,128]{0,1:T(8,128)S(1)} %copy.123) | copy-start | bytes 2359300
  143.2 69.2 %copy-start.56 = (bf16[512,1024]{1,0:T(8,128)(2,1)S(1)}, bf16[512,1024]{1,0:T(8,128)(2,1)}, u32[]{:S(2)}) copy-start(bf16[512,1024]{1,0:T(8,128)(2,1)} %copy.122) | copy-start | bytes 3145732
  225.6 18.2 %copy-start.32 = (bf16[2,2,128,2048]{3,2,1,0:T(8,128)(2,1)S(1)}, bf16[2,2,128,2048]{3,2,1,0:T(8,128)(2,1)}, u32[]{:S(2)}) copy-start(bf16[2,2,128,2048]{3,2,1,0:T(8,128)(2,1)} %copy-done.31) | copy-start | bytes 6291460
  243.8 7.8 copy-start.10
  251.6 61.6 %copy-start.49 = (bf16[192,2048]{1,0:T(8,128)(2,1)S(1)}, bf16[192,2048]{1,0:T(8,128)(2,1)}, u32[]{:S(2)}) copy-start(bf16[192,2048]{1,0:T(8,128)(2,1)} %param.14) | copy-start | bytes 2359300
  313.2 77.3 %copy-start.27 = (bf16[2,2,2,256,704]{4,3,2,1,0:T(8,128)(2,1)}, bf16[2,2,2,256,704]{4,3,2,1,0:T(8,128)(2,1)S(1)}, u32[]{:S(2)}) copy-start(bf16[2,2,2,256,704]{4,3,2,1,0:T(8,128)(2,1)S(1)} %get-tuple-element.44) | copy-start | bytes 8650756
  313.5 76.9 %copy-start.35 = (f32[192,2048]{1,0:T(8,128)}, f32[192,2048]{1,0:T(8,128)S(1)}, u32[]{:S(2)}) copy-start(f32[192,2048]{1,0:T(8,128)S(1)} %get-tuple-element.68) | copy-start | bytes 4718596
  379.7 10.8 %copy-start.29 = (bf16[2,2,2,256,704]{4,3,2,1,0:T(8,128)(2,1)}, bf16[2,2,2,256,704]{4,3,2,1,0:T(8,128)(2,1)S(1)}, u32[]{:S(2)}) copy-start(bf16[2,2,2,256,704]{4,3,2,1,0:T(8,128)(2,1)S(1)} %get-tuple-element.45) | copy-start | bytes 8650756
  379.7 10.8 %copy-start.77 = (bf16[2,2,2,192,2048]{4,3,2,1,0:T(8,128)(2,1)S(1)}, bf16[2,2,2,192,2048]{4,3,2,1,0:T(8,128)(2,1)}, u32[]{:S(2)}) copy-start(bf16[2,2,2,192,2048]{4,3,2,1,0:T(8,128)(2,1)} %get-tuple-element.43) | copy-start | bytes 18874372
  390.5 6.8 copy-start.50
  399.4 19.2 %collective-permute-start.5 = (bf16[1,176,2048]{2,1,0:T(8,128)(2,1)}, bf16[1,176,2048]{2,1,0:T(8,128)(2,1)S(1)}, u32[]{:S(2)}, u32[]{:S(2)}) collective-permute-start(bf16[1,176,2048]{2,1,0:T(8,128)(2,1)} %collective-permute-done.3), channel_id=1, source_target_pairs={{0,16},{8,24},{16,0},{24,8},{1,17},{9,25},{17,1},{25,9},{2,18},{10... | collective-permute-start | bytes 2162696 | tf_op jit(solution)/shard_map/ppermute | solution.py:349
  406.1 11.2 %collective-permute-start.16 = (bf16[96,2048]{1,0:T(8,128)(2,1)S(1)}, bf16[96,2048]{1,0:T(8,128)(2,1)S(1)}, u32[]{:S(2)}, u32[]{:S(2)}) collective-permute-start(bf16[96,2048]{1,0:T(8,128)(2,1)S(1)} %slice.234), channel_id=1, source_target_pairs={{0,2},{1,3},{2,0},{3,1},{4,6},{5,7},{6,4},{7,5},{8,10},{9,11},{10,... | collective-permute-start | bytes 1179656 | tf_op jit(solution)/shard_map/ppermute | solution.py:349
  407.6 11.0 %copy-start.52 = (bf16[2,1,2,176,2048]{4,3,2,1,0:T(8,128)(2,1)S(1)}, bf16[2,1,2,176,2048]{4,3,2,1,0:T(8,128)(2,1)}, u32[]{:S(2)}) copy-start(bf16[2,1,2,176,2048]{4,3,2,1,0:T(8,128)(2,1)} %bitcast_dynamic-update-slice_fusion.9) | copy-start | bytes 8650756
  407.6 10.9 %collective-permute-start.17 = (bf16[96,2048]{1,0:T(8,128)(2,1)S(1)}, bf16[96,2048]{1,0:T(8,128)(2,1)S(1)}, u32[]{:S(2)}, u32[]{:S(2)}) collective-permute-start(bf16[96,2048]{1,0:T(8,128)(2,1)S(1)} %slice.235), channel_id=1, source_target_pairs={{0,8},{8,0},{16,24},{24,16},{1,9},{9,1},{17,25},{25,17},{2,10},{10... | collective-permute-start | bytes 1179656 | tf_op jit(solution)/shard_map/ppermute | solution.py:349
  408.3 13.5 %collective-permute-start.15 = (bf16[192,2048]{1,0:T(8,128)(2,1)}, bf16[192,2048]{1,0:T(8,128)(2,1)S(1)}, u32[]{:S(2)}, u32[]{:S(2)}) collective-permute-start(bf16[192,2048]{1,0:T(8,128)(2,1)} %collective-permute-done.14), channel_id=1, source_target_pairs={{0,1},{1,0},{2,3},{3,2},{4,5},{5,4},{6,7},{7,6},{8,9},{9,8},{10,11... | collective-permute-start | bytes 2359304 | tf_op jit(solution)/shard_map/ppermute | solution.py:349
  408.4 10.3 %collective-permute-start.13 = (bf16[192,2048]{1,0:T(8,128)(2,1)}, bf16[192,2048]{1,0:T(8,128)(2,1)S(1)}, u32[]{:S(2)}, u32[]{:S(2)}) collective-permute-start(bf16[192,2048]{1,0:T(8,128)(2,1)} %collective-permute-done.12), channel_id=1, source_target_pairs={{0,1},{1,0},{2,3},{3,2},{4,5},{5,4},{6,7},{7,6},{8,9},{9,8},{10,11... | collective-permute-start | bytes 2359304 | tf_op jit(solution)/shard_map/ppermute | solution.py:349
  408.8 15.8 %slice-start.2 = ((s8[4325376]{0:T(1024)(128)(4,1)}), s8[4194304]{0:T(1024)(128)(4,1)S(1)}, s32[]{:S(2)}) async-start(s8[4325376]{0:T(1024)(128)(4,1)} %bitcast.223), calls=%async_computation.2 | async-start | bytes 8388608
  418.5 5.1 collective-permute-start.18
  424.6 10.3 %copy-start.62 = (bf16[8,192,2048]{2,1,0:T(8,128)(2,1)S(1)}, bf16[8,192,2048]{2,1,0:T(8,128)(2,1)}, u32[]{:S(2)}) copy-start(bf16[8,192,2048]{2,1,0:T(8,128)(2,1)} %bitcast_dynamic-update-slice_fusion) | copy-start | bytes 18874372
  434.9 7.7 copy-start.82
  448.0 10.2 %slice-start = ((s8[6291456]{0:T(1024)(128)(4,1)}), s8[4194304]{0:T(1024)(128)(4,1)S(1)}, s32[]{:S(2)}) async-start(s8[6291456]{0:T(1024)(128)(4,1)} %bitcast.218), calls=%async_computation | async-start | bytes 8388608
  448.5 25.9 %collective-permute-start.6 = (bf16[2,2,192,2048]{3,2,1,0:T(8,128)(2,1)S(1)}, bf16[2,2,192,2048]{3,2,1,0:T(8,128)(2,1)S(1)}, u32[]{:S(2)}, u32[]{:S(2)}) collective-permute-start(bf16[2,2,192,2048]{3,2,1,0:T(8,128)(2,1)S(1)} %slice_bitcast_fusion), channel_id=1, source_target_pairs={{0,1},{1,0},{2,3},{3,2},{4,5},{5,4},{6,7},{7,6},{8,9},{9,8},{10,11... | collective-permute-start | bytes 9437192 | tf_op jit(solution)/shard_map/ppermute | solution.py:349
  449.9 8.4 slice-start.1
  479.5 71.0 %collective-permute-start.7 = (bf16[2,96,2048]{2,1,0:T(8,128)(2,1)}, bf16[2,96,2048]{2,1,0:T(8,128)(2,1)}, u32[]{:S(2)}, u32[]{:S(2)}) collective-permute-start(bf16[2,96,2048]{2,1,0:T(8,128)(2,1)} %slice_bitcast_fusion.7), channel_id=1, source_target_pairs={{0,8},{8,0},{16,24},{24,16},{1,9},{9,1},{17,25},{25,17},{2,10},{10... | collective-permute-start | bytes 2359304 | tf_op jit(solution)/shard_map/ppermute | solution.py:349
  480.7 69.8 %collective-permute-start.9 = (bf16[2,96,2048]{2,1,0:T(8,128)(2,1)}, bf16[2,96,2048]{2,1,0:T(8,128)(2,1)}, u32[]{:S(2)}, u32[]{:S(2)}) collective-permute-start(bf16[2,96,2048]{2,1,0:T(8,128)(2,1)} %slice_bitcast_fusion.5), channel_id=1, source_target_pairs={{0,2},{1,3},{2,0},{3,1},{4,6},{5,7},{6,4},{7,5},{8,10},{9,11},{10,... | collective-permute-start | bytes 2359304 | tf_op jit(solution)/shard_map/ppermute | solution.py:349
  498.1 51.5 %copy-start.36 = (f32[192,2048]{1,0:T(8,128)S(1)}, f32[192,2048]{1,0:T(8,128)}, u32[]{:S(2)}) copy-start(f32[192,2048]{1,0:T(8,128)} %copy-done.35) | copy-start | bytes 4718596
  553.4 11.2 %collective-permute-start.10 = (bf16[96,2048]{1,0:T(8,128)(2,1)S(1)}, bf16[96,2048]{1,0:T(8,128)(2,1)S(1)}, u32[]{:S(2)}, u32[]{:S(2)}) collective-permute-start(bf16[96,2048]{1,0:T(8,128)(2,1)S(1)} %fusion.40), channel_id=1, source_target_pairs={{0,8},{8,0},{16,24},{24,16},{1,9},{9,1},{17,25},{25,17},{2,10},{10... | collective-permute-start | bytes 1179656 | tf_op jit(solution)/shard_map/ppermute | solution.py:349
  554.3 11.1 %copy-start.2 = (f32[192,2048]{1,0:T(8,128)S(1)}, f32[192,2048]{1,0:T(8,128)}, u32[]{:S(2)}) copy-start(f32[192,2048]{1,0:T(8,128)} %copy-done.1) | copy-start | bytes 4718596
  554.3 11.1 %copy-start.37 = (f32[192,2048]{1,0:T(8,128)S(1)}, f32[192,2048]{1,0:T(8,128)}, u32[]{:S(2)}) copy-start(f32[192,2048]{1,0:T(8,128)} %copy-done.35) | copy-start | bytes 4718596
  554.4 10.9 %collective-permute-start.8 = (bf16[96,2048]{1,0:T(8,128)(2,1)S(1)}, bf16[96,2048]{1,0:T(8,128)(2,1)S(1)}, u32[]{:S(2)}, u32[]{:S(2)}) collective-permute-start(bf16[96,2048]{1,0:T(8,128)(2,1)S(1)} %fusion.39), channel_id=1, source_target_pairs={{0,2},{1,3},{2,0},{3,1},{4,6},{5,7},{6,4},{7,5},{8,10},{9,11},{10,... | collective-permute-start | bytes 1179656 | tf_op jit(solution)/shard_map/ppermute | solution.py:349
  568.4 80.2 %copy-start.80 = (f32[1536,512]{1,0:T(8,128)S(1)}, f32[1536,512]{1,0:T(8,128)}, u32[]{:S(2)}) copy-start(f32[1536,512]{1,0:T(8,128)} %get-tuple-element.39) | copy-start | bytes 9437188
  648.5 7.9 copy-start.23
  648.6 7.8 copy-start.33
  648.6 7.8 copy-start.78
  719.8 63.7 %copy-start.41 = (f32[192,1536]{1,0:T(8,128)S(1)}, f32[192,1536]{1,0:T(8,128)}, u32[]{:S(2)}) copy-start(f32[192,1536]{1,0:T(8,128)} %copy-done.40) | copy-start | bytes 3538948
  719.8 63.7 %copy-start.64 = (f32[1024]{0:T(1024)S(1)}, f32[1024]{0:T(1024)}, u32[]{:S(2)}) copy-start(f32[1024]{0:T(1024)} %copy-done.63) | copy-start | bytes 12292
  719.8 63.7 %copy-start.68 = (f32[192]{0:T(256)S(1)}, f32[192]{0:T(256)}, u32[]{:S(2)}) copy-start(f32[192]{0:T(256)} %copy-done.67) | copy-start | bytes 2308
  785.0 23.5 %collective-permute-start.19 = (bf16[192,512]{1,0:T(8,128)(2,1)S(1)}, bf16[192,512]{1,0:T(8,128)(2,1)S(1)}, u32[]{:S(2)}, u32[]{:S(2)}) collective-permute-start(bf16[192,512]{1,0:T(8,128)(2,1)S(1)} %slice.334), channel_id=1, source_target_pairs={{0,4},{1,5},{2,6},{3,7},{4,0},{5,1},{6,2},{7,3},{8,12},{9,13},{10,... | collective-permute-start | bytes 589832 | tf_op jit(solution)/shard_map/ppermute | solution.py:349
  827.5 9.9 %copy-start.7 = (bf16[512,2048]{1,0:T(8,128)(2,1)S(1)}, bf16[512,2048]{1,0:T(8,128)(2,1)}, u32[]{:S(2)}) copy-start(bf16[512,2048]{1,0:T(8,128)(2,1)} %convolution_convert_fusion.7) | copy-start | bytes 6291460
  827.5 9.9 %copy-start.15 = (bf16[1024,512]{1,0:T(8,128)(2,1)S(1)}, bf16[1024,512]{1,0:T(8,128)(2,1)}, u32[]{:S(2)}) copy-start(bf16[1024,512]{1,0:T(8,128)(2,1)} %fusion.23) | copy-start | bytes 3145732
  909.6 8.4 copy-start.3
  909.6 8.4 copy-start.38
  909.6 8.4 copy-start.72
  918.0 7.5 copy-start.20
  (43 other events, 112.5 us)

commit v2 on v0

--- a/solution.py
+++ b/solution.py
@@ -3,6 +3,8 @@
 import jax
 import jax.numpy as jnp
 from jax import lax
+from jax.experimental import pallas as pl
+from jax.experimental.pallas import tpu as pltpu
 from jax.sharding import PartitionSpec as P
 
 HEADS = 16
@@ -337,9 +339,1307 @@
     )
 
 
+bf16 = jnp.bfloat16
+f32 = jnp.float32
+ANY = pl.BlockSpec(memory_space=pl.ANY)
+VMEM = pl.BlockSpec(memory_space=pltpu.VMEM)
+PLANE = [j // 4 * 8 + j % 4 for j in range(1, 8)]
+LINKS = [16, 8, 4, 2, 1]
+
+
+def flip(number, bits):
+    bit = 1
+    while bit <= bits:
+        if bits & bit:
+            number = number + bit - 2 * bit * ((number // bit) % 2)
+        bit *= 2
+    return number
+
+
+def coordinates():
+    dp = lax.axis_index("dp")
+    seq = lax.axis_index("seq")
+    return dp // 2, dp % 2, seq // 4, (seq // 2) % 2, seq % 2
+
+
+def partner(mask):
+    return flip(lax.axis_index("dp"), mask // 8), flip(lax.axis_index("seq"), mask % 8)
+
+
+def greet(masks):
+    barrier = pltpu.get_barrier_semaphore()
+    for mask in masks:
+        pl.semaphore_signal(barrier, inc=1, device_id=partner(mask), device_id_type=pl.DeviceIdType.MESH)
+    pl.semaphore_wait(barrier, len(masks))
+
+
+class Wire:
+    def __init__(self, send_sem, recv_sem, local_sem):
+        self.send_sem, self.recv_sem, self.local_sem = send_sem, recv_sem, local_sem
+        self.copies = []
+        self.locals = 0
+
+    def send(self, src, dst, mask):
+        k = len(self.copies)
+        copy = pltpu.make_async_remote_copy(
+            src_ref=src,
+            dst_ref=dst,
+            send_sem=self.send_sem.at[k],
+            recv_sem=self.recv_sem.at[k],
+            device_id=partner(mask),
+            device_id_type=pl.DeviceIdType.MESH,
+        )
+        copy.start()
+        self.copies.append(copy)
+        return copy
+
+    def local(self, src, dst):
+        copy = pltpu.make_async_copy(src, dst, self.local_sem.at[self.locals])
+        self.locals += 1
+        copy.start()
+        return copy
+
+    def close(self):
+        for copy in self.copies:
+            copy.wait_send()
+
+
+def wires(remote, local):
+    return [pltpu.SemaphoreType.DMA((remote,)), pltpu.SemaphoreType.DMA((remote,)), pltpu.SemaphoreType.DMA((local,))]
+
+
+def arrived(copies):
+    for copy in copies:
+        copy.wait_recv()
+
+
+def landed(copies):
+    for copy in copies:
+        copy.wait()
+
+
+def moving(kernel, number, outs, operands, scratch, in_specs=None, out_specs=None, limit=56):
+    return pl.pallas_call(
+        kernel,
+        out_shape=outs,
+        in_specs=in_specs or [ANY] * len(operands),
+        out_specs=out_specs or [ANY] * len(outs),
+        scratch_shapes=scratch,
+        compiler_params=pltpu.CompilerParams(
+            collective_id=number, has_side_effects=True, vmem_limit_bytes=limit * 1024 * 1024
+        ),
+        cost_estimate=pl.CostEstimate(flops=0, bytes_accessed=100_000_000, transcendentals=0),
+        name=kernel.__name__,
+    )(*operands)
+
+
+def shaped(shape, dtype=bf16):
+    return jax.ShapeDtypeStruct(tuple(shape), dtype)
+
+
+def each_rows(rows, body, step=16):
+    @pl.loop(0, rows // step)
+    def _(i):
+        body(pl.ds(pl.multiple_of(i * step, step), step))
+
+
+def wide(ref, where):
+    return ref[where].astype(f32)
+
+
+def plane_gather(wire, block, out, own):
+    half = block.shape[0] // 2
+    top, low = pl.ds(0, half), pl.ds(half, half)
+    from_x = wire.send(block, out.at[1, 0, 0], 8)
+    from_l = wire.send(block, out.at[0, 1, 0], 2)
+    cores = [wire.send(block, out.at[0, 0, 1], 1)]
+    mine = wire.local(block, own) if own is not None else None
+
+    def second():
+        from_x.wait_recv()
+        diagonal = [wire.send(out.at[1, 0, 0, top], out.at[1, 1, 0, top], 2)]
+        from_l.wait_recv()
+        diagonal += [wire.send(out.at[0, 1, 0, low], out.at[1, 1, 0, low], 8)]
+        cores.append(wire.send(out.at[1, 0, 0], out.at[1, 0, 1], 1))
+        cores.append(wire.send(out.at[0, 1, 0], out.at[0, 1, 1], 1))
+
+        def finish():
+            diagonal[0].wait_recv()
+            cores.append(wire.send(out.at[1, 1, 0, top], out.at[1, 1, 1, top], 1))
+            diagonal[1].wait_recv()
+            cores.append(wire.send(out.at[1, 1, 0, low], out.at[1, 1, 1, low], 1))
+            if mine is not None:
+                mine.wait()
+            arrived(cores)
+
+        return finish
+
+    return second
+
+
+def plane_reduce(wire, parts, out, kept, from_c, send_one, recv_one, send_two, recv_two):
+    half = kept.shape[2] // 2
+    order = [(1, 1), (1, 0), (0, 1), (0, 0)]
+    cores = {k: wire.send(parts.at[k[0], k[1], 1], from_c.at[k[0], k[1]], 1) for k in order}
+    loads = {k: wire.local(parts.at[k[0], k[1], 0], kept.at[k[0], k[1]]) for k in order}
+
+    def pair(k, r):
+        return wide(kept.at[k[0], k[1]], r) + wide(from_c.at[k[0], k[1]], r)
+
+    def below(r):
+        return pl.ds(half + r.start, r.size)
+
+    state = {}
+
+    def first():
+        for k in order[:3]:
+            loads[k].wait()
+            cores[k].wait_recv()
+            if k[0]:
+
+                def fill(r, k=k):
+                    send_one[0, k[1], r] = pair(k, r).astype(bf16)
+
+                each_rows(half, fill)
+                state["x", k[1]] = wire.send(send_one.at[0, k[1]], recv_one.at[0, k[1]], 8)
+            if k[1]:
+
+                def fill(r, k=k):
+                    send_one[1, k[0], r] = pair(k, below(r)).astype(bf16)
+
+                each_rows(half, fill)
+                state["l", k[0]] = wire.send(send_one.at[1, k[0]], recv_one.at[1, k[0]], 2)
+        loads[0, 0].wait()
+        cores[0, 0].wait_recv()
+
+    def middle():
+        state["x", 1].wait_recv()
+
+        def fill(r):
+            send_two[0, r] = (pair((0, 1), r) + wide(recv_one.at[0, 1], r)).astype(bf16)
+
+        each_rows(half, fill)
+        state["l2"] = wire.send(send_two.at[0], recv_two.at[0], 2)
+        state["l", 1].wait_recv()
+
+        def fill(r):
+            send_two[1, r] = (pair((1, 0), below(r)) + wide(recv_one.at[1, 1], r)).astype(bf16)
+
+        each_rows(half, fill)
+        state["x2"] = wire.send(send_two.at[1], recv_two.at[1], 8)
+
+    def finish():
+        state["x", 0].wait_recv()
+        state["l2"].wait_recv()
+
+        def fill(r):
+            out[r] = pair((0, 0), r) + wide(recv_one.at[0, 0], r) + wide(recv_two.at[0], r)
+
+        each_rows(half, fill)
+        state["l", 0].wait_recv()
+        state["x2"].wait_recv()
+
+        def fill(r):
+            out[below(r)] = pair((0, 0), below(r)) + wide(recv_one.at[1, 0], r) + wide(recv_two.at[1], r)
+
+        each_rows(half, fill)
+
+    return first, middle, finish
+
+
+def reduce_scratch(rows, width):
+    half = rows // 2
+    return [
+        pltpu.VMEM((2, 2, rows, width), bf16),
+        pltpu.VMEM((2, 2, rows, width), bf16),
+        pltpu.VMEM((2, 2, half, width), bf16),
+        pltpu.VMEM((2, 2, half, width), bf16),
+        pltpu.VMEM((2, half, width), bf16),
+        pltpu.VMEM((2, half, width), bf16),
+    ]
+
+
+def over_y(wire, own, far, place):
+    y, x, h, l, c = coordinates()
+    mine = [wire.local(own, place(y, h)), wire.local(far, place(y, 1 - h))]
+    sent = [wire.send(own, place(y, h), 16), wire.send(far, place(y, 1 - h), 16)]
+
+    def finish():
+        landed(mine)
+        arrived(sent)
+
+    return finish
+
+
+def head_kernel(
+    q_down, key, value, gains, q_up, gate, up, out_proj, w_down, places,
+    first_out, upq_out, gu_out, wo_out, wo_far, wd_out, gains_out, places_out,
+    first, upq, gu, staged, send_sem, recv_sem, local_sem,
+):
+    y, x, h, l, c = coordinates()
+    rank = x * 4 + l * 2 + c
+    wire = Wire(send_sem, recv_sem, local_sem)
+    greet([16, 4] + PLANE)
+    r1, r2 = q_down.shape[1], q_down.shape[1] + key.shape[1]
+    first[:, :r1] = q_down[...].astype(bf16)
+    first[:, r1:r2] = key[...].astype(bf16)
+    first[:, r2:] = value[...].astype(bf16)
+    width = first.shape[1]
+    third = width // 3
+    a, b, d = (pl.ds(i * third, third) for i in range(3))
+    mine = [wire.local(first, first_out.at[y, x, h, l, c]), wire.local(gains, gains_out.at[y, x, h, l, c])]
+    one = [wire.send(first.at[:, p], first_out.at[y, x, h, l, c, :, p], 4) for p in (a, b, d)]
+    gain = wire.send(gains, gains_out.at[y, x, h, l, c], 4)
+    place = [wire.send(places, places_out.at[j], PLANE[j - 1]) for j in range(1, 8)]
+    place_mine = wire.local(places, places_out.at[0])
+    heads = q_up.shape[1] // HEAD_DIM
+    for head in range(heads):
+        hy, hx, hh, hl = head // 8, head // 4 % 2, head // 2 % 2, head % 2
+        target = hx * 4 + hl * 2 + hh
+        upq[target, :, hy * HEAD_DIM : (hy + 1) * HEAD_DIM] = q_up[:, head * HEAD_DIM : (head + 1) * HEAD_DIM].astype(bf16)
+    up_rows = upq.shape[1]
+    up_place = lambda: upq_out.at[y, x, h, pl.ds((l * 2 + c) * up_rows, up_rows), :]
+    up_mine = wire.local(upq.at[rank], up_place())
+    up_sent = [wire.send(upq.at[flip(rank, j)], up_place(), PLANE[j - 1]) for j in range(1, 8)]
+    wo_out[...] = out_proj[...].astype(bf16)
+    wo_sent = wire.send(wo_out, wo_far, 4)
+    piece = gate.shape[1] // 32
+    size = 4 * piece
+    main = size // 128 * 128
+    for target in range(8):
+        for where, weight in ((0, gate), (1, up)):
+            for q in range(4):
+                n = q // 2 * 16 + target // 4 * 8 + q % 2 * 4 + target % 4
+                staged[where, :, q * piece : (q + 1) * piece] = weight[:, n * piece : (n + 1) * piece]
+        gu[target, :, :main] = staged[0, :, :main].astype(bf16)
+        rest = size - main
+        both = jnp.concatenate([staged[0, :, main : main + rest], staged[1, :, main : main + rest]], axis=1)
+        gu[target, :, main : main + 2 * rest] = both.astype(bf16)
+        gu[target, :, main + 2 * rest :] = staged[1, :, :main].astype(bf16)
+    gu_rows = gu.shape[1]
+    gu_place = lambda: gu_out.at[x, pl.ds((l * 2 + c) * gu_rows, gu_rows), :]
+    gu_mine = wire.local(gu.at[rank], gu_place())
+    gu_sent = [wire.send(gu.at[flip(rank, j)], gu_place(), PLANE[j - 1]) for j in range(1, 8)]
+    wd_out[...] = w_down[...].astype(bf16)
+    landed(mine)
+
+    every = slice(None)
+
+    def step(held, columns, mask):
+        at = tuple(every if k in held else v for k, v in zip("yxhlc", (y, x, h, l, c)))
+        if columns is None:
+            return wire.send(gains_out.at[at], gains_out.at[at], mask)
+        place = first_out.at[at + (every, columns)]
+        return wire.send(place, place, mask)
+
+    one[0].wait_recv()
+    two_a = step("h", a, 2)
+    one[1].wait_recv()
+    two_b = step("h", b, 8)
+    one[2].wait_recv()
+    two_d = step("h", d, 16)
+    gain.wait_recv()
+    gain = step("h", None, 2)
+    up_mine.wait()
+    arrived(up_sent)
+    up_h = wire.send(upq_out.at[y, :, h], upq_out.at[y, :, h], 4)
+    two_a.wait_recv()
+    three_a = step("hl", a, 8)
+    two_b.wait_recv()
+    three_b = step("hx", b, 16)
+    two_d.wait_recv()
+    three_d = step("hy", d, 2)
+    gain.wait_recv()
+    gain = step("hl", None, 8)
+    up_y = [wire.send(upq_out.at[y, :, h], upq_out.at[y, :, h], 16)]
+    three_a.wait_recv()
+    four_a = step("hlx", a, 16)
+    three_b.wait_recv()
+    four_b = step("hxy", b, 2)
+    three_d.wait_recv()
+    four_d = step("hyl", d, 8)
+    five = [step("hlx", a, 1), step("hxy", b, 1), step("hyl", d, 1)]
+    gain.wait_recv()
+    gain = step("hlx", None, 16)
+    up_h.wait_recv()
+    up_y += [wire.send(upq_out.at[y, :, 1 - h], upq_out.at[y, :, 1 - h], 16)]
+
+    def last(held, bit, columns):
+        at = {k: every if k in held else v for k, v in zip("yxhlc", (y, x, h, l, c))}
+        at[bit] = 1 - dict(zip("yxhlc", (y, x, h, l, c)))[bit]
+        place = first_out.at[tuple(at[k] for k in "yxhlc") + (every, columns)]
+        return wire.send(place, place, 1)
+
+    four_a.wait_recv()
+    five += [last("hlx", "y", a)]
+    four_b.wait_recv()
+    five += [last("hxy", "l", b)]
+    gain.wait_recv()
+    five += [step("hlxy", None, 1)]
+    four_d.wait_recv()
+    five += [last("hyl", "x", d)]
+    gu_mine.wait()
+    place_mine.wait()
+    arrived(five + up_y + gu_sent + place + [wo_sent])
+    wire.close()
+
+
+def head(q_down, key, value, gains, q_up, gate, up, out_proj, w_down, places):
+    rows = q_down.shape[0]
+    width = q_down.shape[1] + 2 * key.shape[1]
+    columns = gate.shape[1] // 4
+    slice_size = gate.shape[1] // 8
+    outs = [
+        shaped((2, 2, 2, 2, 2, rows, width)),
+        shaped((2, 2, 2, 4 * q_up.shape[0], 2 * HEAD_DIM)),
+        shaped((2, 4 * rows, columns)),
+        shaped(out_proj.shape),
+        shaped(out_proj.shape),
+        shaped(w_down.shape),
+        shaped((2, 2, 2, 2, 2) + gains.shape, f32),
+        shaped((8,) + places.shape, jnp.int32),
+    ]
+    scratch = [
+        pltpu.VMEM((rows, width), bf16),
+        pltpu.VMEM((8, q_up.shape[0], 2 * HEAD_DIM), bf16),
+        pltpu.VMEM((8, rows, columns), bf16),
+        pltpu.VMEM((2, rows, slice_size), f32),
+    ]
+    operands = (q_down, key, value, gains, q_up, gate, up, out_proj, w_down, places)
+    return moving(
+        head_kernel, 1, outs, operands, scratch + wires(60, 8),
+        in_specs=[VMEM] * len(operands),
+        out_specs=[ANY, ANY, ANY, VMEM, ANY, VMEM, ANY, ANY],
+    )
+
+
+def turned(values, cosine, sine, sign):
+    half = HEAD_DIM // 2
+    out = []
+    for start in range(0, values.shape[1], HEAD_DIM):
+        one, two = values[:, start : start + half], values[:, start + half : start + HEAD_DIM]
+        out += [one * cosine - sign * two * sine, sign * one * sine + two * cosine]
+    return jnp.concatenate(out, axis=1)
+
+
+def row_scale(values):
+    return lax.rsqrt(jnp.mean(values * values, axis=-1, keepdims=True) + epsilon)
+
+
+def pack_kernel(
+    tokens, gain_in, gain_q, first_weight, cosine, sine, wo_own, wo_far, gu_set,
+    out, weight_out, gu_far, normed, compressed,
+    weight, block, weight_all, send_sem, recv_sem, local_sem,
+):
+    y, x, h, l, c = coordinates()
+    wire = Wire(send_sem, recv_sem, local_sem)
+    load = wire.local(first_weight, weight)
+    greet(LINKS)
+    weight_done = over_y(wire, wo_own, wo_far, lambda yy, hh: weight_all.at[yy, hh])
+    gu_sent = wire.send(gu_set, gu_far, 4)
+    inputs = tokens[...].astype(f32)
+    normed[...] = (inputs * row_scale(inputs) * gain_in[...]).astype(bf16)
+    load.wait()
+    mixed = jnp.dot(normed[...], weight[...], preferred_element_type=f32)
+    rank_dim = compressed.shape[1]
+    query = mixed[:, :rank_dim]
+    compressed[...] = query
+    block[:, :rank_dim] = (query * row_scale(query) * gain_q[...]).astype(bf16)
+    block[:, rank_dim : rank_dim + HEAD_DIM] = turned(
+        mixed[:, rank_dim : rank_dim + HEAD_DIM], cosine[...], sine[...], 1.0
+    ).astype(bf16)
+    block[:, rank_dim + HEAD_DIM :] = mixed[:, rank_dim + HEAD_DIM :].astype(bf16)
+    near = block.shape[1]
+    far = 2 * HEAD_DIM
+    columns, far_columns = pl.ds(0, near), pl.ds(near, far)
+    from_h = wire.send(block.at[:, pl.ds(near - far, far)], out.at[0, 0, 0, :, far_columns], 4)
+    near_out = out.at[:, :, :, :, columns]
+    second = plane_gather(wire, block, near_out, near_out.at[0, 0, 0])
+    from_h.wait_recv()
+    far_out = out.at[:, :, :, :, far_columns]
+    second_far = plane_gather(wire, far_out.at[0, 0, 0], far_out, None)
+    finish = second()
+    finish_far = second_far()
+    weight_done()
+    swapped = wire.send(weight_all.at[:, 1 - c], weight_out.at[:, c], 1)
+    kept = wire.local(weight_all.at[:, c], weight_out.at[:, c])
+    finish()
+    finish_far()
+    kept.wait()
+    arrived([swapped, gu_sent])
+    wire.close()
+
+
+def pack(tokens, gain_in, gain_q, first_weight, cosine, sine, wo_own, wo_far, gu_set):
+    rows, width = tokens.shape
+    near = first_weight.shape[1]
+    rank_dim = near - 2 * HEAD_DIM
+    outs = [
+        shaped((2, 2, 2, rows, near + 2 * HEAD_DIM)),
+        shaped((2, 2) + wo_own.shape),
+        shaped(gu_set.shape),
+        shaped((rows, width)),
+        shaped((rows, rank_dim), f32),
+    ]
+    operands = (tokens, gain_in, gain_q, first_weight, cosine, sine, wo_own, wo_far, gu_set)
+    return moving(
+        pack_kernel, 2, outs, operands,
+        [pltpu.VMEM(first_weight.shape, bf16), pltpu.VMEM((rows, near), bf16), pltpu.VMEM((2, 2) + wo_own.shape, bf16)]
+        + wires(32, 8),
+        in_specs=[VMEM, VMEM, VMEM, ANY, VMEM, VMEM, VMEM, VMEM, ANY],
+        out_specs=[ANY, VMEM, ANY, VMEM, VMEM],
+    )
+
+
+def scores_of(keys, queries, index, first, last):
+    scores = lax.dot_general(keys, queries, (((1,), (1,)), ((), ())), preferred_element_type=f32)
+    seen = (index >= first) & (index <= last)
+    return scores * (1.0 / math.sqrt(HEAD_DIM)), seen
+
+
+def attend_kernel(
+    plane_set, wq, wo, cosine, sine, key_index, query_index, first_index, cotangent, gu_own, gu_far, gu_next,
+    queries_out, attended, lse, parts, cotangents, gu_out, gu_far_next,
+    kv, normed, staged, load_sem, send_sem, recv_sem, local_sem,
+):
+    wire = Wire(send_sem, recv_sem, local_sem)
+    rank_dim = wq.shape[0]
+    loads = [
+        pltpu.make_async_copy(plane_set.at[:, :, :, :, pl.ds(rank_dim, 4 * HEAD_DIM)], kv, load_sem.at[0]),
+        pltpu.make_async_copy(plane_set.at[:, :, :, :, pl.ds(0, rank_dim)], normed, load_sem.at[1]),
+    ]
+    for load in loads:
+        load.start()
+    greet(LINKS)
+    second = plane_gather(wire, cotangent, cotangents, cotangents.at[0, 0, 0])
+    gu_done = over_y(wire, gu_own, gu_far, lambda yy, hh: gu_out.at[yy, hh])
+    gu_sent = wire.send(gu_next, gu_far_next, 4)
+    landed(loads)
+    rows = kv.shape[3]
+    block = 2 * rows
+
+    def one(g, i):
+        start = pl.multiple_of((g * 2 + i) * block, block)
+        place = pl.ds(start, block)
+        raw = jnp.dot(normed[g, i].reshape(block, rank_dim), wq[...], preferred_element_type=f32)
+        queries = turned(raw, cosine[place], sine[place], 1.0).astype(bf16)
+        queries_out[place] = queries
+        keys = jnp.concatenate(
+            [kv[g, :, :, :, :HEAD_DIM].reshape(2 * block, HEAD_DIM), kv[g, :, :, :, 2 * HEAD_DIM : 3 * HEAD_DIM].reshape(2 * block, HEAD_DIM)]
+        )
+        values = jnp.concatenate(
+            [kv[g, :, :, :, HEAD_DIM : 2 * HEAD_DIM].reshape(2 * block, HEAD_DIM), kv[g, :, :, :, 3 * HEAD_DIM :].reshape(2 * block, HEAD_DIM)]
+        )
+        merged = []
+        for a in range(2):
+            scores, seen = scores_of(
+                keys, queries[:, a * HEAD_DIM : (a + 1) * HEAD_DIM], key_index[...], first_index[:, place], query_index[:, place]
+            )
+            scores = jnp.where(seen, scores, masked_score)
+            top = jnp.max(scores, axis=0, keepdims=True)
+            weights = jnp.exp(scores - top)
+            total = jnp.sum(weights, axis=0, keepdims=True)
+            lse[a, :, place] = top + jnp.log(total)
+            probs = (weights * (1.0 / total)).astype(bf16)
+            merged.append(lax.dot_general(probs, values, (((0,), (0,)), ((), ())), preferred_element_type=f32).astype(bf16))
+        merged = jnp.concatenate(merged, axis=1)
+        attended[place] = merged
+        staged[g, i] = jnp.dot(merged, wo[...], preferred_element_type=f32).astype(bf16).reshape(2, rows, -1)
+        pltpu.make_async_copy(staged.at[g, i], parts.at[g, i], load_sem.at[2 + g * 2 + i]).start()
+
+    @pl.loop(0, 2)
+    def _(k):
+        one(0, k)
+
+    finish = second()
+
+    @pl.loop(0, 2)
+    def _(k):
+        one(1, k)
+
+    for k in range(4):
+        pltpu.make_async_copy(staged.at[k // 2, k % 2], parts.at[k // 2, k % 2], load_sem.at[2 + k]).wait()
+    finish()
+    gu_done()
+    gu_sent.wait_recv()
+    wire.close()
+
+
+def attend(plane_set, wq, wo, cosine, sine, key_index, query_index, first_index, cotangent, gu_own, gu_far, gu_next):
+    rows = plane_set.shape[3]
+    tokens = 8 * rows
+    width = wo.shape[1]
+    rank_dim = wq.shape[0]
+    outs = [
+        shaped((tokens, 2 * HEAD_DIM)),
+        shaped((tokens, 2 * HEAD_DIM)),
+        shaped((2, 1, tokens), f32),
+        shaped((2, 2, 2, rows, width)),
+        shaped((2, 2, 2, rows, width)),
+        shaped((2, 2) + gu_own.shape),
+        shaped(gu_next.shape),
+    ]
+    scratch = [
+        pltpu.VMEM((2, 2, 2, rows, 4 * HEAD_DIM), bf16),
+        pltpu.VMEM((2, 2, 2, rows, rank_dim), bf16),
+        pltpu.VMEM((2, 2, 2, rows, width), bf16),
+        pltpu.SemaphoreType.DMA((6,)),
+    ]
+    operands = (plane_set, wq, wo, cosine, sine, key_index, query_index, first_index, cotangent, gu_own, gu_far, gu_next)
+    return moving(
+        attend_kernel, 3, outs, operands, scratch + wires(20, 8),
+        in_specs=[ANY] + [VMEM] * 10 + [ANY],
+        out_specs=[VMEM, VMEM, VMEM, ANY, ANY, ANY, ANY],
+    )
+
+
+def middle_kernel(
+    parts, tokens, gain, gu_own, gu_far, wd_own,
+    middle, plane_mid, gu_out, wd_out,
+    kept, from_c, s1, r1, s2, r2, normed, wd_far, send_sem, recv_sem, local_sem,
+):
+    wire = Wire(send_sem, recv_sem, local_sem)
+    greet(LINKS)
+    first, then, finish = plane_reduce(wire, parts, middle, kept, from_c, s1, r1, s2, r2)
+    wd_sent = wire.send(wd_own, wd_far, 4)
+    gu_done = over_y(wire, gu_own, gu_far, lambda yy, hh: gu_out.at[yy, hh])
+    first()
+    then()
+    finish()
+
+    def norm(r):
+        value = tokens[r].astype(f32) + middle[r]
+        middle[r] = value
+        normed[r] = (value * row_scale(value) * gain[...]).astype(bf16)
+
+    each_rows(normed.shape[0], norm)
+    second = plane_gather(wire, normed, plane_mid, plane_mid.at[0, 0, 0])
+    wd_sent.wait_recv()
+    wd_done = over_y(wire, wd_own, wd_far, lambda yy, hh: wd_out.at[yy, hh])
+    second()()
+    gu_done()
+    wd_done()
+    wire.close()
+
+
+def middle_step(parts, tokens, gain, gu_own, gu_far, wd_own):
+    rows, width = tokens.shape
+    outs = [
+        shaped((rows, width), f32),
+        shaped(parts.shape),
+        shaped((2, 2) + gu_own.shape),
+        shaped((2, 2) + wd_own.shape),
+    ]
+    operands = (parts, tokens, gain, gu_own, gu_far, wd_own)
+    return moving(
+        middle_kernel, 4, outs, operands,
+        reduce_scratch(rows, width) + [pltpu.VMEM((rows, width), bf16), pltpu.VMEM(wd_own.shape, bf16)] + wires(40, 12),
+        in_specs=[ANY, VMEM, VMEM, VMEM, VMEM, VMEM],
+        out_specs=[VMEM, ANY, ANY, ANY],
+    )
+
+
+def feed_kernel(mid, cotangent, gu_one, gu_two, down, hidden, grads, mid_parts, final_parts, gu, wd, sems):
+    main = gu.shape[4] // 2 // 128 * 128
+    units = down.shape[2] * 4
+    padded = wd.shape[0]
+    columns = gu.shape[4]
+
+    @pl.when(pl.program_id(0) == 0)
+    def _():
+        copies = [
+            pltpu.make_async_copy(gu_one, gu.at[:, 0], sems.at[0]),
+            pltpu.make_async_copy(gu_two, gu.at[:, 1], sems.at[1]),
+        ]
+        size = down.shape[2]
+        for k in range(4):
+            copies.append(pltpu.make_async_copy(down.at[k // 2, k % 2], wd.at[pl.ds(k * size, size)], sems.at[2 + k]))
+        for copy in copies:
+            copy.start()
+        wd[units:] = jnp.zeros((padded - units, wd.shape[1]), bf16)
+        landed(copies)
+
+    weight = gu[...].reshape(-1, columns)
+    both = jnp.dot(mid[...], weight, preferred_element_type=f32)
+    gate = both[:, : main + 128]
+    upper = jnp.concatenate([both[:, main + 128 :], pltpu.roll(both[:, main : main + 128], 64, 1)], axis=1)
+    grad = lax.dot_general(cotangent[...], wd[...], (((1,), (1,)), ((), ())), preferred_element_type=f32)
+    sigmoid = 1.0 / (1.0 + jnp.exp(-gate))
+    silu = gate * sigmoid
+    hid = (silu * upper).astype(bf16)
+    hidden[...] = hid[:, :units]
+    final_parts[...] = jnp.dot(hid, wd[...], preferred_element_type=f32).astype(bf16)
+    grad_gate = grad * upper * sigmoid * (1.0 + gate * (1.0 - sigmoid))
+    grad_upper = grad * silu
+    joint = grad_gate[:, main:] + pltpu.roll(grad_upper[:, main:], 64, 1)
+    out = jnp.concatenate([grad_gate[:, :main], joint, grad_upper[:, :main]], axis=1).astype(bf16)
+    grads[...] = out
+    mid_parts[...] = lax.dot_general(out, weight, (((1,), (1,)), ((), ())), preferred_element_type=f32).astype(bf16)
+
+
+def feed(mid, cotangent, gu_one, gu_two, down, block=384):
+    tokens, width = mid.shape
+    columns = gu_one.shape[-1]
+    units = 4 * down.shape[2]
+    padded = (units + 127) // 128 * 128
+    by_block = lambda n: pl.BlockSpec((block, n), lambda i: (i, 0))
+    return pl.pallas_call(
+        feed_kernel,
+        grid=(tokens // block,),
+        in_specs=[by_block(width), by_block(width), ANY, ANY, ANY],
+        out_specs=[by_block(units), by_block(columns), by_block(width), by_block(width)],
+        out_shape=[shaped((tokens, units)), shaped((tokens, columns)), shaped((tokens, width)), shaped((tokens, width))],
+        scratch_shapes=[
+            pltpu.VMEM((2, 2, 2) + gu_one.shape[2:], bf16),
+            pltpu.VMEM((padded, width), bf16),
+            pltpu.SemaphoreType.DMA((6,)),
+        ],
+        compiler_params=pltpu.CompilerParams(vmem_limit_bytes=56 * 1024 * 1024),
+        cost_estimate=pl.CostEstimate(flops=12 * tokens * width * units, bytes_accessed=40_000_000, transcendentals=0),
+        name="feed",
+    )(mid, cotangent, gu_one, gu_two, down)
+
+
+def fold_y(wire, source, mine, recv, passed, kept):
+    y, x, h, l, c = coordinates()
+    sent = [wire.send(source(1 - y, hh), recv.at[hh], 16) for hh in (1 - h, h)]
+    loads = [wire.local(source(y, hh), mine.at[hh]) for hh in (1 - h, h)]
+
+    def finish():
+        for k, hh, target in ((0, 1 - h, passed), (1, h, kept)):
+            loads[k].wait()
+            sent[k].wait_recv()
+
+            def body(r, hh=hh, target=target):
+                target[r] = (wide(mine.at[hh], r) + wide(recv.at[hh], r)).astype(target.dtype)
+
+            each_rows(target.shape[0], body)
+
+    return finish
+
+
+def fold_scratch(rows, width):
+    return [pltpu.VMEM((2, rows, width), bf16), pltpu.VMEM((2, rows, width), bf16)]
+
+
+def fold_h(wire, passed, kept, recv, out):
+    sent = wire.send(passed, recv, 4)
+
+    def finish():
+        sent.wait_recv()
+
+        def body(r):
+            out[r] = (wide(kept, r) + wide(recv, r)).astype(out.dtype)
+
+        each_rows(out.shape[0], body)
+
+    return finish
+
+
+def hand_back(wire, own, out):
+    y, x, h, l, c = coordinates()
+    rank = x * 4 + l * 2 + c
+    mine = wire.local(own(rank), out.at[rank])
+    sent = [wire.send(own(flip(rank, j)), out.at[rank], PLANE[j - 1]) for j in range(1, 8)]
+
+    def finish():
+        mine.wait()
+        arrived(sent)
+
+    return finish
+
+
+def norm_back(value, gain, grad):
+    scale = row_scale(value)
+    weighted = gain * grad
+    inner = scale * weighted - value * scale * scale * scale * jnp.mean(weighted * value, axis=-1, keepdims=True)
+    return inner, grad * value * scale
+
+
+def branch_kernel(
+    parts, middle, cotangent, gain, down_grad, gu_grad,
+    grad_middle, gain_grad, plane_branch, down_out, gu_passed, gu_kept,
+    kept, from_c, s1, r1, s2, r2, normed_grad, branch, wd_mine, wd_recv, wd_passed, wd_kept, wd_far, gu_mine, gu_recv,
+    send_sem, recv_sem, local_sem,
+):
+    wire = Wire(send_sem, recv_sem, local_sem)
+    greet(LINKS)
+    first, then, finish = plane_reduce(wire, parts, normed_grad, kept, from_c, s1, r1, s2, r2)
+    down_y = fold_y(wire, lambda yy, hh: down_grad.at[yy, hh], wd_mine, wd_recv, wd_passed, wd_kept)
+    first()
+    then()
+    gain_grad[...] = jnp.zeros_like(gain_grad)
+    finish()
+
+    def norm(r):
+        inner, outer = norm_back(middle[r], gain[...], normed_grad[r])
+        value = cotangent[r].astype(f32) + inner
+        grad_middle[r] = value
+        branch[r] = value.astype(bf16)
+        gain_grad[...] += jnp.sum(outer, axis=0, keepdims=True)
+
+    each_rows(branch.shape[0], norm)
+    second = plane_gather(wire, branch, plane_branch, plane_branch.at[0, 0, 0])
+    down_y()
+    down_h = fold_h(wire, wd_passed, wd_kept, wd_far, down_out)
+    gu_y = fold_y(wire, lambda yy, hh: gu_grad.at[yy, 0, hh], gu_mine, gu_recv, gu_passed, gu_kept)
+    second()()
+    gu_y()
+    down_h()
+    wire.close()
+
+
+def branch_step(parts, middle, cotangent, gain, down_grad, gu_grad):
+    rows, width = middle.shape
+    down = down_grad.shape[2:]
+    gu = gu_grad.shape[3:]
+    outs = [
+        shaped((rows, width), f32),
+        shaped((1, width), f32),
+        shaped(parts.shape),
+        shaped(down, f32),
+        shaped(gu),
+        shaped(gu),
+    ]
+    scratch = reduce_scratch(rows, width) + [pltpu.VMEM((rows, width), f32), pltpu.VMEM((rows, width), bf16)]
+    scratch += fold_scratch(*down) + [pltpu.VMEM(down, bf16), pltpu.VMEM(down, bf16), pltpu.VMEM(down, bf16)]
+    scratch += fold_scratch(*gu)
+    operands = (parts, middle, cotangent, gain, down_grad, gu_grad)
+    return moving(
+        branch_kernel, 5, outs, operands, scratch + wires(40, 16),
+        in_specs=[ANY, VMEM, VMEM, VMEM, ANY, ANY],
+        out_specs=[VMEM, VMEM, ANY, VMEM, VMEM, VMEM],
+    )
+
+
+def attend_back_kernel(
+    plane_set, plane_branch, queries, attended, lse, wq, wo, cosine, sine, key_index, query_index, first_index,
+    final_parts, middle, gu_passed, gu_kept, gu_grad,
+    query_grad, parts, output, gu_out, gu_passed_next, gu_kept_next,
+    kv, branch, staged, grad_keys, grad_values, kept, from_c, s1, r1, s2, r2, total, gu_recv, gu_mine, gu_recv_y,
+    load_sem, send_sem, recv_sem, local_sem,
+):
+    wire = Wire(send_sem, recv_sem, local_sem)
+    rank_dim = wq.shape[0]
+    rows = kv.shape[3]
+    block = 2 * rows
+    load_kv = pltpu.make_async_copy(plane_set.at[:, :, :, :, pl.ds(rank_dim, 4 * HEAD_DIM)], kv, load_sem.at[0])
+    load_kv.start()
+
+    def load_branch(k):
+        return pltpu.make_async_copy(plane_branch.at[k // 2, k % 2], branch.at[k % 2], load_sem.at[1 + k % 2])
+
+    load_branch(0).start()
+    greet(LINKS)
+    first, then, finish = plane_reduce(wire, final_parts, total, kept, from_c, s1, r1, s2, r2)
+    gu_h = fold_h(wire, gu_passed, gu_kept, gu_recv, gu_out)
+    gu_y = fold_y(wire, lambda yy, hh: gu_grad.at[yy, 1, hh], gu_mine, gu_recv_y, gu_passed_next, gu_kept_next)
+    load_kv.wait()
+    scale = 1.0 / math.sqrt(HEAD_DIM)
+
+    def one(k):
+        g = k // 2
+        i = k % 2
+        load_branch(k).wait()
+
+        @pl.when(k < 3)
+        def _():
+            load_branch(k + 1).start()
+
+        @pl.when(i == 0)
+        def _():
+            grad_keys[...] = jnp.zeros_like(grad_keys)
+            grad_values[...] = jnp.zeros_like(grad_values)
+
+        start = pl.multiple_of(k * block, block)
+        place = pl.ds(start, block)
+        grads = lax.dot_general(
+            branch[i].reshape(block, -1), wo[...], (((1,), (1,)), ((), ())), preferred_element_type=f32
+        ).astype(bf16)
+        keys = jnp.concatenate(
+            [kv[g, :, :, :, :HEAD_DIM].reshape(2 * block, HEAD_DIM), kv[g, :, :, :, 2 * HEAD_DIM : 3 * HEAD_DIM].reshape(2 * block, HEAD_DIM)]
+        )
+        values = jnp.concatenate(
+            [kv[g, :, :, :, HEAD_DIM : 2 * HEAD_DIM].reshape(2 * block, HEAD_DIM), kv[g, :, :, :, 3 * HEAD_DIM :].reshape(2 * block, HEAD_DIM)]
+        )
+        query_parts = []
+        for a in range(2):
+            span = slice(a * HEAD_DIM, (a + 1) * HEAD_DIM)
+            query, grad = queries[place, span], grads[:, span]
+            product = grad.astype(f32) * attended[place, span].astype(f32)
+            delta = lax.dot_general(
+                jnp.ones((8, HEAD_DIM), f32), product, (((1,), (1,)), ((), ())),
+                precision=lax.Precision.HIGHEST, preferred_element_type=f32,
+            )[:1]
+            scores, seen = scores_of(keys, query, key_index[...], first_index[:, place], query_index[:, place])
+            probs = jnp.where(seen, jnp.exp(scores - lse[a, :, place]), 0.0)
+            grad_values[...] += jnp.dot(probs.astype(bf16), grad, preferred_element_type=f32)
+            grad_probs = lax.dot_general(values, grad, (((1,), (1,)), ((), ())), preferred_element_type=f32)
+            grad_scores = (probs * (grad_probs - delta) * scale).astype(bf16)
+            grad_keys[...] += jnp.dot(grad_scores, query, preferred_element_type=f32)
+            query_parts.append(
+                lax.dot_general(grad_scores, keys, (((0,), (0,)), ((), ())), preferred_element_type=f32)
+            )
+        query_sum = turned(jnp.concatenate(query_parts, axis=1), cosine[place], sine[place], -1.0).astype(bf16)
+        query_grad[place] = query_sum
+        normed = lax.dot_general(query_sum, wq[...], (((1,), (1,)), ((), ())), preferred_element_type=f32)
+        staged[g, i, :, :, :rank_dim] = normed.astype(bf16).reshape(2, rows, rank_dim)
+
+        @pl.when(i == 1)
+        def _():
+            for number, (source, side) in enumerate(
+                ((grad_keys, 0), (grad_values, 0), (grad_keys, 1), (grad_values, 1))
+            ):
+                column = rank_dim + number * HEAD_DIM
+                half = source[side * 2 * block : (side + 1) * 2 * block].astype(bf16)
+                staged[g, :, :, :, column : column + HEAD_DIM] = half.reshape(2, 2, rows, HEAD_DIM)
+            pltpu.make_async_copy(staged.at[g], parts.at[g], load_sem.at[3 + g]).start()
+
+    def steps(a, b):
+        @pl.loop(a, b)
+        def _(k):
+            one(k)
+
+    steps(0, 1)
+    first()
+    steps(1, 3)
+    then()
+    gu_h()
+    steps(3, 4)
+    finish()
+
+    def emit(r):
+        output[r] = (middle[r] + total[r]).astype(bf16)
+
+    each_rows(output.shape[0], emit)
+    for g in range(2):
+        pltpu.make_async_copy(staged.at[g], parts.at[g], load_sem.at[3 + g]).wait()
+    gu_y()
+    wire.close()
+
+
+def attend_back(
+    plane_set, plane_branch, queries, attended, lse, wq, wo, cosine, sine, key_index, query_index, first_index,
+    final_parts, middle, gu_passed, gu_kept, gu_grad,
+):
+    rows, width = middle.shape
+    tokens = 8 * rows
+    gu = gu_passed.shape
+    outs = [
+        shaped((tokens, 2 * HEAD_DIM)),
+        shaped((2, 2, 2, rows, wq.shape[0] + 4 * HEAD_DIM)),
+        shaped((rows, width)),
+        shaped(gu),
+        shaped(gu),
+        shaped(gu),
+    ]
+    scratch = [
+        pltpu.VMEM((2, 2, 2, rows, 4 * HEAD_DIM), bf16),
+        pltpu.VMEM((2, 2, rows, width), bf16),
+        pltpu.VMEM((2, 2, 2, rows, wq.shape[0] + 4 * HEAD_DIM), bf16),
+        pltpu.VMEM((8 * rows, HEAD_DIM), f32),
+        pltpu.VMEM((8 * rows, HEAD_DIM), f32),
+    ]
+    scratch += reduce_scratch(rows, width) + [pltpu.VMEM((rows, width), f32), pltpu.VMEM(gu, bf16)]
+    scratch += fold_scratch(*gu) + [pltpu.SemaphoreType.DMA((5,))]
+    operands = (
+        plane_set, plane_branch, queries, attended, lse, wq, wo, cosine, sine, key_index, query_index, first_index,
+        final_parts, middle, gu_passed, gu_kept, gu_grad,
+    )
+    return moving(
+        attend_back_kernel, 6, outs, operands, scratch + wires(30, 12),
+        in_specs=[ANY, ANY] + [VMEM] * 10 + [ANY, VMEM, ANY, VMEM, ANY],
+        out_specs=[VMEM, ANY, VMEM, VMEM, VMEM, VMEM],
+        limit=62,
+    )
+
+
+def tail_kernel(
+    parts, normed, compressed, tokens, grad_middle, first_weight, gain_in, gain_q, gain_mid_grad, cosine, sine,
+    gu_total, gu_passed, gu_kept, up_grad, out_grad,
+    grad_tokens, down_out, key_out, value_out, gains_out, gate_out, up_out, q_up_out, out_out,
+    kept, from_c, s1, r1, s2, r2, back, kv_send, kv_recv, weight, mixed, normed_grad, gain_rows,
+    blocks, acc, recv, core, gains, gains_recv,
+    gu_far, gu_own, gu_back, gu_wide, up_mine, up_recv, up_passed, up_kept, up_far, up_own, up_back,
+    heads, o_mine, o_recv, o_passed, o_kept, o_far,
+    send_sem, recv_sem, local_sem,
+):
+    y, x, h, l, c = coordinates()
+    own = dict(zip("yxhlc", (y, x, h, l, c)))
+    every = slice(None)
+    wire = Wire(send_sem, recv_sem, local_sem)
+    load = wire.local(first_weight, weight)
+    greet([16, 4] + PLANE)
+    first, then, finish = plane_reduce(wire, parts, back, kept, from_c, s1, r1, s2, r2)
+    gu_h = fold_h(wire, gu_passed, gu_kept, gu_far, gu_own)
+    swapped = wire.send(out_grad.at[:, 1 - c], heads.at[:, c], 1)
+    stayed = wire.local(out_grad.at[:, c], heads.at[:, c])
+    first()
+    stayed.wait()
+    swapped.wait_recv()
+    o_y = fold_y(wire, lambda yy, hh: heads.at[yy, hh], o_mine, o_recv, o_passed, o_kept)
+    up_y = [
+        fold_y(wire, lambda yy, hh, k=k: up_grad.at[yy, k, hh], up_mine.at[k], up_recv.at[k], up_passed.at[k], up_kept.at[k])
+        for k in range(2)
+    ]
+    then()
+    finish()
+    rows = back.shape[0]
+    rank_dim = compressed.shape[1]
+    split = rank_dim + 2 * HEAD_DIM
+    kv_send[...] = back[:, split:].astype(bf16)
+    far = wire.send(kv_send, kv_recv, 4)
+    inner, outer = norm_back(compressed[...], gain_q[...], back[:, :rank_dim])
+    mixed[:, :rank_dim] = inner.astype(bf16)
+    gain_rows[1:2, :rank_dim] = jnp.sum(outer, axis=0, keepdims=True)
+    gain_rows[2:3, :] = gain_mid_grad[...]
+    gu_h()
+    piece_rows = gu_back.shape[2]
+    piece = lambda k: pl.ds(pl.multiple_of((k % 4) * piece_rows, piece_rows), piece_rows)
+
+    both = [wire.local(gu_total, gu_wide.at[0]), wire.local(gu_own, gu_wide.at[1])]
+    landed(both)
+    gu_done = hand_back(wire, lambda k: gu_wide.at[k // 4, piece(k)], gu_back.at[0])
+    far.wait_recv()
+    kv = back[:, rank_dim:split] + kv_recv[...].astype(f32)
+    mixed[:, rank_dim : rank_dim + HEAD_DIM] = turned(kv[:, :HEAD_DIM], cosine[...], sine[...], -1.0).astype(bf16)
+    mixed[:, rank_dim + HEAD_DIM :] = kv[:, HEAD_DIM:].astype(bf16)
+    size = normed.shape[1] // 8
+    cores = []
+    for k in range(8):
+        at = (k // 4, k // 2 % 2, k % 2)
+        grad = lax.dot_general(
+            normed[:, k * size : (k + 1) * size], mixed[...], (((0,), (0,)), ((), ())), preferred_element_type=f32
+        )
+        blocks[at] = grad.astype(bf16).reshape(blocks.shape[3:])
+        cores.append(wire.send(blocks.at[at + (every, 1 - c)], core.at[at], 1))
+    o_y()
+    o_h = fold_h(wire, o_passed, o_kept, o_far, out_out)
+    for k in range(2):
+        up_y[k]()
+    up_h = [fold_h(wire, up_passed.at[k], up_kept.at[k], up_far.at[k], up_own.at[k]) for k in range(2)]
+    span = blocks.shape[5]
+    width = blocks.shape[6]
+    third = width // 3
+    columns = [pl.ds(i * third, third) for i in range(3)]
+    orders = ["yxlh", "lyxh", "xlyh"]
+    sent = [None] * 3
+
+    def index(fixed, block):
+        free = [k for k in "yxhl" if k not in fixed]
+        at = dict(fixed)
+        for position, k in enumerate(reversed(free)):
+            at[k] = (block // 2**position) % 2
+        return tuple(at[k] for k in "yxhl")
+
+    def over(fixed, body):
+        count = 2 ** (4 - len(fixed))
+
+        @pl.loop(0, count * (span // 16))
+        def _(i):
+            r = pl.ds(pl.multiple_of((i % (span // 16)) * 16, 16), 16)
+            body(index(fixed, i // (span // 16)), r)
+
+    def pass_on(p, step):
+        order = orders[p]
+        fixed = {k: own[k] for k in order[:step]}
+        bit = order[step]
+        src = {**fixed, bit: 1 - own[bit]}
+        dst = {**fixed, bit: own[bit]}
+        place = lambda at: tuple(at.get(k, every) for k in "yxhl") + (every, columns[p])
+        mask = {"y": 16, "x": 8, "h": 4, "l": 2}[bit]
+        sent[p] = wire.send(acc.at[place(src)], recv.at[place(dst)], mask)
+
+    arrived(cores)
+    for first_side in (True, False):
+        for p in range(3):
+            bit = orders[p][0]
+
+            def body(at, r, p=p):
+                value = wide(blocks, at + (c, r, columns[p])) + wide(core, at + (r, columns[p]))
+                acc[at + (r, columns[p])] = value.astype(bf16)
+
+            over({bit: 1 - own[bit] if first_side else own[bit]}, body)
+            if first_side:
+                pass_on(p, 0)
+    load.wait()
+    normed_grad[...] = lax.dot_general(mixed[...], weight[...], (((1,), (1,)), ((), ())), preferred_element_type=f32)
+    gain_rows[0:1, :] = jnp.zeros((1, gain_rows.shape[1]), f32)
+
+    def norm(r):
+        inner, outer = norm_back(tokens[r].astype(f32), gain_in[...], normed_grad[r])
+        grad_tokens[r] = (grad_middle[r] + inner).astype(bf16)
+        gain_rows[0:1, :] += jnp.sum(outer, axis=0, keepdims=True)
+
+    each_rows(rows, norm)
+    q_span = rank_dim // 32
+    gains[...] = jnp.zeros_like(gains)
+    for n in range(32):
+        at = (n // 16, n // 8 % 2, n // 4 % 2, n // 2 % 2, n % 2, 0)
+        gains[at + (slice(0, 128),)] = jnp.concatenate(
+            [gain_rows[0, n * span : (n + 1) * span], gain_rows[2, n * span : (n + 1) * span]], axis=0
+        )
+        gains[at + (slice(128, 128 + q_span),)] = gain_rows[1, n * q_span : (n + 1) * q_span]
+
+    def pass_gains(order, step):
+        fixed = {k: own[k] for k in order[:step]}
+        bit = order[step]
+        place = lambda at: tuple(at.get(k, every) for k in "yxhlc")
+        mask = {"y": 16, "x": 8, "h": 4, "l": 2, "c": 1}[bit]
+        return wire.send(gains.at[place({**fixed, bit: 1 - own[bit]})], gains_recv.at[place({**fixed, bit: own[bit]})], mask)
+
+    def add_gains(order, step):
+        fixed = {k: own[k] for k in order[:step]}
+        bit = order[step]
+        place = lambda at: tuple(at.get(k, every) for k in "yxhlc")
+        mine = place({**fixed, bit: own[bit]})
+        gains[mine] = gains[mine] + gains_recv[place({**fixed, bit: 1 - own[bit]})]
+
+    gain_order = "cyxlh"
+    gain_sent = pass_gains(gain_order, 0)
+    gain_step = 0
+    for step in range(4):
+        for p in range(3):
+            order = orders[p]
+            fixed = {k: own[k] for k in order[:step]}
+            bit = order[step]
+            sent[p].wait_recv()
+
+            def body(at, r, p=p, bit=bit, last=step == 3):
+                other = tuple(1 - own[k] if k == bit else v for k, v in zip("yxhl", at))
+                value = wide(acc, at + (r, columns[p])) + wide(recv, other + (r, columns[p]))
+                if last:
+                    back[r, columns[p]] = value
+                else:
+                    acc[at + (r, columns[p])] = value.astype(bf16)
+
+            if step < 3:
+                over({**fixed, bit: own[bit], order[step + 1]: 1 - own[order[step + 1]]}, body)
+                pass_on(p, step + 1)
+                over({**fixed, bit: own[bit], order[step + 1]: own[order[step + 1]]}, body)
+            else:
+                over({**fixed, bit: own[bit]}, body)
+        if gain_step < 5:
+            gain_sent.wait_recv()
+            add_gains(gain_order, gain_step)
+            gain_step += 1
+            if gain_step < 5:
+                gain_sent = pass_gains(gain_order, gain_step)
+        if step == 0:
+            for k in range(2):
+                up_h[k]()
+            up_rows = up_back.shape[1]
+            up_piece = lambda k: up_own.at[k // 4, pl.ds(pl.multiple_of((k % 4) * up_rows, up_rows), up_rows)]
+            up_done = hand_back(wire, up_piece, up_back)
+            gu_done()
+            unit = gate_out.shape[1] // 32
+            units = 4 * unit
+            main = units // 128 * 128
+            rest = units - main
+            for source in range(8):
+                tile = gu_back[0, source].astype(f32)
+                halves = (
+                    tile[:, : main + rest],
+                    jnp.concatenate([tile[:, main + 2 * rest :], tile[:, main + rest : main + 2 * rest]], axis=1),
+                )
+                for half, target in zip(halves, (gate_out, up_out)):
+                    for q in range(4):
+                        n = q // 2 * 16 + source // 4 * 8 + q % 2 * 4 + source % 4
+                        target[:, n * unit : (n + 1) * unit] = half[:, q * unit : (q + 1) * unit]
+        if step == 1:
+            o_h()
+            up_done()
+            for head in range(q_up_out.shape[1] // HEAD_DIM):
+                hy, hx, hh, hl = head // 8, head // 4 % 2, head // 2 % 2, head % 2
+                source = hx * 4 + hl * 2 + hh
+                q_up_out[:, head * HEAD_DIM : (head + 1) * HEAD_DIM] = up_back[
+                    source, :, hy * HEAD_DIM : (hy + 1) * HEAD_DIM
+                ].astype(f32)
+    while gain_step < 5:
+        gain_sent.wait_recv()
+        add_gains(gain_order, gain_step)
+        gain_step += 1
+        if gain_step < 5:
+            gain_sent = pass_gains(gain_order, gain_step)
+    gains_out[...] = gains[y, x, h, l, c]
+    down_out[...] = back[:span, :rank_dim]
+    key_out[...] = back[:span, rank_dim : rank_dim + HEAD_DIM]
+    value_out[...] = back[:span, rank_dim + HEAD_DIM : split]
+    wire.close()
+
+
+def tail(
+    parts, normed, compressed, tokens, grad_middle, first_weight, gain_in, gain_q, gain_mid_grad, cosine, sine,
+    gu_total, gu_passed, gu_kept, up_grad, out_grad,
+):
+    rows, width = tokens.shape
+    rank_dim = compressed.shape[1]
+    near = first_weight.shape[1]
+    span = width // 32
+    gu = gu_total.shape
+    units = gu[1] * 4
+    up = up_grad.shape[3:]
+    heads = out_grad.shape[2:]
+    outs = [
+        shaped((rows, width)),
+        shaped((span, rank_dim), f32),
+        shaped((span, HEAD_DIM), f32),
+        shaped((span, HEAD_DIM), f32),
+        shaped((1, 256), f32),
+        shaped((span, units), f32),
+        shaped((span, units), f32),
+        shaped((up[0] // 4, 8 * up[1]), f32),
+        shaped(heads, f32),
+    ]
+    sums = (2, 2, 2, 2, span, near)
+    scratch = reduce_scratch(rows, width) + [
+        pltpu.VMEM((rows, width), f32),
+        pltpu.VMEM((rows, 2 * HEAD_DIM), bf16),
+        pltpu.VMEM((rows, 2 * HEAD_DIM), bf16),
+        pltpu.VMEM(first_weight.shape, bf16),
+        pltpu.VMEM((rows, near), bf16),
+        pltpu.VMEM((rows, width), f32),
+        pltpu.VMEM((8, width), f32),
+        pltpu.VMEM((2, 2, 2, 2, 2, span, near), bf16),
+        pltpu.VMEM(sums, bf16),
+        pltpu.VMEM(sums, bf16),
+        pltpu.VMEM(sums, bf16),
+        pltpu.VMEM((2, 2, 2, 2, 2, 1, 256), f32),
+        pltpu.VMEM((2, 2, 2, 2, 2, 1, 256), f32),
+        pltpu.VMEM(gu, bf16),
+        pltpu.VMEM(gu, bf16),
+        pltpu.VMEM((1, 8, span, gu[1]), bf16),
+        pltpu.VMEM((2,) + gu, bf16),
+        pltpu.VMEM((2, 2) + up, bf16),
+        pltpu.VMEM((2, 2) + up, bf16),
+        pltpu.VMEM((2,) + up, bf16),
+        pltpu.VMEM((2,) + up, bf16),
+        pltpu.VMEM((2,) + up, bf16),
+        pltpu.VMEM((2,) + up, bf16),
+        pltpu.VMEM((8, up[0] // 4, up[1]), bf16),
+        pltpu.VMEM((2, 2) + heads, bf16),
+        pltpu.VMEM((2,) + heads, bf16),
+        pltpu.VMEM((2,) + heads, bf16),
+        pltpu.VMEM(heads, bf16),
+        pltpu.VMEM(heads, bf16),
+        pltpu.VMEM(heads, bf16),
+    ]
+    operands = (
+        parts, normed, compressed, tokens, grad_middle, first_weight, gain_in, gain_q, gain_mid_grad, cosine, sine,
+        gu_total, gu_passed, gu_kept, up_grad, out_grad,
+    )
+    return moving(
+        tail_kernel, 7, outs, operands, scratch + wires(80, 24),
+        in_specs=[ANY] + [VMEM] * 4 + [ANY] + [VMEM] * 5 + [ANY, ANY, VMEM, ANY, ANY],
+        out_specs=[VMEM] * 9,
+        limit=62,
+    )
+
+
+def rope_table(places):
+    half = HEAD_DIM // 2
+    freqs = rope_base ** (-(2.0 * jnp.arange(half).astype(f32)) / HEAD_DIM)
+    angles = places.astype(f32)[:, None] * freqs[None, :]
+    return jnp.cos(angles), jnp.sin(angles)
+
+
+def plane_local(
+    tokens,
+    positions,
+    cotangent,
+    norm_in_gain,
+    q_down,
+    q_gain,
+    q_up,
+    key_proj,
+    value_proj,
+    out_proj,
+    norm_mid_gain,
+    w_gate,
+    w_up,
+    w_down,
+):
+    rows, width = tokens.shape
+    rank_dim = q_down.shape[1]
+    seq = lax.axis_index("seq")
+    h, l, c = seq // 4, (seq // 2) % 2, seq % 2
+    span, q_span = norm_in_gain.shape[0], q_gain.shape[0]
+
+    gains = jnp.concatenate([norm_in_gain, norm_mid_gain, q_gain, jnp.zeros((256 - 2 * span - q_span,), f32)])
+    gains = lax.reduce_precision(gains, 8, 7).reshape(1, 256)
+    first_weight, up_query, gu_set, wo_own, wo_far, wd_own, gains, places = head(
+        q_down, key_proj, value_proj, gains, q_up, w_gate, w_up, out_proj, w_down, positions.reshape(1, rows)
+    )
+    first_weight = first_weight.reshape(width, rank_dim + 2 * HEAD_DIM)
+    up_query = up_query.reshape(rank_dim, 2 * HEAD_DIM)
+    gains = gains.reshape(32, 256)
+    in_gain = gains[:, :span].reshape(1, width)
+    mid_gain = gains[:, span : 2 * span].reshape(1, width)
+    query_gain = gains[:, 2 * span : 2 * span + q_span].reshape(1, rank_dim)
+
+    blocks = jnp.arange(4, dtype=jnp.int32) ^ (l * 2 + c)
+    in_half = (blocks[:, None] * rows + jnp.arange(rows, dtype=jnp.int32)[None, :]).reshape(-1)
+    own_index = h * (4 * rows) + in_half
+    query_index = jnp.concatenate([own_index, own_index]).reshape(1, 8 * rows)
+    places = places.reshape(1, 8 * rows)
+    first_index = query_index - places
+    key_index = jnp.concatenate([own_index, (1 - h) * (4 * rows) + in_half]).reshape(8 * rows, 1)
+    cosine, sine = rope_table(places.reshape(-1))
+
+    plane_set, out_weight, gu_far, normed, compressed = pack(
+        tokens, in_gain, query_gain, first_weight, cosine[:rows], sine[:rows], wo_own, wo_far, gu_set[0]
+    )
+    out_weight = out_weight.reshape(2 * HEAD_DIM, width)
+    queries, attended, lse, out_parts, plane_cotangent, gu_one, gu_far = attend(
+        plane_set, up_query, out_weight, cosine, sine, key_index, query_index, first_index, cotangent,
+        gu_set[0], gu_far, gu_set[1],
+    )
+    middle, plane_mid, gu_two, down_weight = middle_step(out_parts, tokens, mid_gain, gu_set[1], gu_far, wd_own)
+    plane_mid = plane_mid.reshape(8 * rows, width)
+    plane_cotangent = plane_cotangent.reshape(8 * rows, width)
+    hidden, gu_grads, mid_parts, final_parts = feed(plane_mid, plane_cotangent, gu_one, gu_two, down_weight)
+
+    def over_tokens(left, right):
+        grad = lax.dot_general(left, right, (((0,), (0,)), ((), ())), preferred_element_type=f32)
+        return grad.astype(bf16)
+
+    by_rows = lambda grad: grad.reshape(2, 2, 2, -1, grad.shape[-1])
+    by_plane = lambda parts: parts.reshape(2, 2, 2, rows, -1)
+    down_grad = over_tokens(hidden, plane_cotangent).reshape(2, 2, -1, width)
+    gu_grad = by_rows(over_tokens(plane_mid, gu_grads))
+    grad_middle, mid_gain_grad, plane_branch, grad_down, gu_passed, gu_kept = branch_step(
+        by_plane(mid_parts), middle, cotangent, mid_gain, down_grad, gu_grad
+    )
+    query_grad, back_parts, output, gu_total, gu_passed, gu_kept = attend_back(
+        plane_set, plane_branch, queries, attended, lse, up_query, out_weight, cosine, sine,
+        key_index, query_index, first_index, by_plane(final_parts), middle, gu_passed, gu_kept, gu_grad,
+    )
+    out_grad = over_tokens(attended, plane_branch.reshape(8 * rows, width)).reshape(2, 2, -1, width)
+    up_grad = by_rows(over_tokens(plane_set.reshape(8 * rows, -1)[:, :rank_dim], query_grad))
+    grad_tokens, grad_q_down, grad_key, grad_value, grad_gains, grad_gate, grad_up, grad_q_up, grad_out = tail(
+        back_parts, normed, compressed, tokens, grad_middle, first_weight, in_gain, query_gain, mid_gain_grad,
+        cosine[:rows], sine[:rows], gu_total, gu_passed, gu_kept, up_grad, out_grad,
+    )
+    return (
+        output,
+        grad_tokens,
+        grad_gains[0, :span],
+        grad_q_down,
+        grad_gains[0, 2 * span : 2 * span + q_span],
+        grad_q_up,
+        grad_key,
+        grad_value,
+        grad_out,
+        grad_gains[0, span : 2 * span],
+        grad_gate,
+        grad_up,
+        grad_down,
+    )
+
+
 def solution(mesh):
     return jax.shard_map(
-        local,
+        plane_local if dict(mesh.shape) == {"dp": 4, "seq": 8} else local,
         mesh=mesh,
         in_specs=(
             P(("dp", "seq"), None),

time: 3570 us -> 670 us (0.19)
  waiting for transfers between devices: 2900 us -> 0 us
  Pallas kernels: 0 us -> 601 us
  matrix products: 390 us -> 33.7 us
  blocking collectives: 115 us -> 0 us
  local copies, waits for them, and re-layouts: 72.8 us -> 21 us
  other arithmetic: 53.4 us -> 7.1 us
    reduce_scatter x10 -> x0, waiting for transfers between devices: 2340 us -> none  [the longest x1 491 us: local(): lax.psum_scatter(grad_up_weight, ('dp', 'seq'), scatter_dimension=0, tile...]
    pallas_call x0 -> x8, Pallas kernels: none -> 601 us  [the longest x7 563 us: moving(): pl.pallas_call(kernel, out_shape=outs, in_specs=in_specs or [ANY] * len(o...]
    all_gather x8 -> x0, waiting for transfers between devices: 556 us -> none  [the longest x1 134 us: local(): lax.all_gather(w_up.astype(jnp.bfloat16), ('dp', 'seq'), axis=0, tiled=True)]
    dot_general x80 -> x4, matrix products: 390 us -> 33.7 us  [over_tokens(): lax.dot_general(left, right, (((0,), (0,)), ((), ())), preferred_element_...]
    unnamed x2 -> x0, blocking collectives: 80.6 us -> none
    convert_element_type x29 -> x1, other arithmetic: 43.3 us -> 0.72 us  [rope_table(): angles = places.astype(f32)[:, None] * freqs[None, :]]
    convert_element_type x17 -> x1, local copies, waits for them, and re-layouts: 41.3 us -> 0.07 us  [rope_table(): angles = places.astype(f32)[:, None] * freqs[None, :]]
  transfers between devices with their start and end apart: 18 -> 0, of which waited for: 16 -> 0; matrix products, arithmetic and copies ran while one was open for 8% -> 0% of each run, Pallas kernels for 0% -> 0%
where the time goes in v2:
time: 670 us; the launch traced here: 664 us
  Pallas kernels  601 us (90%)
  matrix products  33.7 us (5%)
  local copies, waits for them, and re-layouts  21 us (3%)
  other arithmetic  7.1 us (1%)
    pallas_call x7, Pallas kernels, moving(): pl.pallas_call(kernel, out_shape=outs, in_specs=in_specs or [ANY] * len(o...  563 us
    pallas_call x1, Pallas kernels, feed(): pl.pallas_call(feed_kernel, grid=(tokens // block,), in_specs=[by_block(w...  37.7 us
    dot_general x4, matrix products, over_tokens(): lax.dot_general(left, right, (((0,), (0,)), ((), ())), preferred_element_...  33.7 us

profile of v2, /device:TPU:0, one launch (start us, length us, event | category | flops | bytes accessed | tf_op | source)
XLA Modules:
  0.0 663.8 jit_solution(13610265713972198455)
XLA Ops:
  0.7 0.1 pad.9.clone
  0.8 1.3 maximum_reduce-precision_fusion.gains
  2.1 0.1 fusion.5
  2.2 0.1 add.74
  2.3 0.1 concatenate.39
  2.4 0.1 add.71
  2.4 0.6 reshape.220.query_index
  3.1 1.1 reshape.233.key_index
  4.2 83.8 %head_kernel.1 = (bf16[2,2,2,2,2,64,1536]{6,5,4,3,2,1,0:T(8,128)(2,1)}, bf16[2,2,2,128,512]{4,3,2,1,0:T(8,128)(2,1)}, bf16[2,256,1408]{2,1,0:T(8,128)(2,1)}, bf1...) custom-call(f32[64,1024]{1,0:T(8,128)} %q_down.1, ...), custom_call_target="tpu_custom_call" | custom-call | bytes 100000000 | tf_op jit(solution)/shard_map/head_kernel/pallas_call | solution.py:422
  88.0 0.9 reduce
  88.9 0.7 reduce.2
  89.6 0.1 reshape.221
  89.7 0.6 add_subtract_fusion.first_index
  90.3 0.7 convert_reduce_fusion
  91.0 0.1 convert_element_type.30
  91.1 0.7 reshape.215.gain_q
  91.7 0.1 fusion.7
  91.8 0.7 reshape.222.gain
  92.5 0.7 reshape.214.gain_in
  93.2 2.5 slice_bitcast_fusion
  95.7 2.8 multiply_sine_fusion
  98.5 0.0 copy-start
  98.5 0.0 copy-start.1
  98.5 0.7 slice.51.sine
  99.2 0.6 slice.50.cosine
  99.9 65.1 %pack_kernel.1 = (bf16[2,2,2,192,2048]{4,3,2,1,0:T(8,128)(2,1)}, bf16[2,2,128,2048]{3,2,1,0:T(8,128)(2,1)}, bf16[256,1408]{1,0:T(8,128)(2,1)}, bf16[192,2048]{1,0:T(8,128)(2,1)}, f32[192,1024]{1,0:T(8,128)}) custom-call(bf16[192,2048]{1,0:T(8,128)(2,1)} %tokens.5, f32[1,2048]{1,0:T(1,128)} %reshape.214.gain_in, f32[1,1024]{1,0:T(1,128)} %reshape.215.gain_q, ...), custom_call_target="tpu_custom_call" | custom-call | bytes 100000000 | tf_op jit(solution)/shard_map/pack_kernel/pallas_call | solution.py:422
  165.0 0.0 copy-done
  165.0 0.0 copy-done.1
  165.0 54.5 %attend_kernel.1 = (bf16[1536,512]{1,0:T(8,128)(2,1)}, bf16[1536,512]{1,0:T(8,128)(2,1)}, f32[2,1,1536]{2,1,0:T(1,128)}, bf16[2,2,2,192,2048]{4,3,2,1,0:T(8,128)...) custom-call(bf16[2,2,2,192,2048]{4,3,2,1,0:T(8,128)(2,1)} %get-tuple-elem, ...), custom_call_target="tpu_custom_call" | custom-call | bytes 100000000 | tf_op jit(solution)/shard_map/attend_kernel/pallas_call | solution.py:422
  219.5 0.0 slice-start
  219.5 84.2 %middle_kernel.1 = (f32[192,2048]{1,0:T(8,128)}, bf16[2,2,2,192,2048]{4,3,2,1,0:T(8,128)(2,1)}, bf16[2,2,256,1408]{3,2,1,0:T(8,128)(2,1)}, bf16[2,2,176,2048]{3,2,1,0:T(8,128)(2,1)}) custom-call(bf16[2,2,2,192,2048]{4,3,2,1,0:T(8,128)(2,1)} %get-tuple-element.72.parts, bf16[192,2048]{1,0:T(8,128)(2,1)} %tokens.5, f32[1,2048]{1,0:T(1,128)} %reshape.222.gain, ...), custom_call_target="tpu_custom_call" | custom-call | bytes 100000000 | tf_op jit(solution)/shard_map/middle_kernel/pallas_call | solution.py:422
  303.7 0.0 slice-start.1
  303.7 37.7 %feed.1 = (bf16[1536,704]{1,0:T(8,128)(2,1)}, bf16[1536,1408]{1,0:T(8,128)(2,1)}, bf16[1536,2048]{1,0:T(8,128)(2,1)}, bf16[1536,2048]{1,0:T(8,128)(2,1)}) custom-call(bf16[1536,2048]{1,0:T(8,128)(2,1)} %bitcast.59, bf16[1536,2048]{1,0:T(8,128)(2,1)} %bitcast.55, bf16[2,2,256,1408]{3,2,1,0:T(8,128)(2,1)} %get-tuple-element.77.gu_one, ...), custom_call_target="tpu_custom_call" | custom-call | flops 26575110144 | bytes 40000000 | tf_op jit(solution)/shard_map/feed/pallas_call | solution.py:986
  341.5 0.0 copy-start.13
  341.5 15.2 %convolution_convert_fusion = bf16[2048,1408]{1,0:T(8,128)(2,1)} fusion(bf16[1536,2048]{1,0:T(8,128)(2,1)} %bitcast.60, bf16[1536,1408]{1,0:T(8,128)(2,1)} %get-tuple-element.83), kind=kOutput, calls=%fused_computation | convolution fusion | flops 8861253632 | bytes 16384000 | tf_op jit(solution)/shard_map/dot_general | solution.py:1603
  356.6 0.0 slice-done
  356.6 0.0 slice-done.1
  356.6 0.0 copy-done.13
  356.7 6.2 convolution_convert_fusion.1
  362.9 84.1 %branch_kernel.1 = (f32[192,2048]{1,0:T(8,128)}, f32[1,2048]{1,0:T(1,128)}, bf16[2,2,2,192,2048]{4,3,2,1,0:T(8,128)(2,1)}, f32[176,2048]{1,0:T(8,128)}, bf16[256...) custom-call(bf16[2,2,2,192,2048]{4,3,2,1,0:T(8,128)(2,1)} %bitcast.44, f32[192,2048]{1,0:T(8,128)} %get-tuple-element.81.middle, ...), custom_call_target="tpu_custom_call" | custom-call | bytes 100000000 | tf_op jit(solution)/shard_map/branch_kernel/pallas_call | solution.py:422
  447.0 0.0 copy-start.2
  447.0 58.4 %attend_back_kernel.1 = (bf16[1536,512]{1,0:T(8,128)(2,1)}, bf16[2,2,2,192,2048]{4,3,2,1,0:T(8,128)(2,1)}, bf16[192,2048]{1,0:T(8,128)(2,1)}, bf16[256,1408]{1,0...) custom-call(bf16[2,2,2,192,2048]{4,3,2,1,0:T(8,128)(2,1)} %get-tuple-element.68.plane_set, ...), custom_call_target="tpu_custom_call" | custom-call | bytes 100000000 | tf_op jit(solution)/shard_map/attend_back_kernel/pallas_call | solution.py:422
  505.4 0.0 copy-done.2
  505.4 0.0 copy-start.12
  505.4 7.5 %convolution_convert_fusion.2 = bf16[512,2048]{1,0:T(8,128)(2,1)} fusion(bf16[1536,512]{1,0:T(8,128)(2,1)S(1)} %copy-done.2, bf16[1536,2048]{1,0:T(8,128)(2,1)} %bitcast.43), kind=kOutput, calls=%fused_computation.4 | convolution fusion | flops 3222274048 | bytes 9961472 | tf_op jit(solution)/shard_map/dot_general | solution.py:1603
  513.0 0.0 copy-done.12
  513.0 4.7 fusion.2
  517.7 132.9 %tail_kernel.1 = (bf16[192,2048]{1,0:T(8,128)(2,1)}, f32[64,1024]{1,0:T(8,128)}, f32[64,256]{1,0:T(8,128)}, f32[64,256]{1,0:T(8,128)}, f32[1,256]{1,0:T(1,128)},...) custom-call(bf16[2,2,2,192,2048]{4,3,2,1,0:T(8,128)(2,1)} %get-tuple-element.92.parts, ...), custom_call_target="tpu_custom_call" | custom-call | bytes 100000000 | tf_op jit(solution)/shard_map/tail_kernel/pallas_call | solution.py:422
  650.6 0.0 copy-start.9
  650.6 0.0 copy-start.8
  650.6 0.0 copy-start.11
  650.7 1.3 slice_bitcast_fusion.3
  651.9 1.3 slice_bitcast_fusion.2
  653.2 0.9 copy.40
  654.1 2.2 copy.41
  656.3 0.7 copy.42
  657.0 0.8 copy.43
  657.8 0.6 copy.44
  658.4 0.6 copy.45
  659.1 1.0 copy.46
  660.1 1.1 copy.47
  661.2 0.0 copy-done.4
  661.2 1.1 copy.48
  662.3 1.1 copy.49
  (21 shorter events, 0.1 us)
Async XLA Ops:
  98.5 66.5 %copy-start = (f32[1536,128]{1,0:T(8,128)}, f32[1536,128]{1,0:T(8,128)S(1)}, u32[]{:S(2)}) copy-start(f32[1536,128]{1,0:T(8,128)S(1)} %get-tuple-element.115.sine) | copy-start | bytes 2359300
  98.5 66.5 %copy-start.1 = (f32[1536,128]{1,0:T(8,128)}, f32[1536,128]{1,0:T(8,128)S(1)}, u32[]{:S(2)}) copy-start(f32[1536,128]{1,0:T(8,128)S(1)} %get-tuple-element.116.cosine) | copy-start | bytes 2359300
  219.5 137.1 %slice-start = ((s8[6291456]{0:T(1024)(128)(4,1)}), s8[4194304]{0:T(1024)(128)(4,1)S(1)}, s32[]{:S(2)}) async-start(s8[6291456]{0:T(1024)(128)(4,1)} %bitcast.56), calls=%async_computation | async-start | bytes 8388608
  303.7 52.9 %slice-start.1 = ((s8[6291456]{0:T(1024)(128)(4,1)}), s8[2097152]{0:T(1024)(128)(4,1)S(1)}, s32[]{:S(2)}) async-start(s8[6291456]{0:T(1024)(128)(4,1)} %bitcast.56), calls=%async_computation.1 | async-start | bytes 4194304
  341.5 15.2 %copy-start.13 = (bf16[1536,704]{1,0:T(8,128)(2,1)S(1)}, bf16[1536,704]{1,0:T(8,128)(2,1)}, u32[]{:S(2)}) copy-start(bf16[1536,704]{1,0:T(8,128)(2,1)} %get-tuple-element.82) | copy-start | bytes 6488068
  447.0 58.4 %copy-start.2 = (bf16[1536,512]{1,0:T(8,128)(2,1)S(1)}, bf16[1536,512]{1,0:T(8,128)(2,1)}, u32[]{:S(2)}) copy-start(bf16[1536,512]{1,0:T(8,128)(2,1)} %get-tuple-element.86.attended) | copy-start | bytes 4718596
  505.4 7.6 %copy-start.12 = (bf16[1536,512]{1,0:T(8,128)(2,1)S(1)}, bf16[1536,512]{1,0:T(8,128)(2,1)}, u32[]{:S(2)}) copy-start(bf16[1536,512]{1,0:T(8,128)(2,1)} %get-tuple-element.100) | copy-start | bytes 4718596
  517.7 135.6 %copy-start.7 = (bf16[192,2048]{1,0:T(8,128)(2,1)S(1)}, bf16[192,2048]{1,0:T(8,128)(2,1)}, u32[]{:S(2)}) copy-start(bf16[192,2048]{1,0:T(8,128)(2,1)} %get-tuple-element.136) | copy-start | bytes 2359300
  650.6 5.7 copy-start.9
  650.6 6.4 copy-start.8
  650.6 7.2 %copy-start.11 = (f32[64,256]{1,0:T(8,128)S(1)}, f32[64,256]{1,0:T(8,128)}, u32[]{:S(2)}) copy-start(f32[64,256]{1,0:T(8,128)} %get-tuple-element.142) | copy-start | bytes 196612
  650.6 7.8 %copy-start.10 = (f32[64,256]{1,0:T(8,128)S(1)}, f32[64,256]{1,0:T(8,128)}, u32[]{:S(2)}) copy-start(f32[64,256]{1,0:T(8,128)} %get-tuple-element.143) | copy-start | bytes 196612
  650.6 8.4 %copy-start.6 = (f32[128,2048]{1,0:T(8,128)S(1)}, f32[128,2048]{1,0:T(8,128)}, u32[]{:S(2)}) copy-start(f32[128,2048]{1,0:T(8,128)} %get-tuple-element.144) | copy-start | bytes 3145732
  654.1 5.9 copy-start.5
  657.0 4.1 copy-start.4
  660.0 2.2 copy-start.3

commit v3 on v2

--- a/solution.py
+++ b/solution.py
@@ -447,134 +447,159 @@
     return ref[where].astype(f32)
 
 
-def plane_gather(wire, block, out, own):
-    half = block.shape[0] // 2
-    top, low = pl.ds(0, half), pl.ds(half, half)
-    from_x = wire.send(block, out.at[1, 0, 0], 8)
-    from_l = wire.send(block, out.at[0, 1, 0], 2)
+def routes(rows, pieces, direct):
+    size = rows // pieces
+    return [(pl.ds(i * size, size), "xl" if i < direct else "lx") for i in range(pieces)]
+
+
+def plane_gather(wire, block, out, own, ways):
+    links = {"x": (out.at[1, 0, 0], out.at[1, 0, 1], 8), "l": (out.at[0, 1, 0], out.at[0, 1, 1], 2)}
+    far, far_core = out.at[1, 1, 0], out.at[1, 1, 1]
+    ordered = [k for k in range(len(ways)) if ways[k][1] == "xl"] + [k for k in range(len(ways)) if ways[k][1] == "lx"]
+    came = {}
+    for turn in (0, 1):
+        for k in ordered:
+            rows, way = ways[k]
+            target, _, mask = links[way[turn]]
+            came[way[turn], k] = wire.send(block.at[rows], target.at[rows], mask)
     cores = [wire.send(block, out.at[0, 0, 1], 1)]
     mine = wire.local(block, own) if own is not None else None
-
-    def second():
-        from_x.wait_recv()
-        diagonal = [wire.send(out.at[1, 0, 0, top], out.at[1, 1, 0, top], 2)]
-        from_l.wait_recv()
-        diagonal += [wire.send(out.at[0, 1, 0, low], out.at[1, 1, 0, low], 8)]
-        cores.append(wire.send(out.at[1, 0, 0], out.at[1, 0, 1], 1))
-        cores.append(wire.send(out.at[0, 1, 0], out.at[0, 1, 1], 1))
-
-        def finish():
-            diagonal[0].wait_recv()
-            cores.append(wire.send(out.at[1, 1, 0, top], out.at[1, 1, 1, top], 1))
-            diagonal[1].wait_recv()
-            cores.append(wire.send(out.at[1, 1, 0, low], out.at[1, 1, 1, low], 1))
-            if mine is not None:
-                mine.wait()
-            arrived(cores)
-
-        return finish
-
-    return second
-
-
-def plane_reduce(wire, parts, out, kept, from_c, send_one, recv_one, send_two, recv_two):
-    half = kept.shape[2] // 2
-    order = [(1, 1), (1, 0), (0, 1), (0, 0)]
-    cores = {k: wire.send(parts.at[k[0], k[1], 1], from_c.at[k[0], k[1]], 1) for k in order}
-    loads = {k: wire.local(parts.at[k[0], k[1], 0], kept.at[k[0], k[1]]) for k in order}
+    diagonal = {}
+
+    def step(k):
+        rows, way = ways[k]
+        target, core, _ = links[way[0]]
+        came[way[0], k].wait_recv()
+        diagonal[k] = wire.send(target.at[rows], far.at[rows], links[way[1]][2])
+        cores.append(wire.send(target.at[rows], core.at[rows], 1))
+
+    def finish():
+        for k in ordered:
+            rows, way = ways[k]
+            target, core, _ = links[way[1]]
+            came[way[1], k].wait_recv()
+            cores.append(wire.send(target.at[rows], core.at[rows], 1))
+        for k in ordered:
+            rows, way = ways[k]
+            diagonal[k].wait_recv()
+            cores.append(wire.send(far.at[rows], far_core.at[rows], 1))
+        if mine is not None:
+            mine.wait()
+        arrived(cores)
+
+    return [lambda k=k: step(k) for k in ordered], finish
+
+
+ARRIVAL = [(1, 1), (1, 0), (0, 1), (0, 0)]
+
+
+def plane_reduce(wire, parts, out, kept, from_c, send_one, recv_one, send_two, recv_two, ways, load=True):
+    cores = {}
+    loads = {}
+    masks = {"x": 8, "l": 2}
+    beside = {"xl": (1, 0), "lx": (0, 1)}
+    after = {"xl": (0, 1), "lx": (1, 0)}
+    came = {}
+    passed = {}
+
+    def give(k):
+        cores[k] = wire.send(parts.at[k[0], k[1], 1], from_c.at[k[0], k[1]], 1)
+        if load:
+            loads[k] = wire.local(parts.at[k[0], k[1], 0], kept.at[k[0], k[1]])
 
     def pair(k, r):
         return wide(kept.at[k[0], k[1]], r) + wide(from_c.at[k[0], k[1]], r)
 
-    def below(r):
-        return pl.ds(half + r.start, r.size)
-
-    state = {}
-
-    def first():
-        for k in order[:3]:
+    def within(rows, body):
+        @pl.loop(0, rows.size // 16)
+        def _(i):
+            body(pl.ds(pl.multiple_of(rows.start + i * 16, 16), 16))
+
+    def put(slot, k, j):
+        rows, way = ways[j]
+
+        def fill(r):
+            send_one[slot, r] = pair(k, r).astype(bf16)
+
+        within(rows, fill)
+        came[slot, j] = wire.send(send_one.at[slot, rows], recv_one.at[slot, rows], masks[way[0]])
+
+    def arrive(k):
+        if load:
             loads[k].wait()
-            cores[k].wait_recv()
-            if k[0]:
-
-                def fill(r, k=k):
-                    send_one[0, k[1], r] = pair(k, r).astype(bf16)
-
-                each_rows(half, fill)
-                state["x", k[1]] = wire.send(send_one.at[0, k[1]], recv_one.at[0, k[1]], 8)
-            if k[1]:
-
-                def fill(r, k=k):
-                    send_one[1, k[0], r] = pair(k, below(r)).astype(bf16)
-
-                each_rows(half, fill)
-                state["l", k[0]] = wire.send(send_one.at[1, k[0]], recv_one.at[1, k[0]], 2)
-        loads[0, 0].wait()
-        cores[0, 0].wait_recv()
-
-    def middle():
-        state["x", 1].wait_recv()
+        cores[k].wait_recv()
+        for j in range(len(ways)):
+            if k == (1, 1):
+                put(0, k, j)
+            elif beside[ways[j][1]] == k:
+                put(1, k, j)
+
+    def step(j):
+        rows, way = ways[j]
+        came[0, j].wait_recv()
 
         def fill(r):
-            send_two[0, r] = (pair((0, 1), r) + wide(recv_one.at[0, 1], r)).astype(bf16)
-
-        each_rows(half, fill)
-        state["l2"] = wire.send(send_two.at[0], recv_two.at[0], 2)
-        state["l", 1].wait_recv()
-
-        def fill(r):
-            send_two[1, r] = (pair((1, 0), below(r)) + wide(recv_one.at[1, 1], r)).astype(bf16)
-
-        each_rows(half, fill)
-        state["x2"] = wire.send(send_two.at[1], recv_two.at[1], 8)
+            send_two[r] = (pair(after[way], r) + wide(recv_one.at[0], r)).astype(bf16)
+
+        within(rows, fill)
+        passed[j] = wire.send(send_two.at[rows], recv_two.at[rows], masks[way[1]])
 
     def finish():
-        state["x", 0].wait_recv()
-        state["l2"].wait_recv()
-
-        def fill(r):
-            out[r] = pair((0, 0), r) + wide(recv_one.at[0, 0], r) + wide(recv_two.at[0], r)
-
-        each_rows(half, fill)
-        state["l", 0].wait_recv()
-        state["x2"].wait_recv()
-
-        def fill(r):
-            out[below(r)] = pair((0, 0), below(r)) + wide(recv_one.at[1, 0], r) + wide(recv_two.at[1], r)
-
-        each_rows(half, fill)
-
-    return first, middle, finish
+        for j, (rows, way) in enumerate(ways):
+            came[1, j].wait_recv()
+            passed[j].wait_recv()
+
+            def fill(r):
+                out[r] = pair((0, 0), r) + wide(recv_one.at[1], r) + wide(recv_two, r)
+
+            within(rows, fill)
+
+    return give, arrive, [lambda j=j: step(j) for j in range(len(ways))], finish
+
+
+def each(action, items=ARRIVAL):
+    for item in items:
+        action(item)
+
+
+def do(steps):
+    for step in steps:
+        step()
 
 
 def reduce_scratch(rows, width):
-    half = rows // 2
     return [
         pltpu.VMEM((2, 2, rows, width), bf16),
         pltpu.VMEM((2, 2, rows, width), bf16),
-        pltpu.VMEM((2, 2, half, width), bf16),
-        pltpu.VMEM((2, 2, half, width), bf16),
-        pltpu.VMEM((2, half, width), bf16),
-        pltpu.VMEM((2, half, width), bf16),
+        pltpu.VMEM((2, rows, width), bf16),
+        pltpu.VMEM((2, rows, width), bf16),
+        pltpu.VMEM((rows, width), bf16),
+        pltpu.VMEM((rows, width), bf16),
     ]
 
 
-def over_y(wire, own, far, place):
+def over_y(wire, block, place, side):
     y, x, h, l, c = coordinates()
-    mine = [wire.local(own, place(y, h)), wire.local(far, place(y, 1 - h))]
-    sent = [wire.send(own, place(y, h), 16), wire.send(far, place(y, 1 - h), 16)]
+    hh = h if side == 0 else 1 - h
+    mine = wire.local(block, place(y, hh))
+    sent = wire.send(block, place(y, hh), 16)
 
     def finish():
-        landed(mine)
-        arrived(sent)
+        mine.wait()
+        sent.wait_recv()
 
     return finish
+
+
+def thirds(width):
+    main = (width * 5 // 12) // 128 * 128
+    return [pl.ds(0, main), pl.ds(main, main), pl.ds(2 * main, width - 2 * main)]
 
 
 def head_kernel(
     q_down, key, value, gains, q_up, gate, up, out_proj, w_down, places,
-    first_out, upq_out, gu_out, wo_out, wo_far, wd_out, gains_out, places_out,
-    first, upq, gu, staged, send_sem, recv_sem, local_sem,
+    first_out, upq_out, gu, wo_out, wo_far, wd_out, in_gain, mid_gain, q_gain, place_row,
+    first, upq, staged, gains_out, places_out, send_sem, recv_sem, local_sem,
 ):
     y, x, h, l, c = coordinates()
     rank = x * 4 + l * 2 + c
@@ -585,8 +610,7 @@
     first[:, r1:r2] = key[...].astype(bf16)
     first[:, r2:] = value[...].astype(bf16)
     width = first.shape[1]
-    third = width // 3
-    a, b, d = (pl.ds(i * third, third) for i in range(3))
+    a, b, d = thirds(width)
     mine = [wire.local(first, first_out.at[y, x, h, l, c]), wire.local(gains, gains_out.at[y, x, h, l, c])]
     one = [wire.send(first.at[:, p], first_out.at[y, x, h, l, c, :, p], 4) for p in (a, b, d)]
     gain = wire.send(gains, gains_out.at[y, x, h, l, c], 4)
@@ -602,7 +626,6 @@
     up_mine = wire.local(upq.at[rank], up_place())
     up_sent = [wire.send(upq.at[flip(rank, j)], up_place(), PLANE[j - 1]) for j in range(1, 8)]
     wo_out[...] = out_proj[...].astype(bf16)
-    wo_sent = wire.send(wo_out, wo_far, 4)
     piece = gate.shape[1] // 32
     size = 4 * piece
     main = size // 128 * 128
@@ -616,10 +639,6 @@
         both = jnp.concatenate([staged[0, :, main : main + rest], staged[1, :, main : main + rest]], axis=1)
         gu[target, :, main : main + 2 * rest] = both.astype(bf16)
         gu[target, :, main + 2 * rest :] = staged[1, :, :main].astype(bf16)
-    gu_rows = gu.shape[1]
-    gu_place = lambda: gu_out.at[x, pl.ds((l * 2 + c) * gu_rows, gu_rows), :]
-    gu_mine = wire.local(gu.at[rank], gu_place())
-    gu_sent = [wire.send(gu.at[flip(rank, j)], gu_place(), PLANE[j - 1]) for j in range(1, 8)]
     wd_out[...] = w_down[...].astype(bf16)
     landed(mine)
 
@@ -632,55 +651,51 @@
         place = first_out.at[at + (every, columns)]
         return wire.send(place, place, mask)
 
-    one[0].wait_recv()
-    two_a = step("h", a, 2)
-    one[1].wait_recv()
-    two_b = step("h", b, 8)
-    one[2].wait_recv()
-    two_d = step("h", d, 16)
-    gain.wait_recv()
-    gain = step("h", None, 2)
-    up_mine.wait()
-    arrived(up_sent)
-    up_h = wire.send(upq_out.at[y, :, h], upq_out.at[y, :, h], 4)
-    two_a.wait_recv()
-    three_a = step("hl", a, 8)
-    two_b.wait_recv()
-    three_b = step("hx", b, 16)
-    two_d.wait_recv()
-    three_d = step("hy", d, 2)
-    gain.wait_recv()
-    gain = step("hl", None, 8)
-    up_y = [wire.send(upq_out.at[y, :, h], upq_out.at[y, :, h], 16)]
-    three_a.wait_recv()
-    four_a = step("hlx", a, 16)
-    three_b.wait_recv()
-    four_b = step("hxy", b, 2)
-    three_d.wait_recv()
-    four_d = step("hyl", d, 8)
-    five = [step("hlx", a, 1), step("hxy", b, 1), step("hyl", d, 1)]
-    gain.wait_recv()
-    gain = step("hlx", None, 16)
-    up_h.wait_recv()
-    up_y += [wire.send(upq_out.at[y, :, 1 - h], upq_out.at[y, :, 1 - h], 16)]
-
     def last(held, bit, columns):
         at = {k: every if k in held else v for k, v in zip("yxhlc", (y, x, h, l, c))}
         at[bit] = 1 - dict(zip("yxhlc", (y, x, h, l, c)))[bit]
         place = first_out.at[tuple(at[k] for k in "yxhlc") + (every, columns)]
         return wire.send(place, place, 1)
 
-    four_a.wait_recv()
-    five += [last("hlx", "y", a)]
-    four_b.wait_recv()
-    five += [last("hxy", "l", b)]
+    bits = {"y": 16, "x": 8, "h": 4, "l": 2}
+    orders = [("hlxy", a), ("hlyx", b), ("hxyl", d)]
+    sent = one
+    for k in range(1, 4):
+        following = []
+        for (order, columns), copy in zip(orders, sent):
+            copy.wait_recv()
+            following.append(step(order[:k], columns, bits[order[k]]))
+        sent = following
+        gain.wait_recv()
+        gain = step("hlxy"[:k], None, bits["hlxy"[k]])
+        if k == 1:
+            up_mine.wait()
+            arrived(up_sent)
+            up_h = wire.send(upq_out.at[y, :, h], upq_out.at[y, :, h], 4)
+            up_y = [wire.send(upq_out.at[y, :, h], upq_out.at[y, :, h], 16)]
+            wo_sent = wire.send(wo_out, wo_far, 4)
+        if k == 3:
+            five = [step(order[:3], columns, 1) for order, columns in orders]
+    up_h.wait_recv()
+    up_y += [wire.send(upq_out.at[y, :, 1 - h], upq_out.at[y, :, 1 - h], 16)]
     gain.wait_recv()
-    five += [step("hlxy", None, 1)]
-    four_d.wait_recv()
-    five += [last("hyl", "x", d)]
-    gu_mine.wait()
+    gain = step("hlxy", None, 1)
+    for (order, columns), copy in zip(orders, sent):
+        copy.wait_recv()
+        five.append(last(order[:3], order[3], columns))
     place_mine.wait()
-    arrived(five + up_y + gu_sent + place + [wo_sent])
+    arrived(place)
+    rows = places.shape[1]
+    first_rows = jnp.concatenate([places_out[j] for j in range(8)], axis=1)
+    place_row[...] = first_rows
+    gain.wait_recv()
+    span, q_span = in_gain.shape[1] // 32, q_gain.shape[1] // 32
+    for n in range(32):
+        row = gains_out[n // 16, n // 8 % 2, n // 4 % 2, n // 2 % 2, n % 2]
+        in_gain[:, n * span : (n + 1) * span] = row[:, :span]
+        mid_gain[:, n * span : (n + 1) * span] = row[:, span : 2 * span]
+        q_gain[:, n * q_span : (n + 1) * q_span] = row[:, 2 * span : 2 * span + q_span]
+    arrived(five + up_y + [wo_sent])
     wire.close()
 
 
@@ -692,24 +707,27 @@
     outs = [
         shaped((2, 2, 2, 2, 2, rows, width)),
         shaped((2, 2, 2, 4 * q_up.shape[0], 2 * HEAD_DIM)),
-        shaped((2, 4 * rows, columns)),
+        shaped((8, rows, columns)),
         shaped(out_proj.shape),
         shaped(out_proj.shape),
         shaped(w_down.shape),
-        shaped((2, 2, 2, 2, 2) + gains.shape, f32),
-        shaped((8,) + places.shape, jnp.int32),
+        shaped((1, 32 * rows), f32),
+        shaped((1, 32 * rows), f32),
+        shaped((1, q_down.shape[1]), f32),
+        shaped((1, 8 * places.shape[1]), jnp.int32),
     ]
     scratch = [
         pltpu.VMEM((rows, width), bf16),
         pltpu.VMEM((8, q_up.shape[0], 2 * HEAD_DIM), bf16),
-        pltpu.VMEM((8, rows, columns), bf16),
         pltpu.VMEM((2, rows, slice_size), f32),
+        pltpu.VMEM((2, 2, 2, 2, 2) + gains.shape, f32),
+        pltpu.VMEM((8,) + places.shape, jnp.int32),
     ]
     operands = (q_down, key, value, gains, q_up, gate, up, out_proj, w_down, places)
     return moving(
-        head_kernel, 1, outs, operands, scratch + wires(60, 8),
+        head_kernel, 1, outs, operands, scratch + wires(100, 8),
         in_specs=[VMEM] * len(operands),
-        out_specs=[ANY, ANY, ANY, VMEM, ANY, VMEM, ANY, ANY],
+        out_specs=[ANY, ANY, VMEM, VMEM, ANY, VMEM, VMEM, VMEM, VMEM, VMEM],
     )
 
 
@@ -727,16 +745,20 @@
 
 
 def pack_kernel(
-    tokens, gain_in, gain_q, first_weight, cosine, sine, wo_own, wo_far, gu_set,
-    out, weight_out, gu_far, normed, compressed,
+    tokens, gain_in, gain_q, first_weight, cosine, sine, wo_own, wo_far, gu, wd_own,
+    out, weight_out, gu_out, wd_far, normed, compressed,
     weight, block, weight_all, send_sem, recv_sem, local_sem,
 ):
     y, x, h, l, c = coordinates()
     wire = Wire(send_sem, recv_sem, local_sem)
     load = wire.local(first_weight, weight)
-    greet(LINKS)
-    weight_done = over_y(wire, wo_own, wo_far, lambda yy, hh: weight_all.at[yy, hh])
-    gu_sent = wire.send(gu_set, gu_far, 4)
+    greet([16, 4] + PLANE)
+    rank = x * 4 + l * 2 + c
+    gu_rows = gu.shape[1]
+    gu_place = gu_out.at[x, pl.ds((l * 2 + c) * gu_rows, gu_rows), :]
+    gu_mine = wire.local(gu.at[rank], gu_place)
+    gu_sent = [wire.send(gu.at[flip(rank, j)], gu_place, PLANE[j - 1]) for j in range(1, 8)]
+    weight_done = [over_y(wire, ref, lambda yy, hh: weight_all.at[yy, hh], k) for k, ref in enumerate((wo_own, wo_far))]
     inputs = tokens[...].astype(f32)
     normed[...] = (inputs * row_scale(inputs) * gain_in[...]).astype(bf16)
     load.wait()
@@ -753,54 +775,60 @@
     far = 2 * HEAD_DIM
     columns, far_columns = pl.ds(0, near), pl.ds(near, far)
     from_h = wire.send(block.at[:, pl.ds(near - far, far)], out.at[0, 0, 0, :, far_columns], 4)
+    wd_sent = wire.send(wd_own, wd_far, 4)
     near_out = out.at[:, :, :, :, columns]
-    second = plane_gather(wire, block, near_out, near_out.at[0, 0, 0])
+    size = block.shape[0]
+    steps, finish = plane_gather(wire, block, near_out, near_out.at[0, 0, 0], routes(size, 4, 1))
     from_h.wait_recv()
     far_out = out.at[:, :, :, :, far_columns]
-    second_far = plane_gather(wire, far_out.at[0, 0, 0], far_out, None)
-    finish = second()
-    finish_far = second_far()
-    weight_done()
+    far_steps, far_finish = plane_gather(wire, far_out.at[0, 0, 0], far_out, None, routes(size, 2, 1))
+    do(steps)
+    do(far_steps)
+    do(weight_done)
     swapped = wire.send(weight_all.at[:, 1 - c], weight_out.at[:, c], 1)
     kept = wire.local(weight_all.at[:, c], weight_out.at[:, c])
     finish()
-    finish_far()
+    far_finish()
     kept.wait()
-    arrived([swapped, gu_sent])
+    gu_mine.wait()
+    arrived([swapped, wd_sent] + gu_sent)
     wire.close()
 
 
-def pack(tokens, gain_in, gain_q, first_weight, cosine, sine, wo_own, wo_far, gu_set):
+def pack(tokens, gain_in, gain_q, first_weight, cosine, sine, wo_own, wo_far, gu, wd_own):
     rows, width = tokens.shape
     near = first_weight.shape[1]
     rank_dim = near - 2 * HEAD_DIM
     outs = [
         shaped((2, 2, 2, rows, near + 2 * HEAD_DIM)),
         shaped((2, 2) + wo_own.shape),
-        shaped(gu_set.shape),
+        shaped((2, 4 * gu.shape[1], gu.shape[2])),
+        shaped(wd_own.shape),
         shaped((rows, width)),
         shaped((rows, rank_dim), f32),
     ]
-    operands = (tokens, gain_in, gain_q, first_weight, cosine, sine, wo_own, wo_far, gu_set)
+    operands = (tokens, gain_in, gain_q, first_weight, cosine, sine, wo_own, wo_far, gu, wd_own)
     return moving(
         pack_kernel, 2, outs, operands,
         [pltpu.VMEM(first_weight.shape, bf16), pltpu.VMEM((rows, near), bf16), pltpu.VMEM((2, 2) + wo_own.shape, bf16)]
-        + wires(32, 8),
-        in_specs=[VMEM, VMEM, VMEM, ANY, VMEM, VMEM, VMEM, VMEM, ANY],
-        out_specs=[ANY, VMEM, ANY, VMEM, VMEM],
-    )
-
-
-def scores_of(keys, queries, index, first, last):
-    scores = lax.dot_general(keys, queries, (((1,), (1,)), ((), ())), preferred_element_type=f32)
-    seen = (index >= first) & (index <= last)
-    return scores * (1.0 / math.sqrt(HEAD_DIM)), seen
+        + wires(60, 12),
+        in_specs=[VMEM, VMEM, VMEM, ANY, VMEM, VMEM, VMEM, VMEM, VMEM, VMEM],
+        out_specs=[ANY, VMEM, ANY, ANY, VMEM, VMEM],
+    )
+
+
+def mask_of(index, first, last):
+    return jnp.where((index >= first) & (index <= last), 0.0, masked_score)
+
+
+def scores_of(keys, queries):
+    return lax.dot_general(keys, queries, (((1,), (1,)), ((), ())), preferred_element_type=f32)
 
 
 def attend_kernel(
-    plane_set, wq, wo, cosine, sine, key_index, query_index, first_index, cotangent, gu_own, gu_far, gu_next,
-    queries_out, attended, lse, parts, cotangents, gu_out, gu_far_next,
-    kv, normed, staged, load_sem, send_sem, recv_sem, local_sem,
+    plane_set, wq, wo, cosine, sine, key_index, query_index, first_index, tokens, gain, cotangent, gu_set, wd_own, wd_far,
+    queries_out, attended, lse, middle, plane_mid, cotangents, gu_zero, gu_one, wd_out,
+    kv, normed, staged, mask, from_c, s1, r1, s2, r2, mid, gu_far, gu_next, load_sem, send_sem, recv_sem, local_sem,
 ):
     wire = Wire(send_sem, recv_sem, local_sem)
     rank_dim = wq.shape[0]
@@ -811,19 +839,23 @@
     for load in loads:
         load.start()
     greet(LINKS)
-    second = plane_gather(wire, cotangent, cotangents, cotangents.at[0, 0, 0])
-    gu_done = over_y(wire, gu_own, gu_far, lambda yy, hh: gu_out.at[yy, hh])
-    gu_sent = wire.send(gu_next, gu_far_next, 4)
+    places = [lambda yy, hh: gu_zero.at[yy, hh], lambda yy, hh: gu_one.at[yy, hh]]
+    passing, gathered = plane_gather(
+        wire, cotangent, cotangents, cotangents.at[0, 0, 0], routes(cotangent.shape[0], 4, 1)
+    )
+    far_sent = wire.send(gu_set.at[0], gu_far, 4)
+    gu_done = [over_y(wire, ref, lambda yy, hh: wd_out.at[yy, hh], k) for k, ref in enumerate((wd_own, wd_far))]
     landed(loads)
     rows = kv.shape[3]
     block = 2 * rows
 
     def one(g, i):
-        start = pl.multiple_of((g * 2 + i) * block, block)
+        start = (g * 2 + i) * block
         place = pl.ds(start, block)
         raw = jnp.dot(normed[g, i].reshape(block, rank_dim), wq[...], preferred_element_type=f32)
-        queries = turned(raw, cosine[place], sine[place], 1.0).astype(bf16)
+        queries = (turned(raw, cosine[place], sine[place], 1.0) * (1.0 / math.sqrt(HEAD_DIM))).astype(bf16)
         queries_out[place] = queries
+        mask[...] = mask_of(key_index[...], first_index[:, place], query_index[:, place])
         keys = jnp.concatenate(
             [kv[g, :, :, :, :HEAD_DIM].reshape(2 * block, HEAD_DIM), kv[g, :, :, :, 2 * HEAD_DIM : 3 * HEAD_DIM].reshape(2 * block, HEAD_DIM)]
         )
@@ -832,10 +864,7 @@
         )
         merged = []
         for a in range(2):
-            scores, seen = scores_of(
-                keys, queries[:, a * HEAD_DIM : (a + 1) * HEAD_DIM], key_index[...], first_index[:, place], query_index[:, place]
-            )
-            scores = jnp.where(seen, scores, masked_score)
+            scores = scores_of(keys, queries[:, a * HEAD_DIM : (a + 1) * HEAD_DIM]) + mask[...]
             top = jnp.max(scores, axis=0, keepdims=True)
             weights = jnp.exp(scores - top)
             total = jnp.sum(weights, axis=0, keepdims=True)
@@ -845,101 +874,81 @@
         merged = jnp.concatenate(merged, axis=1)
         attended[place] = merged
         staged[g, i] = jnp.dot(merged, wo[...], preferred_element_type=f32).astype(bf16).reshape(2, rows, -1)
-        pltpu.make_async_copy(staged.at[g, i], parts.at[g, i], load_sem.at[2 + g * 2 + i]).start()
-
-    @pl.loop(0, 2)
-    def _(k):
-        one(0, k)
-
-    finish = second()
-
-    @pl.loop(0, 2)
-    def _(k):
-        one(1, k)
-
-    for k in range(4):
-        pltpu.make_async_copy(staged.at[k // 2, k % 2], parts.at[k // 2, k % 2], load_sem.at[2 + k]).wait()
+
+    give, arrive, steps, finish = plane_reduce(
+        wire, staged, middle, staged.at[:, :, 0], from_c, s1, r1, s2, r2, routes(rows, 4, 3), load=False
+    )
+    for number, k in enumerate(ARRIVAL):
+        one(*k)
+        give(k)
+        if number == 0:
+            arrive(k)
+        elif number > 1:
+            arrive(ARRIVAL[number - 1])
+        if number == 1:
+            do(passing[:2])
+        if number == 2:
+            do(passing[2:])
+    arrive((0, 0))
+    gu_done += [over_y(wire, gu_set.at[k], places[k], 0) for k in range(2)]
+    do(steps)
+    far_sent.wait_recv()
+    next_sent = wire.send(gu_set.at[1], gu_next, 4)
+    gu_done.append(over_y(wire, gu_far, places[0], 1))
+    gathered()
     finish()
-    gu_done()
-    gu_sent.wait_recv()
+
+    def norm(r):
+        value = tokens[r].astype(f32) + middle[r]
+        middle[r] = value
+        mid[r] = (value * row_scale(value) * gain[...]).astype(bf16)
+
+    each_rows(rows, norm)
+    steps, finish = plane_gather(wire, mid, plane_mid, plane_mid.at[0, 0, 0], routes(rows, 4, 2))
+    do(steps)
+    next_sent.wait_recv()
+    gu_done.append(over_y(wire, gu_next, places[1], 1))
+    finish()
+    do(gu_done)
     wire.close()
 
 
-def attend(plane_set, wq, wo, cosine, sine, key_index, query_index, first_index, cotangent, gu_own, gu_far, gu_next):
-    rows = plane_set.shape[3]
-    tokens = 8 * rows
-    width = wo.shape[1]
+def attend(plane_set, wq, wo, cosine, sine, key_index, query_index, first_index, tokens, gain, cotangent, gu_set, wd_own, wd_far):
+    rows, width = tokens.shape
+    count = 8 * rows
     rank_dim = wq.shape[0]
+    gu = gu_set.shape[1:]
     outs = [
-        shaped((tokens, 2 * HEAD_DIM)),
-        shaped((tokens, 2 * HEAD_DIM)),
-        shaped((2, 1, tokens), f32),
+        shaped((count, 2 * HEAD_DIM)),
+        shaped((count, 2 * HEAD_DIM)),
+        shaped((2, 1, count), f32),
+        shaped((rows, width), f32),
         shaped((2, 2, 2, rows, width)),
         shaped((2, 2, 2, rows, width)),
-        shaped((2, 2) + gu_own.shape),
-        shaped(gu_next.shape),
+        shaped((2, 2) + gu),
+        shaped((2, 2) + gu),
+        shaped((2, 2) + wd_own.shape),
     ]
     scratch = [
         pltpu.VMEM((2, 2, 2, rows, 4 * HEAD_DIM), bf16),
         pltpu.VMEM((2, 2, 2, rows, rank_dim), bf16),
         pltpu.VMEM((2, 2, 2, rows, width), bf16),
-        pltpu.SemaphoreType.DMA((6,)),
+        pltpu.VMEM((count, 2 * rows), f32),
     ]
-    operands = (plane_set, wq, wo, cosine, sine, key_index, query_index, first_index, cotangent, gu_own, gu_far, gu_next)
+    scratch += reduce_scratch(rows, width)[1:]
+    scratch += [pltpu.VMEM((rows, width), bf16), pltpu.VMEM(gu, bf16), pltpu.VMEM(gu, bf16), pltpu.SemaphoreType.DMA((2,))]
+    operands = (
+        plane_set, wq, wo, cosine, sine, key_index, query_index, first_index, tokens, gain, cotangent, gu_set, wd_own, wd_far,
+    )
     return moving(
-        attend_kernel, 3, outs, operands, scratch + wires(20, 8),
-        in_specs=[ANY] + [VMEM] * 10 + [ANY],
-        out_specs=[VMEM, VMEM, VMEM, ANY, ANY, ANY, ANY],
-    )
-
-
-def middle_kernel(
-    parts, tokens, gain, gu_own, gu_far, wd_own,
-    middle, plane_mid, gu_out, wd_out,
-    kept, from_c, s1, r1, s2, r2, normed, wd_far, send_sem, recv_sem, local_sem,
-):
-    wire = Wire(send_sem, recv_sem, local_sem)
-    greet(LINKS)
-    first, then, finish = plane_reduce(wire, parts, middle, kept, from_c, s1, r1, s2, r2)
-    wd_sent = wire.send(wd_own, wd_far, 4)
-    gu_done = over_y(wire, gu_own, gu_far, lambda yy, hh: gu_out.at[yy, hh])
-    first()
-    then()
-    finish()
-
-    def norm(r):
-        value = tokens[r].astype(f32) + middle[r]
-        middle[r] = value
-        normed[r] = (value * row_scale(value) * gain[...]).astype(bf16)
-
-    each_rows(normed.shape[0], norm)
-    second = plane_gather(wire, normed, plane_mid, plane_mid.at[0, 0, 0])
-    wd_sent.wait_recv()
-    wd_done = over_y(wire, wd_own, wd_far, lambda yy, hh: wd_out.at[yy, hh])
-    second()()
-    gu_done()
-    wd_done()
-    wire.close()
-
-
-def middle_step(parts, tokens, gain, gu_own, gu_far, wd_own):
-    rows, width = tokens.shape
-    outs = [
-        shaped((rows, width), f32),
-        shaped(parts.shape),
-        shaped((2, 2) + gu_own.shape),
-        shaped((2, 2) + wd_own.shape),
-    ]
-    operands = (parts, tokens, gain, gu_own, gu_far, wd_own)
-    return moving(
-        middle_kernel, 4, outs, operands,
-        reduce_scratch(rows, width) + [pltpu.VMEM((rows, width), bf16), pltpu.VMEM(wd_own.shape, bf16)] + wires(40, 12),
-        in_specs=[ANY, VMEM, VMEM, VMEM, VMEM, VMEM],
-        out_specs=[VMEM, ANY, ANY, ANY],
-    )
-
-
-def feed_kernel(mid, cotangent, gu_one, gu_two, down, hidden, grads, mid_parts, final_parts, gu, wd, sems):
+        attend_kernel, 3, outs, operands, scratch + wires(80, 16),
+        in_specs=[ANY] + [VMEM] * 13,
+        out_specs=[VMEM, VMEM, VMEM, VMEM, ANY, ANY, ANY, ANY, ANY],
+        limit=62,
+    )
+
+
+def feed_kernel(mid, cotangent, gu_zero, gu_one, down, hidden, grads, mid_parts, final_parts, gu, wd, sems):
     main = gu.shape[4] // 2 // 128 * 128
     units = down.shape[2] * 4
     padded = wd.shape[0]
@@ -948,8 +957,8 @@
     @pl.when(pl.program_id(0) == 0)
     def _():
         copies = [
-            pltpu.make_async_copy(gu_one, gu.at[:, 0], sems.at[0]),
-            pltpu.make_async_copy(gu_two, gu.at[:, 1], sems.at[1]),
+            pltpu.make_async_copy(gu_zero, gu.at[:, 0], sems.at[0]),
+            pltpu.make_async_copy(gu_one, gu.at[:, 1], sems.at[1]),
         ]
         size = down.shape[2]
         for k in range(4):
@@ -977,9 +986,9 @@
     mid_parts[...] = lax.dot_general(out, weight, (((1,), (1,)), ((), ())), preferred_element_type=f32).astype(bf16)
 
 
-def feed(mid, cotangent, gu_one, gu_two, down, block=384):
+def feed(mid, cotangent, gu_zero, gu_one, down, block=384):
     tokens, width = mid.shape
-    columns = gu_one.shape[-1]
+    columns = gu_zero.shape[-1]
     units = 4 * down.shape[2]
     padded = (units + 127) // 128 * 128
     by_block = lambda n: pl.BlockSpec((block, n), lambda i: (i, 0))
@@ -990,36 +999,30 @@
         out_specs=[by_block(units), by_block(columns), by_block(width), by_block(width)],
         out_shape=[shaped((tokens, units)), shaped((tokens, columns)), shaped((tokens, width)), shaped((tokens, width))],
         scratch_shapes=[
-            pltpu.VMEM((2, 2, 2) + gu_one.shape[2:], bf16),
+            pltpu.VMEM((2, 2, 2) + gu_zero.shape[2:], bf16),
             pltpu.VMEM((padded, width), bf16),
             pltpu.SemaphoreType.DMA((6,)),
         ],
         compiler_params=pltpu.CompilerParams(vmem_limit_bytes=56 * 1024 * 1024),
         cost_estimate=pl.CostEstimate(flops=12 * tokens * width * units, bytes_accessed=40_000_000, transcendentals=0),
         name="feed",
-    )(mid, cotangent, gu_one, gu_two, down)
-
-
-def fold_y(wire, source, mine, recv, passed, kept):
+    )(mid, cotangent, gu_zero, gu_one, down)
+
+
+def fold_y(wire, source, recv, passed, kept):
     y, x, h, l, c = coordinates()
     sent = [wire.send(source(1 - y, hh), recv.at[hh], 16) for hh in (1 - h, h)]
-    loads = [wire.local(source(y, hh), mine.at[hh]) for hh in (1 - h, h)]
-
-    def finish():
-        for k, hh, target in ((0, 1 - h, passed), (1, h, kept)):
-            loads[k].wait()
-            sent[k].wait_recv()
-
-            def body(r, hh=hh, target=target):
-                target[r] = (wide(mine.at[hh], r) + wide(recv.at[hh], r)).astype(target.dtype)
-
-            each_rows(target.shape[0], body)
-
-    return finish
-
-
-def fold_scratch(rows, width):
-    return [pltpu.VMEM((2, rows, width), bf16), pltpu.VMEM((2, rows, width), bf16)]
+
+    def half(k, hh, target):
+        sent[k].wait_recv()
+        mine = source(y, hh)
+
+        def body(r):
+            target[r] = (wide(mine, r) + wide(recv.at[hh], r)).astype(target.dtype)
+
+        each_rows(target.shape[0], body)
+
+    return lambda: half(0, 1 - h, passed), lambda: half(1, h, kept)
 
 
 def fold_h(wire, passed, kept, recv, out):
@@ -1056,18 +1059,49 @@
     return inner, grad * value * scale
 
 
+def over_tokens(left, right):
+    return lax.dot_general(left, right, (((0,), (0,)), ((), ())), preferred_element_type=f32).astype(bf16)
+
+
 def branch_kernel(
-    parts, middle, cotangent, gain, down_grad, gu_grad,
-    grad_middle, gain_grad, plane_branch, down_out, gu_passed, gu_kept,
-    kept, from_c, s1, r1, s2, r2, normed_grad, branch, wd_mine, wd_recv, wd_passed, wd_kept, wd_far, gu_mine, gu_recv,
-    send_sem, recv_sem, local_sem,
+    parts, middle, cotangent, gain, mid, hidden, gu_grads, cotangents,
+    grad_middle, gain_grad, plane_branch, down_out, gu_passed, gu_kept, gu_one,
+    kept, from_c, s1, r1, s2, r2, normed_grad, branch, wd_grad, wd_recv, wd_passed, wd_kept, wd_far, gu_zero, gu_recv,
+    mid_v, hidden_v, gu_v, cotangents_v, load_sem, send_sem, recv_sem, local_sem,
 ):
     wire = Wire(send_sem, recv_sem, local_sem)
+    loads = [
+        pltpu.make_async_copy(source, target, load_sem.at[k])
+        for k, (source, target) in enumerate(
+            ((hidden, hidden_v), (cotangents, cotangents_v), (gu_grads, gu_v), (mid, mid_v))
+        )
+    ]
     greet(LINKS)
-    first, then, finish = plane_reduce(wire, parts, normed_grad, kept, from_c, s1, r1, s2, r2)
-    down_y = fold_y(wire, lambda yy, hh: down_grad.at[yy, hh], wd_mine, wd_recv, wd_passed, wd_kept)
-    first()
-    then()
+    size = middle.shape[0]
+    give, arrive, steps, finish = plane_reduce(
+        wire, parts, normed_grad, kept, from_c, s1, r1, s2, r2, routes(size, 4, 3)
+    )
+    each(give)
+    for load in loads:
+        load.start()
+    each(arrive)
+    landed(loads[:2])
+    down_rows = wd_grad.shape[2]
+    for k in range(4):
+        wd_grad[k // 2, k % 2] = over_tokens(hidden_v[:, k * down_rows : (k + 1) * down_rows], cotangents_v[...])
+    down_passed, down_kept = fold_y(wire, lambda yy, hh: wd_grad.at[yy, hh], wd_recv, wd_passed, wd_kept)
+    landed(loads[2:])
+    gu_rows = gu_one.shape[2]
+
+    def columns(yy, xx, hh):
+        start = (yy * 4 + xx * 2 + hh) * gu_rows
+        return over_tokens(mid_v[:, start : start + gu_rows], gu_v[...])
+
+    for k in range(4):
+        gu_zero[k // 2, k % 2] = columns(k // 2, 0, k % 2)
+        steps[k]()
+    down_passed()
+    down_h = fold_h(wire, wd_passed, wd_kept, wd_far, down_out)
     gain_grad[...] = jnp.zeros_like(gain_grad)
     finish()
 
@@ -1078,21 +1112,24 @@
         branch[r] = value.astype(bf16)
         gain_grad[...] += jnp.sum(outer, axis=0, keepdims=True)
 
-    each_rows(branch.shape[0], norm)
-    second = plane_gather(wire, branch, plane_branch, plane_branch.at[0, 0, 0])
-    down_y()
-    down_h = fold_h(wire, wd_passed, wd_kept, wd_far, down_out)
-    gu_y = fold_y(wire, lambda yy, hh: gu_grad.at[yy, 0, hh], gu_mine, gu_recv, gu_passed, gu_kept)
-    second()()
-    gu_y()
+    each_rows(size, norm)
+    steps, finish = plane_gather(wire, branch, plane_branch, plane_branch.at[0, 0, 0], routes(size, 4, 2))
+    gu_sums = fold_y(wire, lambda yy, hh: gu_zero.at[yy, hh], gu_recv, gu_passed, gu_kept)
+    for k in range(4):
+        gu_one[k // 2, k % 2] = columns(k // 2, 1, k % 2)
+        steps[k]()
+    down_kept()
+    finish()
+    do(gu_sums)
     down_h()
     wire.close()
 
 
-def branch_step(parts, middle, cotangent, gain, down_grad, gu_grad):
+def branch_step(parts, middle, cotangent, gain, mid, hidden, gu_grads, cotangents):
     rows, width = middle.shape
-    down = down_grad.shape[2:]
-    gu = gu_grad.shape[3:]
+    columns = gu_grads.shape[1]
+    down = (hidden.shape[1] // 4, width)
+    gu = (width // 8, columns)
     outs = [
         shaped((rows, width), f32),
         shaped((1, width), f32),
@@ -1100,23 +1137,26 @@
         shaped(down, f32),
         shaped(gu),
         shaped(gu),
+        shaped((2, 2) + gu),
     ]
     scratch = reduce_scratch(rows, width) + [pltpu.VMEM((rows, width), f32), pltpu.VMEM((rows, width), bf16)]
-    scratch += fold_scratch(*down) + [pltpu.VMEM(down, bf16), pltpu.VMEM(down, bf16), pltpu.VMEM(down, bf16)]
-    scratch += fold_scratch(*gu)
-    operands = (parts, middle, cotangent, gain, down_grad, gu_grad)
+    scratch += [pltpu.VMEM((2, 2) + down, bf16), pltpu.VMEM((2,) + down, bf16)] + [pltpu.VMEM(down, bf16)] * 3
+    scratch += [pltpu.VMEM((2, 2) + gu, bf16), pltpu.VMEM((2,) + gu, bf16)]
+    scratch += [pltpu.VMEM(v.shape, bf16) for v in (mid, hidden, gu_grads, cotangents)]
+    operands = (parts, middle, cotangent, gain, mid, hidden, gu_grads, cotangents)
     return moving(
-        branch_kernel, 5, outs, operands, scratch + wires(40, 16),
-        in_specs=[ANY, VMEM, VMEM, VMEM, ANY, ANY],
-        out_specs=[VMEM, VMEM, ANY, VMEM, VMEM, VMEM],
+        branch_kernel, 4, outs, operands, scratch + [pltpu.SemaphoreType.DMA((4,))] + wires(60, 16),
+        in_specs=[ANY, VMEM, VMEM, VMEM, ANY, ANY, ANY, ANY],
+        out_specs=[VMEM, VMEM, ANY, VMEM, VMEM, VMEM, VMEM],
+        limit=62,
     )
 
 
 def attend_back_kernel(
     plane_set, plane_branch, queries, attended, lse, wq, wo, cosine, sine, key_index, query_index, first_index,
-    final_parts, middle, gu_passed, gu_kept, gu_grad,
+    final_parts, middle, gu_passed, gu_kept, gu_one,
     query_grad, parts, output, gu_out, gu_passed_next, gu_kept_next,
-    kv, branch, staged, grad_keys, grad_values, kept, from_c, s1, r1, s2, r2, total, gu_recv, gu_mine, gu_recv_y,
+    kv, branch, staged, grad_keys, grad_values, kept, from_c, s1, r1, s2, r2, total, gu_recv, gu_recv_y, mask,
     load_sem, send_sem, recv_sem, local_sem,
 ):
     wire = Wire(send_sem, recv_sem, local_sem)
@@ -1131,12 +1171,13 @@
 
     load_branch(0).start()
     greet(LINKS)
-    first, then, finish = plane_reduce(wire, final_parts, total, kept, from_c, s1, r1, s2, r2)
+    give, arrive, passing, finish = plane_reduce(
+        wire, final_parts, total, kept, from_c, s1, r1, s2, r2, routes(middle.shape[0], 4, 3)
+    )
+    each(give)
     gu_h = fold_h(wire, gu_passed, gu_kept, gu_recv, gu_out)
-    gu_y = fold_y(wire, lambda yy, hh: gu_grad.at[yy, 1, hh], gu_mine, gu_recv_y, gu_passed_next, gu_kept_next)
+    gu_sums = fold_y(wire, lambda yy, hh: gu_one.at[yy, hh], gu_recv_y, gu_passed_next, gu_kept_next)
     load_kv.wait()
-    scale = 1.0 / math.sqrt(HEAD_DIM)
-
     def one(k):
         g = k // 2
         i = k % 2
@@ -1163,6 +1204,7 @@
             [kv[g, :, :, :, HEAD_DIM : 2 * HEAD_DIM].reshape(2 * block, HEAD_DIM), kv[g, :, :, :, 3 * HEAD_DIM :].reshape(2 * block, HEAD_DIM)]
         )
         query_parts = []
+        mask[...] = mask_of(key_index[...], first_index[:, place], query_index[:, place])
         for a in range(2):
             span = slice(a * HEAD_DIM, (a + 1) * HEAD_DIM)
             query, grad = queries[place, span], grads[:, span]
@@ -1171,16 +1213,16 @@
                 jnp.ones((8, HEAD_DIM), f32), product, (((1,), (1,)), ((), ())),
                 precision=lax.Precision.HIGHEST, preferred_element_type=f32,
             )[:1]
-            scores, seen = scores_of(keys, query, key_index[...], first_index[:, place], query_index[:, place])
-            probs = jnp.where(seen, jnp.exp(scores - lse[a, :, place]), 0.0)
+            probs = jnp.exp(scores_of(keys, query) + mask[...] - lse[a, :, place])
             grad_values[...] += jnp.dot(probs.astype(bf16), grad, preferred_element_type=f32)
             grad_probs = lax.dot_general(values, grad, (((1,), (1,)), ((), ())), preferred_element_type=f32)
-            grad_scores = (probs * (grad_probs - delta) * scale).astype(bf16)
+            grad_scores = (probs * (grad_probs - delta)).astype(bf16)
             grad_keys[...] += jnp.dot(grad_scores, query, preferred_element_type=f32)
             query_parts.append(
                 lax.dot_general(grad_scores, keys, (((0,), (0,)), ((), ())), preferred_element_type=f32)
             )
-        query_sum = turned(jnp.concatenate(query_parts, axis=1), cosine[place], sine[place], -1.0).astype(bf16)
+        query_sum = turned(jnp.concatenate(query_parts, axis=1), cosine[place], sine[place], -1.0)
+        query_sum = (query_sum * (1.0 / math.sqrt(HEAD_DIM))).astype(bf16)
         query_grad[place] = query_sum
         normed = lax.dot_general(query_sum, wq[...], (((1,), (1,)), ((), ())), preferred_element_type=f32)
         staged[g, i, :, :, :rank_dim] = normed.astype(bf16).reshape(2, rows, rank_dim)
@@ -1200,10 +1242,13 @@
         def _(k):
             one(k)
 
+    each(arrive)
     steps(0, 1)
-    first()
-    steps(1, 3)
-    then()
+    do(passing[:1])
+    steps(1, 2)
+    do(passing[1:3])
+    steps(2, 3)
+    do(passing[3:])
     gu_h()
     steps(3, 4)
     finish()
@@ -1214,13 +1259,13 @@
     each_rows(output.shape[0], emit)
     for g in range(2):
         pltpu.make_async_copy(staged.at[g], parts.at[g], load_sem.at[3 + g]).wait()
-    gu_y()
+    do(gu_sums)
     wire.close()
 
 
 def attend_back(
     plane_set, plane_branch, queries, attended, lse, wq, wo, cosine, sine, key_index, query_index, first_index,
-    final_parts, middle, gu_passed, gu_kept, gu_grad,
+    final_parts, middle, gu_passed, gu_kept, gu_one,
 ):
     rows, width = middle.shape
     tokens = 8 * rows
@@ -1241,14 +1286,14 @@
         pltpu.VMEM((8 * rows, HEAD_DIM), f32),
     ]
     scratch += reduce_scratch(rows, width) + [pltpu.VMEM((rows, width), f32), pltpu.VMEM(gu, bf16)]
-    scratch += fold_scratch(*gu) + [pltpu.SemaphoreType.DMA((5,))]
+    scratch += [pltpu.VMEM((2,) + gu, bf16), pltpu.VMEM((tokens, 2 * rows), f32), pltpu.SemaphoreType.DMA((5,))]
     operands = (
         plane_set, plane_branch, queries, attended, lse, wq, wo, cosine, sine, key_index, query_index, first_index,
-        final_parts, middle, gu_passed, gu_kept, gu_grad,
+        final_parts, middle, gu_passed, gu_kept, gu_one,
     )
     return moving(
-        attend_back_kernel, 6, outs, operands, scratch + wires(30, 12),
-        in_specs=[ANY, ANY] + [VMEM] * 10 + [ANY, VMEM, ANY, VMEM, ANY],
+        attend_back_kernel, 5, outs, operands, scratch + wires(60, 12),
+        in_specs=[ANY, ANY] + [VMEM] * 10 + [ANY, VMEM, ANY, VMEM, VMEM],
         out_specs=[VMEM, ANY, VMEM, VMEM, VMEM, VMEM],
         limit=62,
     )
@@ -1260,8 +1305,8 @@
     grad_tokens, down_out, key_out, value_out, gains_out, gate_out, up_out, q_up_out, out_out,
     kept, from_c, s1, r1, s2, r2, back, kv_send, kv_recv, weight, mixed, normed_grad, gain_rows,
     blocks, acc, recv, core, gains, gains_recv,
-    gu_far, gu_own, gu_back, gu_wide, up_mine, up_recv, up_passed, up_kept, up_far, up_own, up_back,
-    heads, o_mine, o_recv, o_passed, o_kept, o_far,
+    gu_far, gu_own, gu_back, gu_wide, up_recv, up_passed, up_kept, up_far, up_own, up_back,
+    heads, o_recv, o_passed, o_kept, o_far,
     send_sem, recv_sem, local_sem,
 ):
     y, x, h, l, c = coordinates()
@@ -1270,25 +1315,34 @@
     wire = Wire(send_sem, recv_sem, local_sem)
     load = wire.local(first_weight, weight)
     greet([16, 4] + PLANE)
-    first, then, finish = plane_reduce(wire, parts, back, kept, from_c, s1, r1, s2, r2)
+    rows = back.shape[0]
+    rank_dim = compressed.shape[1]
+    split = rank_dim + 2 * HEAD_DIM
+    buffers = (parts, back, kept, from_c, s1, r1, s2, r2)
+    of = lambda columns: [ref.at[(every,) * (len(ref.shape) - 1) + (columns,)] for ref in buffers]
+    far_columns = pl.ds(split, back.shape[1] - split)
+    far_give, far_arrive, far_steps, far_finish = plane_reduce(wire, *of(far_columns), routes(rows, 2, 1))
+    give, arrive, steps, finish = plane_reduce(wire, *of(pl.ds(0, split)), routes(rows, 4, 3))
+    each(far_give)
+    each(give)
+    each(far_arrive)
     gu_h = fold_h(wire, gu_passed, gu_kept, gu_far, gu_own)
     swapped = wire.send(out_grad.at[:, 1 - c], heads.at[:, c], 1)
     stayed = wire.local(out_grad.at[:, c], heads.at[:, c])
-    first()
+    each(arrive)
     stayed.wait()
     swapped.wait_recv()
-    o_y = fold_y(wire, lambda yy, hh: heads.at[yy, hh], o_mine, o_recv, o_passed, o_kept)
-    up_y = [
-        fold_y(wire, lambda yy, hh, k=k: up_grad.at[yy, k, hh], up_mine.at[k], up_recv.at[k], up_passed.at[k], up_kept.at[k])
+    o_sums = fold_y(wire, lambda yy, hh: heads.at[yy, hh], o_recv, o_passed, o_kept)
+    up_sums = [
+        fold_y(wire, lambda yy, hh, k=k: up_grad.at[yy, k, hh], up_recv.at[k], up_passed.at[k], up_kept.at[k])
         for k in range(2)
     ]
-    then()
-    finish()
-    rows = back.shape[0]
-    rank_dim = compressed.shape[1]
-    split = rank_dim + 2 * HEAD_DIM
+    do(far_steps)
+    far_finish()
     kv_send[...] = back[:, split:].astype(bf16)
     far = wire.send(kv_send, kv_recv, 4)
+    do(steps)
+    finish()
     inner, outer = norm_back(compressed[...], gain_q[...], back[:, :rank_dim])
     mixed[:, :rank_dim] = inner.astype(bf16)
     gain_rows[1:2, :rank_dim] = jnp.sum(outer, axis=0, keepdims=True)
@@ -1313,16 +1367,15 @@
         )
         blocks[at] = grad.astype(bf16).reshape(blocks.shape[3:])
         cores.append(wire.send(blocks.at[at + (every, 1 - c)], core.at[at], 1))
-    o_y()
+    do(o_sums)
     o_h = fold_h(wire, o_passed, o_kept, o_far, out_out)
     for k in range(2):
-        up_y[k]()
+        do(up_sums[k])
     up_h = [fold_h(wire, up_passed.at[k], up_kept.at[k], up_far.at[k], up_own.at[k]) for k in range(2)]
     span = blocks.shape[5]
     width = blocks.shape[6]
-    third = width // 3
-    columns = [pl.ds(i * third, third) for i in range(3)]
-    orders = ["yxlh", "lyxh", "xlyh"]
+    columns = thirds(width)
+    orders = ["yxlh", "xylh", "lyxh"]
     sent = [None] * 3
 
     def index(fixed, block):
@@ -1333,12 +1386,9 @@
         return tuple(at[k] for k in "yxhl")
 
     def over(fixed, body):
-        count = 2 ** (4 - len(fixed))
-
-        @pl.loop(0, count * (span // 16))
+        @pl.loop(0, 2 ** (4 - len(fixed)))
         def _(i):
-            r = pl.ds(pl.multiple_of((i % (span // 16)) * 16, 16), 16)
-            body(index(fixed, i // (span // 16)), r)
+            body(index(fixed, i))
 
     def pass_on(p, step):
         order = orders[p]
@@ -1355,9 +1405,9 @@
         for p in range(3):
             bit = orders[p][0]
 
-            def body(at, r, p=p):
-                value = wide(blocks, at + (c, r, columns[p])) + wide(core, at + (r, columns[p]))
-                acc[at + (r, columns[p])] = value.astype(bf16)
+            def body(at, p=p):
+                value = wide(blocks, at + (c, every, columns[p])) + wide(core, at + (every, columns[p]))
+                acc[at + (every, columns[p])] = value.astype(bf16)
 
             over({bit: 1 - own[bit] if first_side else own[bit]}, body)
             if first_side:
@@ -1405,13 +1455,13 @@
             bit = order[step]
             sent[p].wait_recv()
 
-            def body(at, r, p=p, bit=bit, last=step == 3):
+            def body(at, p=p, bit=bit, last=step == 3):
                 other = tuple(1 - own[k] if k == bit else v for k, v in zip("yxhl", at))
-                value = wide(acc, at + (r, columns[p])) + wide(recv, other + (r, columns[p]))
+                value = wide(acc, at + (every, columns[p])) + wide(recv, other + (every, columns[p]))
                 if last:
-                    back[r, columns[p]] = value
+                    back[:span, columns[p]] = value
                 else:
-                    acc[at + (r, columns[p])] = value.astype(bf16)
+                    acc[at + (every, columns[p])] = value.astype(bf16)
 
             if step < 3:
                 over({**fixed, bit: own[bit], order[step + 1]: 1 - own[order[step + 1]]}, body)
@@ -1511,14 +1561,12 @@
         pltpu.VMEM((1, 8, span, gu[1]), bf16),
         pltpu.VMEM((2,) + gu, bf16),
         pltpu.VMEM((2, 2) + up, bf16),
-        pltpu.VMEM((2, 2) + up, bf16),
         pltpu.VMEM((2,) + up, bf16),
         pltpu.VMEM((2,) + up, bf16),
         pltpu.VMEM((2,) + up, bf16),
         pltpu.VMEM((2,) + up, bf16),
         pltpu.VMEM((8, up[0] // 4, up[1]), bf16),
         pltpu.VMEM((2, 2) + heads, bf16),
-        pltpu.VMEM((2,) + heads, bf16),
         pltpu.VMEM((2,) + heads, bf16),
         pltpu.VMEM(heads, bf16),
         pltpu.VMEM(heads, bf16),
@@ -1529,8 +1577,8 @@
         gu_total, gu_passed, gu_kept, up_grad, out_grad,
     )
     return moving(
-        tail_kernel, 7, outs, operands, scratch + wires(80, 24),
-        in_specs=[ANY] + [VMEM] * 4 + [ANY] + [VMEM] * 5 + [ANY, ANY, VMEM, ANY, ANY],
+        tail_kernel, 6, outs, operands, scratch + wires(100, 24),
+        in_specs=[ANY] + [VMEM] * 4 + [ANY] + [VMEM] * 5 + [ANY, ANY, VMEM, VMEM, ANY],
         out_specs=[VMEM] * 9,
         limit=62,
     )
@@ -1567,55 +1615,42 @@
 
     gains = jnp.concatenate([norm_in_gain, norm_mid_gain, q_gain, jnp.zeros((256 - 2 * span - q_span,), f32)])
     gains = lax.reduce_precision(gains, 8, 7).reshape(1, 256)
-    first_weight, up_query, gu_set, wo_own, wo_far, wd_own, gains, places = head(
+    first_weight, up_query, gu_pieces, wo_own, wo_far, wd_own, in_gain, mid_gain, query_gain, places = head(
         q_down, key_proj, value_proj, gains, q_up, w_gate, w_up, out_proj, w_down, positions.reshape(1, rows)
     )
     first_weight = first_weight.reshape(width, rank_dim + 2 * HEAD_DIM)
     up_query = up_query.reshape(rank_dim, 2 * HEAD_DIM)
-    gains = gains.reshape(32, 256)
-    in_gain = gains[:, :span].reshape(1, width)
-    mid_gain = gains[:, span : 2 * span].reshape(1, width)
-    query_gain = gains[:, 2 * span : 2 * span + q_span].reshape(1, rank_dim)
 
     blocks = jnp.arange(4, dtype=jnp.int32) ^ (l * 2 + c)
     in_half = (blocks[:, None] * rows + jnp.arange(rows, dtype=jnp.int32)[None, :]).reshape(-1)
     own_index = h * (4 * rows) + in_half
     query_index = jnp.concatenate([own_index, own_index]).reshape(1, 8 * rows)
-    places = places.reshape(1, 8 * rows)
     first_index = query_index - places
     key_index = jnp.concatenate([own_index, (1 - h) * (4 * rows) + in_half]).reshape(8 * rows, 1)
     cosine, sine = rope_table(places.reshape(-1))
 
-    plane_set, out_weight, gu_far, normed, compressed = pack(
-        tokens, in_gain, query_gain, first_weight, cosine[:rows], sine[:rows], wo_own, wo_far, gu_set[0]
+    plane_set, out_weight, gu_set, wd_far, normed, compressed = pack(
+        tokens, in_gain, query_gain, first_weight, cosine[:rows], sine[:rows], wo_own, wo_far, gu_pieces, wd_own
     )
     out_weight = out_weight.reshape(2 * HEAD_DIM, width)
-    queries, attended, lse, out_parts, plane_cotangent, gu_one, gu_far = attend(
-        plane_set, up_query, out_weight, cosine, sine, key_index, query_index, first_index, cotangent,
-        gu_set[0], gu_far, gu_set[1],
-    )
-    middle, plane_mid, gu_two, down_weight = middle_step(out_parts, tokens, mid_gain, gu_set[1], gu_far, wd_own)
+    queries, attended, lse, middle, plane_mid, plane_cotangent, gu_zero, gu_one, down_weight = attend(
+        plane_set, up_query, out_weight, cosine, sine, key_index, query_index, first_index, tokens, mid_gain, cotangent,
+        gu_set, wd_own, wd_far,
+    )
     plane_mid = plane_mid.reshape(8 * rows, width)
     plane_cotangent = plane_cotangent.reshape(8 * rows, width)
-    hidden, gu_grads, mid_parts, final_parts = feed(plane_mid, plane_cotangent, gu_one, gu_two, down_weight)
-
-    def over_tokens(left, right):
-        grad = lax.dot_general(left, right, (((0,), (0,)), ((), ())), preferred_element_type=f32)
-        return grad.astype(bf16)
-
-    by_rows = lambda grad: grad.reshape(2, 2, 2, -1, grad.shape[-1])
+    hidden, gu_grads, mid_parts, final_parts = feed(plane_mid, plane_cotangent, gu_zero, gu_one, down_weight)
+
     by_plane = lambda parts: parts.reshape(2, 2, 2, rows, -1)
-    down_grad = over_tokens(hidden, plane_cotangent).reshape(2, 2, -1, width)
-    gu_grad = by_rows(over_tokens(plane_mid, gu_grads))
-    grad_middle, mid_gain_grad, plane_branch, grad_down, gu_passed, gu_kept = branch_step(
-        by_plane(mid_parts), middle, cotangent, mid_gain, down_grad, gu_grad
+    grad_middle, mid_gain_grad, plane_branch, grad_down, gu_passed, gu_kept, gu_one_grad = branch_step(
+        by_plane(mid_parts), middle, cotangent, mid_gain, plane_mid, hidden, gu_grads, plane_cotangent
     )
     query_grad, back_parts, output, gu_total, gu_passed, gu_kept = attend_back(
         plane_set, plane_branch, queries, attended, lse, up_query, out_weight, cosine, sine,
-        key_index, query_index, first_index, by_plane(final_parts), middle, gu_passed, gu_kept, gu_grad,
+        key_index, query_index, first_index, by_plane(final_parts), middle, gu_passed, gu_kept, gu_one_grad,
     )
     out_grad = over_tokens(attended, plane_branch.reshape(8 * rows, width)).reshape(2, 2, -1, width)
-    up_grad = by_rows(over_tokens(plane_set.reshape(8 * rows, -1)[:, :rank_dim], query_grad))
+    up_grad = over_tokens(plane_set.reshape(8 * rows, -1)[:, :rank_dim], query_grad).reshape(2, 2, 2, -1, 2 * HEAD_DIM)
     grad_tokens, grad_q_down, grad_key, grad_value, grad_gains, grad_gate, grad_up, grad_q_up, grad_out = tail(
         back_parts, normed, compressed, tokens, grad_middle, first_weight, in_gain, query_gain, mid_gain_grad,
         cosine[:rows], sine[:rows], gu_total, gu_passed, gu_kept, up_grad, out_grad,

time: 670 us -> 586 us (0.87)
  Pallas kernels: 601 us -> 546 us
  matrix products: 33.7 us -> 12.2 us
    pallas_call x7 -> x6, Pallas kernels: 563 us -> 509 us  [moving(): pl.pallas_call(kernel, out_shape=outs, in_specs=in_specs or [ANY] * len(o...]
    dot_general x4 -> x2, matrix products: 33.7 us -> 12.2 us  [over_tokens(): lax.dot_general(left, right, (((0,), (0,)), ((), ())), preferred_element_...]
where the time goes in v3:
time: 586 us; the launch traced here: 581 us
  Pallas kernels  546 us (93%)
  local copies, waits for them, and re-layouts  15.6 us (3%)
  matrix products  12.2 us (2%)
  other arithmetic  6.21 us (1%)
    pallas_call x6, Pallas kernels, moving(): pl.pallas_call(kernel, out_shape=outs, in_specs=in_specs or [ANY] * len(o...  509 us
    pallas_call x1, Pallas kernels, feed(): pl.pallas_call(feed_kernel, grid=(tokens // block,), in_specs=[by_block(w...  37.1 us
    dot_general x2, matrix products, over_tokens(): lax.dot_general(left, right, (((0,), (0,)), ((), ())), preferred_element_...  12.2 us

profile of v3, /device:TPU:0, one launch (start us, length us, event | category | flops | bytes accessed | tf_op | source)
XLA Modules:
  0.0 580.8 jit_solution(15655359904407342485)
XLA Ops:
  0.7 0.1 pad.7.clone
  0.8 1.3 maximum_reduce-precision_fusion.gains
  2.1 0.1 fusion.5
  2.2 0.1 add.56
  2.3 0.1 add.53
  2.4 0.6 reshape.152.query_index
  3.0 1.1 reshape.161.key_index
  4.1 65.4 %head_kernel.1 = (bf16[2,2,2,2,2,64,1536]{6,5,4,3,2,1,0:T(8,128)(2,1)}, bf16[2,2,2,128,512]{4,3,2,1,0:T(8,128)(2,1)}, bf16[8,64,1408]{2,1,0:T(8,128)(2,1)}, bf16...) custom-call(f32[64,1024]{1,0:T(8,128)} %q_down.1, ...), custom_call_target="tpu_custom_call" | custom-call | bytes 100000000 | tf_op jit(solution)/shard_map/head_kernel/pallas_call | solution.py:422
  69.5 1.3 reshape_subtract_fusion.first_index
  70.8 0.7 convert_reduce_fusion
  71.5 2.8 multiply_sine_fusion
  74.3 0.0 copy-start
  74.3 0.0 copy-start.1
  74.3 0.7 slice.27.sine
  75.1 0.6 slice.26.cosine
  75.7 69.3 %pack_kernel.1 = (bf16[2,2,2,192,2048]{4,3,2,1,0:T(8,128)(2,1)}, bf16[2,2,128,2048]{3,2,1,0:T(8,128)(2,1)}, bf16[2,256,1408]{2,1,0:T(8,128)(2,1)}, bf16[176,2048...) custom-call(bf16[192,2048]{1,0:T(8,128)(2,1)} %tokens.5, f32[1,2048]{1,0:T(1,128)} %get-tuple-element.64.gain_in, ...), custom_call_target="tpu_custom_call" | custom-call | bytes 100000000 | tf_op jit(solution)/shard_map/pack_kernel/pallas_call | solution.py:422
  145.0 0.0 copy-done
  145.0 0.0 copy-done.1
  145.0 114.2 %attend_kernel.1 = (bf16[1536,512]{1,0:T(8,128)(2,1)}, bf16[1536,512]{1,0:T(8,128)(2,1)}, f32[2,1,1536]{2,1,0:T(1,128)}, f32[192,2048]{1,0:T(8,128)}, bf16[2,2,2...) custom-call(bf16[2,2,2,192,2048]{4,3,2,1,0:T(8,128)(2,1)} %get-tuple, ...), custom_call_target="tpu_custom_call" | custom-call | bytes 100000000 | tf_op jit(solution)/shard_map/attend_kernel/pallas_call | solution.py:422
  259.3 37.1 %feed.1 = (bf16[1536,704]{1,0:T(8,128)(2,1)}, bf16[1536,1408]{1,0:T(8,128)(2,1)}, bf16[1536,2048]{1,0:T(8,128)(2,1)}, bf16[1536,2048]{1,0:T(8,128)(2,1)}) custom-call(bf16[1536,2048]{1,0:T(8,128)(2,1)} %bitcast.32, bf16[1536,2048]{1,0:T(8,128)(2,1)} %bitcast.34, bf16[2,2,256,1408]{3,2,1,0:T(8,128)(2,1)} %get-tuple-element.80.gu_zero, ...), custom_call_target="tpu_custom_call" | custom-call | flops 26575110144 | bytes 40000000 | tf_op jit(solution)/shard_map/feed/pallas_call | solution.py:995
  296.4 87.9 %branch_kernel.1 = (f32[192,2048]{1,0:T(8,128)}, f32[1,2048]{1,0:T(1,128)}, bf16[2,2,2,192,2048]{4,3,2,1,0:T(8,128)(2,1)}, f32[176,2048]{1,0:T(8,128)}, bf16[256...) custom-call(bf16[2,2,2,192,2048]{4,3,2,1,0:T(8,128)(2,1)} %bitcast.36, ...), custom_call_target="tpu_custom_call" | custom-call | bytes 100000000 | tf_op jit(solution)/shard_map/branch_kernel/pallas_call | solution.py:422
  384.3 0.0 copy-start.2
  384.3 53.8 %attend_back_kernel.1 = (bf16[1536,512]{1,0:T(8,128)(2,1)}, bf16[2,2,2,192,2048]{4,3,2,1,0:T(8,128)(2,1)}, bf16[192,2048]{1,0:T(8,128)(2,1)}, bf16[256,1408]{1,0...) custom-call(bf16[2,2,2,192,2048]{4,3,2,1,0:T(8,128)(2,1)} %get-tuple-element.72.plane_set, ...), custom_call_target="tpu_custom_call" | custom-call | bytes 100000000 | tf_op jit(solution)/shard_map/attend_back_kernel/pallas_call | solution.py:422
  438.1 0.0 copy-done.2
  438.1 0.0 copy-start.13
  438.1 7.6 %convolution_convert_fusion = bf16[512,2048]{1,0:T(8,128)(2,1)} fusion(bf16[1536,512]{1,0:T(8,128)(2,1)S(1)} %copy-done.2, bf16[1536,2048]{1,0:T(8,128)(2,1)} %bitcast.31), kind=kOutput, calls=%fused_computation.2 | convolution fusion | flops 3222274048 | bytes 9961472 | tf_op jit(solution)/shard_map/dot_general | solution.py:1063
  445.7 0.0 copy-done.13
  445.7 4.7 fusion.2
  450.3 0.0 copy-start.7
  450.3 118.0 %tail_kernel.1 = (bf16[192,2048]{1,0:T(8,128)(2,1)}, f32[64,1024]{1,0:T(8,128)}, f32[64,256]{1,0:T(8,128)}, f32[64,256]{1,0:T(8,128)}, f32[1,256]{1,0:T(1,128)},...) custom-call(bf16[2,2,2,192,2048]{4,3,2,1,0:T(8,128)(2,1)} %get-tuple-element.96.parts, ...), custom_call_target="tpu_custom_call" | custom-call | bytes 100000000 | tf_op jit(solution)/shard_map/tail_kernel/pallas_call | solution.py:422
  568.4 0.0 copy-start.8
  568.4 0.0 copy-start.10
  568.4 0.0 copy-start.9
  568.4 1.2 slice_bitcast_fusion.1
  569.6 1.3 slice_bitcast_fusion
  571.0 0.0 copy-done.7
  571.0 0.0 copy-start.12
  571.0 0.0 copy-start.11
  571.0 0.0 copy-start.6
  571.0 0.9 copy.39
  571.9 0.0 copy-done.8
  571.9 0.9 copy.40
  572.8 0.0 copy-done.10
  572.8 0.0 copy-start.5
  572.8 0.7 copy.41
  573.5 0.0 copy-done.9
  573.5 0.8 copy.42
  574.3 0.0 copy-done.12
  574.3 0.6 copy.43
  574.9 0.0 copy-done.11
  574.9 0.6 copy.44
  575.5 0.0 copy-done.6
  575.5 0.0 copy-start.4
  575.5 1.0 copy.45
  576.5 0.0 copy-done.5
  576.5 1.1 copy.46
  577.6 0.0 copy-done.4
  577.6 0.0 copy-start.3
  577.6 1.1 copy.47
  578.7 0.8 copy-done.3
  579.5 1.1 copy.48
  (4 shorter events, 0.0 us)
Async XLA Ops:
  74.3 70.7 %copy-start = (f32[1536,128]{1,0:T(8,128)}, f32[1536,128]{1,0:T(8,128)S(1)}, u32[]{:S(2)}) copy-start(f32[1536,128]{1,0:T(8,128)S(1)} %get-tuple-element.115.sine) | copy-start | bytes 2359300
  74.3 70.7 %copy-start.1 = (f32[1536,128]{1,0:T(8,128)}, f32[1536,128]{1,0:T(8,128)S(1)}, u32[]{:S(2)}) copy-start(f32[1536,128]{1,0:T(8,128)S(1)} %get-tuple-element.116.cosine) | copy-start | bytes 2359300
  384.3 53.8 %copy-start.2 = (bf16[1536,512]{1,0:T(8,128)(2,1)S(1)}, bf16[1536,512]{1,0:T(8,128)(2,1)}, u32[]{:S(2)}) copy-start(bf16[1536,512]{1,0:T(8,128)(2,1)} %get-tuple-element.89.attended) | copy-start | bytes 4718596
  438.1 7.6 %copy-start.13 = (bf16[1536,512]{1,0:T(8,128)(2,1)S(1)}, bf16[1536,512]{1,0:T(8,128)(2,1)}, u32[]{:S(2)}) copy-start(bf16[1536,512]{1,0:T(8,128)(2,1)} %get-tuple-element.104) | copy-start | bytes 4718596
  450.3 120.6 %copy-start.7 = (bf16[192,2048]{1,0:T(8,128)(2,1)S(1)}, bf16[192,2048]{1,0:T(8,128)(2,1)}, u32[]{:S(2)}) copy-start(bf16[192,2048]{1,0:T(8,128)(2,1)} %get-tuple-element.136) | copy-start | bytes 2359300
  568.4 3.5 copy-start.8
  568.4 4.4 copy-start.10
  568.4 5.1 copy-start.9
  571.0 3.3 copy-start.12
  571.0 3.9 copy-start.11
  571.0 4.5 copy-start.6
  572.8 3.7 copy-start.5
  575.5 2.1 copy-start.4
  577.6 1.9 copy-start.3

commit v4 on v3

--- a/solution.py
+++ b/solution.py
@@ -377,9 +377,15 @@
     def __init__(self, send_sem, recv_sem, local_sem):
         self.send_sem, self.recv_sem, self.local_sem = send_sem, recv_sem, local_sem
         self.copies = []
+        self.gone = []
         self.locals = 0
 
     def send(self, src, dst, mask):
+        copy = self.later(src, dst, mask)
+        copy.start()
+        return copy
+
+    def later(self, src, dst, mask):
         k = len(self.copies)
         copy = pltpu.make_async_remote_copy(
             src_ref=src,
@@ -389,19 +395,28 @@
             device_id=partner(mask),
             device_id_type=pl.DeviceIdType.MESH,
         )
-        copy.start()
         self.copies.append(copy)
         return copy
 
     def local(self, src, dst):
+        copy = self.later_local(src, dst)
+        copy.start()
+        return copy
+
+    def later_local(self, src, dst):
         copy = pltpu.make_async_copy(src, dst, self.local_sem.at[self.locals])
         self.locals += 1
-        copy.start()
         return copy
+
+    def left(self, copies):
+        for copy in copies:
+            copy.wait_send()
+        self.gone += copies
 
     def close(self):
         for copy in self.copies:
-            copy.wait_send()
+            if not any(copy is other for other in self.gone):
+                copy.wait_send()
 
 
 def wires(remote, local):
@@ -598,8 +613,8 @@
 
 def head_kernel(
     q_down, key, value, gains, q_up, gate, up, out_proj, w_down, places,
-    first_out, upq_out, gu, wo_out, wo_far, wd_out, in_gain, mid_gain, q_gain, place_row,
-    first, upq, staged, gains_out, places_out, send_sem, recv_sem, local_sem,
+    first_out, upq_out, gu, wo_out, wo_far, wd_out, in_gain, mid_gain, q_gain, first_index, query_index, key_index,
+    cosine, sine, first, upq, staged, gains_out, places_out, send_sem, recv_sem, local_sem,
 ):
     y, x, h, l, c = coordinates()
     rank = x * 4 + l * 2 + c
@@ -686,8 +701,25 @@
     place_mine.wait()
     arrived(place)
     rows = places.shape[1]
-    first_rows = jnp.concatenate([places_out[j] for j in range(8)], axis=1)
-    place_row[...] = first_rows
+    half = HEAD_DIM // 2
+    powers = lax.broadcasted_iota(jnp.int32, (rows, half), 1).astype(f32)
+    freqs = jnp.exp(powers * (-2.0 / HEAD_DIM * math.log(rope_base)))
+    eye = lax.broadcasted_iota(jnp.int32, (rows, rows), 0) == lax.broadcasted_iota(jnp.int32, (rows, rows), 1)
+    index = []
+    for j in range(8):
+        place = jnp.sum(jnp.where(eye, places_out[j].astype(f32), 0.0), axis=1, keepdims=True)
+        angles = place * freqs
+        cosine[j * rows : (j + 1) * rows] = jnp.cos(angles)
+        sine[j * rows : (j + 1) * rows] = jnp.sin(angles)
+        b, d = j // 2 % 2, j % 2
+        block = (l + b - 2 * l * b) * 2 + (c + d - 2 * c * d)
+        start = (h * 4 + block) * rows
+        index.append(start + lax.broadcasted_iota(jnp.int32, (1, rows), 1))
+        side = h if j < 4 else 1 - h
+        key_index[j * rows : (j + 1) * rows] = (side * 4 + block) * rows + lax.broadcasted_iota(jnp.int32, (rows, 1), 0)
+    index = jnp.concatenate(index, axis=1)
+    query_index[...] = index
+    first_index[...] = index - jnp.concatenate([places_out[j] for j in range(8)], axis=1)
     gain.wait_recv()
     span, q_span = in_gain.shape[1] // 32, q_gain.shape[1] // 32
     for n in range(32):
@@ -701,6 +733,7 @@
 
 def head(q_down, key, value, gains, q_up, gate, up, out_proj, w_down, places):
     rows = q_down.shape[0]
+    count = 8 * places.shape[1]
     width = q_down.shape[1] + 2 * key.shape[1]
     columns = gate.shape[1] // 4
     slice_size = gate.shape[1] // 8
@@ -714,7 +747,11 @@
         shaped((1, 32 * rows), f32),
         shaped((1, 32 * rows), f32),
         shaped((1, q_down.shape[1]), f32),
-        shaped((1, 8 * places.shape[1]), jnp.int32),
+        shaped((1, count), jnp.int32),
+        shaped((1, count), jnp.int32),
+        shaped((count, 1), jnp.int32),
+        shaped((count, HEAD_DIM // 2), f32),
+        shaped((count, HEAD_DIM // 2), f32),
     ]
     scratch = [
         pltpu.VMEM((rows, width), bf16),
@@ -727,7 +764,7 @@
     return moving(
         head_kernel, 1, outs, operands, scratch + wires(100, 8),
         in_specs=[VMEM] * len(operands),
-        out_specs=[ANY, ANY, VMEM, VMEM, ANY, VMEM, VMEM, VMEM, VMEM, VMEM],
+        out_specs=[ANY, ANY, VMEM, VMEM, ANY] + [VMEM] * 9,
     )
 
 
@@ -759,6 +796,7 @@
     gu_mine = wire.local(gu.at[rank], gu_place)
     gu_sent = [wire.send(gu.at[flip(rank, j)], gu_place, PLANE[j - 1]) for j in range(1, 8)]
     weight_done = [over_y(wire, ref, lambda yy, hh: weight_all.at[yy, hh], k) for k, ref in enumerate((wo_own, wo_far))]
+    rows = tokens.shape[0]
     inputs = tokens[...].astype(f32)
     normed[...] = (inputs * row_scale(inputs) * gain_in[...]).astype(bf16)
     load.wait()
@@ -768,18 +806,18 @@
     compressed[...] = query
     block[:, :rank_dim] = (query * row_scale(query) * gain_q[...]).astype(bf16)
     block[:, rank_dim : rank_dim + HEAD_DIM] = turned(
-        mixed[:, rank_dim : rank_dim + HEAD_DIM], cosine[...], sine[...], 1.0
+        mixed[:, rank_dim : rank_dim + HEAD_DIM], cosine[:rows], sine[:rows], 1.0
     ).astype(bf16)
     block[:, rank_dim + HEAD_DIM :] = mixed[:, rank_dim + HEAD_DIM :].astype(bf16)
     near = block.shape[1]
     far = 2 * HEAD_DIM
     columns, far_columns = pl.ds(0, near), pl.ds(near, far)
     from_h = wire.send(block.at[:, pl.ds(near - far, far)], out.at[0, 0, 0, :, far_columns], 4)
-    wd_sent = wire.send(wd_own, wd_far, 4)
     near_out = out.at[:, :, :, :, columns]
     size = block.shape[0]
     steps, finish = plane_gather(wire, block, near_out, near_out.at[0, 0, 0], routes(size, 4, 1))
     from_h.wait_recv()
+    wd_sent = wire.send(wd_own, wd_far, 4)
     far_out = out.at[:, :, :, :, far_columns]
     far_steps, far_finish = plane_gather(wire, far_out.at[0, 0, 0], far_out, None, routes(size, 2, 1))
     do(steps)
@@ -948,65 +986,116 @@
     )
 
 
-def feed_kernel(mid, cotangent, gu_zero, gu_one, down, hidden, grads, mid_parts, final_parts, gu, wd, sems):
+def feed_kernel(
+    mid, cotangents, gu_zero, gu_one, down,
+    hidden, grads, final_parts, normed_grad,
+    gu, wd, mid_v, cot_v, hid_v, grads_v, final_v, staged, from_c, s1, r1, s2, r2,
+    weight_sem, load_sem, store_sem, send_sem, recv_sem, local_sem,
+):
+    wire = Wire(send_sem, recv_sem, local_sem)
     main = gu.shape[4] // 2 // 128 * 128
-    units = down.shape[2] * 4
-    padded = wd.shape[0]
-    columns = gu.shape[4]
-
-    @pl.when(pl.program_id(0) == 0)
-    def _():
-        copies = [
-            pltpu.make_async_copy(gu_zero, gu.at[:, 0], sems.at[0]),
-            pltpu.make_async_copy(gu_one, gu.at[:, 1], sems.at[1]),
+    size = down.shape[2]
+    units = 4 * size
+    rows = staged.shape[3]
+    block = 2 * rows
+    copies = [
+        pltpu.make_async_copy(gu_zero, gu.at[:, 0], weight_sem.at[0]),
+        pltpu.make_async_copy(gu_one, gu.at[:, 1], weight_sem.at[1]),
+    ]
+    for k in range(4):
+        copies.append(pltpu.make_async_copy(down.at[k // 2, k % 2], wd.at[pl.ds(k * size, size)], weight_sem.at[2 + k]))
+    for copy in copies:
+        copy.start()
+
+    def load(n):
+        k = ARRIVAL[n]
+        pairs = [(mid.at[k[0], k[1]], mid_v.at[n % 2]), (cotangents.at[k[0], k[1]], cot_v.at[n % 2])]
+        moves = [pltpu.make_async_copy(src, dst, load_sem.at[2 * (n % 2) + q]) for q, (src, dst) in enumerate(pairs)]
+        for move in moves:
+            move.start()
+        return moves
+
+    def store(n):
+        k = ARRIVAL[n]
+        place = pl.ds((k[0] * 2 + k[1]) * block, block)
+        pairs = [(hid_v, hidden.at[place]), (grads_v, grads.at[place]), (final_v, final_parts.at[place])]
+        moves = [
+            pltpu.make_async_copy(src.at[n % 2], dst, store_sem.at[3 * (n % 2) + q]) for q, (src, dst) in enumerate(pairs)
         ]
-        size = down.shape[2]
-        for k in range(4):
-            copies.append(pltpu.make_async_copy(down.at[k // 2, k % 2], wd.at[pl.ds(k * size, size)], sems.at[2 + k]))
-        for copy in copies:
-            copy.start()
-        wd[units:] = jnp.zeros((padded - units, wd.shape[1]), bf16)
-        landed(copies)
-
-    weight = gu[...].reshape(-1, columns)
-    both = jnp.dot(mid[...], weight, preferred_element_type=f32)
-    gate = both[:, : main + 128]
-    upper = jnp.concatenate([both[:, main + 128 :], pltpu.roll(both[:, main : main + 128], 64, 1)], axis=1)
-    grad = lax.dot_general(cotangent[...], wd[...], (((1,), (1,)), ((), ())), preferred_element_type=f32)
-    sigmoid = 1.0 / (1.0 + jnp.exp(-gate))
-    silu = gate * sigmoid
-    hid = (silu * upper).astype(bf16)
-    hidden[...] = hid[:, :units]
-    final_parts[...] = jnp.dot(hid, wd[...], preferred_element_type=f32).astype(bf16)
-    grad_gate = grad * upper * sigmoid * (1.0 + gate * (1.0 - sigmoid))
-    grad_upper = grad * silu
-    joint = grad_gate[:, main:] + pltpu.roll(grad_upper[:, main:], 64, 1)
-    out = jnp.concatenate([grad_gate[:, :main], joint, grad_upper[:, :main]], axis=1).astype(bf16)
-    grads[...] = out
-    mid_parts[...] = lax.dot_general(out, weight, (((1,), (1,)), ((), ())), preferred_element_type=f32).astype(bf16)
-
-
-def feed(mid, cotangent, gu_zero, gu_one, down, block=384):
-    tokens, width = mid.shape
+        for move in moves:
+            move.start()
+        return moves
+
+    moves = [load(0)]
+    greet(LINKS)
+    wd[units:] = jnp.zeros((wd.shape[0] - units, wd.shape[1]), bf16)
+    landed(copies)
+    give, arrive, steps, finish = plane_reduce(
+        wire, staged, normed_grad, staged.at[:, :, 0], from_c, s1, r1, s2, r2, routes(rows, 4, 2), load=False
+    )
+    weight = lambda: gu[...].reshape(-1, gu.shape[4])
+    stores = []
+    for n, k in enumerate(ARRIVAL):
+        landed(moves[n])
+        if n < 3:
+            moves.append(load(n + 1))
+        if n > 1:
+            landed(stores[n - 2])
+        slot = n % 2
+        both = jnp.dot(mid_v[slot].reshape(block, -1), weight(), preferred_element_type=f32)
+        if n > 0:
+            arrive(ARRIVAL[n - 1])
+        if n > 2:
+            do(steps)
+        gate = both[:, : main + 128]
+        upper = jnp.concatenate([both[:, main + 128 :], pltpu.roll(both[:, main : main + 128], 64, 1)], axis=1)
+        cotangent = cot_v[slot].reshape(block, -1)
+        grad = lax.dot_general(cotangent, wd[...], (((1,), (1,)), ((), ())), preferred_element_type=f32)
+        sigmoid = 1.0 / (1.0 + jnp.exp(-gate))
+        silu = gate * sigmoid
+        hid = (silu * upper).astype(bf16)
+        hid_v[slot] = hid[:, :units]
+        grad_gate = grad * upper * sigmoid * (1.0 + gate * (1.0 - sigmoid))
+        grad_upper = grad * silu
+        joint = grad_gate[:, main:] + pltpu.roll(grad_upper[:, main:], 64, 1)
+        out = jnp.concatenate([grad_gate[:, :main], joint, grad_upper[:, :main]], axis=1).astype(bf16)
+        grads_v[slot] = out
+        mid_grad = lax.dot_general(out, weight(), (((1,), (1,)), ((), ())), preferred_element_type=f32)
+        staged[k] = mid_grad.astype(bf16).reshape(2, rows, -1)
+        give(k)
+        final_v[slot] = jnp.dot(hid, wd[...], preferred_element_type=f32).astype(bf16)
+        stores.append(store(n))
+    arrive((0, 0))
+    finish()
+    landed(stores[2] + stores[3])
+    wire.close()
+
+
+def feed(mid, cotangents, gu_zero, gu_one, down):
+    rows, width = mid.shape[3:]
+    count = 8 * rows
     columns = gu_zero.shape[-1]
     units = 4 * down.shape[2]
     padded = (units + 127) // 128 * 128
-    by_block = lambda n: pl.BlockSpec((block, n), lambda i: (i, 0))
-    return pl.pallas_call(
-        feed_kernel,
-        grid=(tokens // block,),
-        in_specs=[by_block(width), by_block(width), ANY, ANY, ANY],
-        out_specs=[by_block(units), by_block(columns), by_block(width), by_block(width)],
-        out_shape=[shaped((tokens, units)), shaped((tokens, columns)), shaped((tokens, width)), shaped((tokens, width))],
-        scratch_shapes=[
-            pltpu.VMEM((2, 2, 2) + gu_zero.shape[2:], bf16),
-            pltpu.VMEM((padded, width), bf16),
-            pltpu.SemaphoreType.DMA((6,)),
-        ],
-        compiler_params=pltpu.CompilerParams(vmem_limit_bytes=56 * 1024 * 1024),
-        cost_estimate=pl.CostEstimate(flops=12 * tokens * width * units, bytes_accessed=40_000_000, transcendentals=0),
-        name="feed",
-    )(mid, cotangent, gu_zero, gu_one, down)
+    block = 2 * rows
+    outs = [shaped((count, units)), shaped((count, columns)), shaped((count, width)), shaped((rows, width), f32)]
+    scratch = [
+        pltpu.VMEM((2, 2, 2) + gu_one.shape[2:], bf16),
+        pltpu.VMEM((padded, width), bf16),
+        pltpu.VMEM((2, 2, rows, width), bf16),
+        pltpu.VMEM((2, 2, rows, width), bf16),
+        pltpu.VMEM((2, block, units), bf16),
+        pltpu.VMEM((2, block, columns), bf16),
+        pltpu.VMEM((2, block, width), bf16),
+        pltpu.VMEM((2, 2, 2, rows, width), bf16),
+    ]
+    scratch += reduce_scratch(rows, width)[1:]
+    scratch += [pltpu.SemaphoreType.DMA((6,)), pltpu.SemaphoreType.DMA((4,)), pltpu.SemaphoreType.DMA((6,))]
+    return moving(
+        feed_kernel, 4, outs, (mid, cotangents, gu_zero, gu_one, down), scratch + wires(30, 2),
+        out_specs=[ANY, ANY, ANY, VMEM],
+        limit=62,
+    )
 
 
 def fold_y(wire, source, recv, passed, kept):
@@ -1052,6 +1141,30 @@
     return finish
 
 
+def hand_back_halves(wire, own, out):
+    y, x, h, l, c = coordinates()
+    rank = x * 4 + l * 2 + c
+    sent = {j: wire.later(own(flip(rank, j)), out.at[rank], PLANE[j - 1]) for j in range(1, 8)}
+    mine = wire.later_local(own(rank), out.at[rank])
+
+    def start(target):
+        for side in (0, 1):
+
+            @pl.when(x == side)
+            def _(side=side):
+                for j in range(1, 8):
+                    if side ^ (j // 4) == target:
+                        sent[j].start()
+                if side == target:
+                    mine.start()
+
+    def finish():
+        mine.wait()
+        arrived(sent.values())
+
+    return lambda: start(0), lambda: start(1), finish
+
+
 def norm_back(value, gain, grad):
     scale = row_scale(value)
     weighted = gain * grad
@@ -1064,46 +1177,23 @@
 
 
 def branch_kernel(
-    parts, middle, cotangent, gain, mid, hidden, gu_grads, cotangents,
-    grad_middle, gain_grad, plane_branch, down_out, gu_passed, gu_kept, gu_one,
-    kept, from_c, s1, r1, s2, r2, normed_grad, branch, wd_grad, wd_recv, wd_passed, wd_kept, wd_far, gu_zero, gu_recv,
-    mid_v, hidden_v, gu_v, cotangents_v, load_sem, send_sem, recv_sem, local_sem,
+    normed_grad, final_parts, middle, cotangent, gain, mid, hidden, gu_grads, cotangents,
+    grad_middle, gain_grad, plane_branch, output, down_out, gu_passed, gu_kept, gu_one,
+    kept, from_c, s1, r1, s2, r2, total, branch, wd_grad, wd_recv, wd_passed, wd_kept, wd_far, gu_zero, gu_recv,
+    hidden_v, gu_v, tokens_v, load_sem, send_sem, recv_sem, local_sem,
 ):
     wire = Wire(send_sem, recv_sem, local_sem)
     loads = [
         pltpu.make_async_copy(source, target, load_sem.at[k])
         for k, (source, target) in enumerate(
-            ((hidden, hidden_v), (cotangents, cotangents_v), (gu_grads, gu_v), (mid, mid_v))
+            ((hidden, hidden_v), (cotangents, tokens_v), (gu_grads, gu_v), (mid, tokens_v))
         )
     ]
+    for load in loads[:3]:
+        load.start()
     greet(LINKS)
     size = middle.shape[0]
-    give, arrive, steps, finish = plane_reduce(
-        wire, parts, normed_grad, kept, from_c, s1, r1, s2, r2, routes(size, 4, 3)
-    )
-    each(give)
-    for load in loads:
-        load.start()
-    each(arrive)
-    landed(loads[:2])
-    down_rows = wd_grad.shape[2]
-    for k in range(4):
-        wd_grad[k // 2, k % 2] = over_tokens(hidden_v[:, k * down_rows : (k + 1) * down_rows], cotangents_v[...])
-    down_passed, down_kept = fold_y(wire, lambda yy, hh: wd_grad.at[yy, hh], wd_recv, wd_passed, wd_kept)
-    landed(loads[2:])
-    gu_rows = gu_one.shape[2]
-
-    def columns(yy, xx, hh):
-        start = (yy * 4 + xx * 2 + hh) * gu_rows
-        return over_tokens(mid_v[:, start : start + gu_rows], gu_v[...])
-
-    for k in range(4):
-        gu_zero[k // 2, k % 2] = columns(k // 2, 0, k % 2)
-        steps[k]()
-    down_passed()
-    down_h = fold_h(wire, wd_passed, wd_kept, wd_far, down_out)
     gain_grad[...] = jnp.zeros_like(gain_grad)
-    finish()
 
     def norm(r):
         inner, outer = norm_back(middle[r], gain[...], normed_grad[r])
@@ -1113,19 +1203,48 @@
         gain_grad[...] += jnp.sum(outer, axis=0, keepdims=True)
 
     each_rows(size, norm)
-    steps, finish = plane_gather(wire, branch, plane_branch, plane_branch.at[0, 0, 0], routes(size, 4, 2))
+    passing, gathered = plane_gather(wire, branch, plane_branch, plane_branch.at[0, 0, 0], routes(size, 4, 2))
+    give, arrive, steps, finish = plane_reduce(
+        wire, final_parts, total, kept, from_c, s1, r1, s2, r2, routes(size, 4, 3)
+    )
+    each(give)
+    landed(loads[:2])
+    down_rows = wd_grad.shape[2]
+    for k in range(4):
+        wd_grad[k // 2, k % 2] = over_tokens(hidden_v[:, k * down_rows : (k + 1) * down_rows], tokens_v[...])
+    down_passed, down_kept = fold_y(wire, lambda yy, hh: wd_grad.at[yy, hh], wd_recv, wd_passed, wd_kept)
+    loads[3].start()
+    each(arrive)
+    landed(loads[2:])
+    gu_rows = gu_one.shape[2]
+
+    def columns(yy, xx, hh):
+        start = (yy * 4 + xx * 2 + hh) * gu_rows
+        return over_tokens(tokens_v[:, start : start + gu_rows], gu_v[...])
+
+    for k in range(4):
+        gu_zero[k // 2, k % 2] = columns(k // 2, 0, k % 2)
+        passing[k]()
     gu_sums = fold_y(wire, lambda yy, hh: gu_zero.at[yy, hh], gu_recv, gu_passed, gu_kept)
+    down_passed()
+    down_h = fold_h(wire, wd_passed, wd_kept, wd_far, down_out)
     for k in range(4):
+        steps[k]()
         gu_one[k // 2, k % 2] = columns(k // 2, 1, k % 2)
-        steps[k]()
+    gathered()
+    finish()
+
+    def emit(r):
+        output[r] = (middle[r] + total[r]).astype(bf16)
+
+    each_rows(size, emit)
     down_kept()
-    finish()
     do(gu_sums)
     down_h()
     wire.close()
 
 
-def branch_step(parts, middle, cotangent, gain, mid, hidden, gu_grads, cotangents):
+def branch_step(normed_grad, final_parts, middle, cotangent, gain, mid, hidden, gu_grads, cotangents):
     rows, width = middle.shape
     columns = gu_grads.shape[1]
     down = (hidden.shape[1] // 4, width)
@@ -1133,7 +1252,8 @@
     outs = [
         shaped((rows, width), f32),
         shaped((1, width), f32),
-        shaped(parts.shape),
+        shaped(final_parts.shape),
+        shaped((rows, width)),
         shaped(down, f32),
         shaped(gu),
         shaped(gu),
@@ -1142,21 +1262,21 @@
     scratch = reduce_scratch(rows, width) + [pltpu.VMEM((rows, width), f32), pltpu.VMEM((rows, width), bf16)]
     scratch += [pltpu.VMEM((2, 2) + down, bf16), pltpu.VMEM((2,) + down, bf16)] + [pltpu.VMEM(down, bf16)] * 3
     scratch += [pltpu.VMEM((2, 2) + gu, bf16), pltpu.VMEM((2,) + gu, bf16)]
-    scratch += [pltpu.VMEM(v.shape, bf16) for v in (mid, hidden, gu_grads, cotangents)]
-    operands = (parts, middle, cotangent, gain, mid, hidden, gu_grads, cotangents)
+    scratch += [pltpu.VMEM(v.shape, bf16) for v in (hidden, gu_grads, mid)]
+    operands = (normed_grad, final_parts, middle, cotangent, gain, mid, hidden, gu_grads, cotangents)
     return moving(
-        branch_kernel, 4, outs, operands, scratch + [pltpu.SemaphoreType.DMA((4,))] + wires(60, 16),
-        in_specs=[ANY, VMEM, VMEM, VMEM, ANY, ANY, ANY, ANY],
-        out_specs=[VMEM, VMEM, ANY, VMEM, VMEM, VMEM, VMEM],
+        branch_kernel, 5, outs, operands, scratch + [pltpu.SemaphoreType.DMA((4,))] + wires(60, 16),
+        in_specs=[VMEM, ANY, VMEM, VMEM, VMEM, ANY, ANY, ANY, ANY],
+        out_specs=[VMEM, VMEM, ANY, VMEM, VMEM, VMEM, VMEM, VMEM],
         limit=62,
     )
 
 
 def attend_back_kernel(
     plane_set, plane_branch, queries, attended, lse, wq, wo, cosine, sine, key_index, query_index, first_index,
-    final_parts, middle, gu_passed, gu_kept, gu_one,
-    query_grad, parts, output, gu_out, gu_passed_next, gu_kept_next,
-    kv, branch, staged, grad_keys, grad_values, kept, from_c, s1, r1, s2, r2, total, gu_recv, gu_recv_y, mask,
+    gu_passed, gu_kept, gu_one,
+    query_grad, back, gu_out, gu_passed_next, gu_kept_next, o_passed, o_kept,
+    kv, branch, out_grad, heads, o_recv, staged, grad_keys, grad_values, from_c, s1, r1, s2, r2, gu_recv, gu_recv_y, mask,
     load_sem, send_sem, recv_sem, local_sem,
 ):
     wire = Wire(send_sem, recv_sem, local_sem)
@@ -1166,36 +1286,32 @@
     load_kv = pltpu.make_async_copy(plane_set.at[:, :, :, :, pl.ds(rank_dim, 4 * HEAD_DIM)], kv, load_sem.at[0])
     load_kv.start()
 
-    def load_branch(k):
-        return pltpu.make_async_copy(plane_branch.at[k // 2, k % 2], branch.at[k % 2], load_sem.at[1 + k % 2])
-
-    load_branch(0).start()
+    loads = [pltpu.make_async_copy(plane_branch.at[k], branch.at[k], load_sem.at[1 + n]) for n, k in enumerate(ARRIVAL)]
+    for load in loads:
+        load.start()
     greet(LINKS)
-    give, arrive, passing, finish = plane_reduce(
-        wire, final_parts, total, kept, from_c, s1, r1, s2, r2, routes(middle.shape[0], 4, 3)
-    )
-    each(give)
     gu_h = fold_h(wire, gu_passed, gu_kept, gu_recv, gu_out)
     gu_sums = fold_y(wire, lambda yy, hh: gu_one.at[yy, hh], gu_recv_y, gu_passed_next, gu_kept_next)
+    buffers = (staged, back, staged.at[:, :, 0], from_c, s1, r1, s2, r2)
+
+    def of(columns):
+        every = slice(None)
+        return [ref.at[(every,) * (len(ref.shape) - 1) + (columns,)] for ref in buffers]
+
+    normed_sum = plane_reduce(wire, *of(pl.ds(0, rank_dim)), routes(rows, 2, 1), load=False)
+    kv_sum = plane_reduce(wire, *of(pl.ds(rank_dim, 4 * HEAD_DIM)), routes(rows, 2, 1), load=False)
     load_kv.wait()
-    def one(k):
-        g = k // 2
-        i = k % 2
-        load_branch(k).wait()
-
-        @pl.when(k < 3)
-        def _():
-            load_branch(k + 1).start()
-
-        @pl.when(i == 0)
-        def _():
+
+    def one(n):
+        g, i = ARRIVAL[n]
+        if n < 2:
+            loads[n].wait()
+        if n % 2 == 0:
             grad_keys[...] = jnp.zeros_like(grad_keys)
             grad_values[...] = jnp.zeros_like(grad_values)
-
-        start = pl.multiple_of(k * block, block)
-        place = pl.ds(start, block)
+        place = pl.ds((g * 2 + i) * block, block)
         grads = lax.dot_general(
-            branch[i].reshape(block, -1), wo[...], (((1,), (1,)), ((), ())), preferred_element_type=f32
+            branch[g, i].reshape(block, -1), wo[...], (((1,), (1,)), ((), ())), preferred_element_type=f32
         ).astype(bf16)
         keys = jnp.concatenate(
             [kv[g, :, :, :, :HEAD_DIM].reshape(2 * block, HEAD_DIM), kv[g, :, :, :, 2 * HEAD_DIM : 3 * HEAD_DIM].reshape(2 * block, HEAD_DIM)]
@@ -1226,137 +1342,133 @@
         query_grad[place] = query_sum
         normed = lax.dot_general(query_sum, wq[...], (((1,), (1,)), ((), ())), preferred_element_type=f32)
         staged[g, i, :, :, :rank_dim] = normed.astype(bf16).reshape(2, rows, rank_dim)
-
-        @pl.when(i == 1)
-        def _():
+        if n % 2 == 1:
             for number, (source, side) in enumerate(
                 ((grad_keys, 0), (grad_values, 0), (grad_keys, 1), (grad_values, 1))
             ):
                 column = rank_dim + number * HEAD_DIM
                 half = source[side * 2 * block : (side + 1) * 2 * block].astype(bf16)
                 staged[g, :, :, :, column : column + HEAD_DIM] = half.reshape(2, 2, rows, HEAD_DIM)
-            pltpu.make_async_copy(staged.at[g], parts.at[g], load_sem.at[3 + g]).start()
-
-    def steps(a, b):
-        @pl.loop(a, b)
-        def _(k):
-            one(k)
-
-    each(arrive)
-    steps(0, 1)
-    do(passing[:1])
-    steps(1, 2)
-    do(passing[1:3])
-    steps(2, 3)
-    do(passing[3:])
+
+    one(0)
+    normed_sum[0](ARRIVAL[0])
+    one(1)
+    kv_sum[0](ARRIVAL[0])
+    kv_sum[0](ARRIVAL[1])
+    normed_sum[0](ARRIVAL[1])
+    normed_sum[1](ARRIVAL[0])
+    kv_sum[1](ARRIVAL[0])
+    kv_sum[1](ARRIVAL[1])
+    normed_sum[1](ARRIVAL[1])
+    landed(loads[2:])
+    y, x, h, l, c = coordinates()
+    head_rows = out_grad.shape[2]
+    for k in range(4):
+        part = attended[:, k * head_rows : (k + 1) * head_rows]
+        out_grad[k // 2, k % 2] = over_tokens(part, branch[...].reshape(8 * rows, -1))
+    swapped = wire.send(out_grad.at[:, 1 - c], heads.at[:, c], 1)
+    stayed = wire.local(out_grad.at[:, c], heads.at[:, c])
+    one(2)
+    normed_sum[0](ARRIVAL[2])
+    stayed.wait()
+    swapped.wait_recv()
+    o_sums = fold_y(wire, lambda yy, hh: heads.at[yy, hh], o_recv, o_passed, o_kept)
     gu_h()
-    steps(3, 4)
-    finish()
-
-    def emit(r):
-        output[r] = (middle[r] + total[r]).astype(bf16)
-
-    each_rows(output.shape[0], emit)
-    for g in range(2):
-        pltpu.make_async_copy(staged.at[g], parts.at[g], load_sem.at[3 + g]).wait()
+    one(3)
+    kv_sum[0](ARRIVAL[2])
+    kv_sum[0](ARRIVAL[3])
+    normed_sum[0](ARRIVAL[3])
+    kv_sum[1](ARRIVAL[2])
+    normed_sum[1](ARRIVAL[2])
+    kv_sum[1](ARRIVAL[3])
+    normed_sum[1](ARRIVAL[3])
+    do(kv_sum[2])
+    do(normed_sum[2])
     do(gu_sums)
+    do(o_sums)
+    kv_sum[3]()
+    normed_sum[3]()
     wire.close()
 
 
 def attend_back(
     plane_set, plane_branch, queries, attended, lse, wq, wo, cosine, sine, key_index, query_index, first_index,
-    final_parts, middle, gu_passed, gu_kept, gu_one,
+    gu_passed, gu_kept, gu_one,
 ):
-    rows, width = middle.shape
+    rows = plane_set.shape[3]
     tokens = 8 * rows
     gu = gu_passed.shape
+    width = wq.shape[0] + 4 * HEAD_DIM
+    heads = (wo.shape[0] // 4, wo.shape[1])
     outs = [
         shaped((tokens, 2 * HEAD_DIM)),
-        shaped((2, 2, 2, rows, wq.shape[0] + 4 * HEAD_DIM)),
-        shaped((rows, width)),
+        shaped((rows, width), f32),
         shaped(gu),
         shaped(gu),
         shaped(gu),
+        shaped(heads),
+        shaped(heads),
     ]
     scratch = [
         pltpu.VMEM((2, 2, 2, rows, 4 * HEAD_DIM), bf16),
-        pltpu.VMEM((2, 2, rows, width), bf16),
-        pltpu.VMEM((2, 2, 2, rows, wq.shape[0] + 4 * HEAD_DIM), bf16),
+        pltpu.VMEM((2, 2, 2, rows, wo.shape[1]), bf16),
+        pltpu.VMEM((2, 2) + heads, bf16),
+        pltpu.VMEM((2, 2) + heads, bf16),
+        pltpu.VMEM((2,) + heads, bf16),
+        pltpu.VMEM((2, 2, 2, rows, width), bf16),
         pltpu.VMEM((8 * rows, HEAD_DIM), f32),
         pltpu.VMEM((8 * rows, HEAD_DIM), f32),
     ]
-    scratch += reduce_scratch(rows, width) + [pltpu.VMEM((rows, width), f32), pltpu.VMEM(gu, bf16)]
+    scratch += reduce_scratch(rows, width)[1:] + [pltpu.VMEM(gu, bf16)]
     scratch += [pltpu.VMEM((2,) + gu, bf16), pltpu.VMEM((tokens, 2 * rows), f32), pltpu.SemaphoreType.DMA((5,))]
     operands = (
         plane_set, plane_branch, queries, attended, lse, wq, wo, cosine, sine, key_index, query_index, first_index,
-        final_parts, middle, gu_passed, gu_kept, gu_one,
+        gu_passed, gu_kept, gu_one,
     )
     return moving(
-        attend_back_kernel, 5, outs, operands, scratch + wires(60, 12),
-        in_specs=[ANY, ANY] + [VMEM] * 10 + [ANY, VMEM, ANY, VMEM, VMEM],
-        out_specs=[VMEM, ANY, VMEM, VMEM, VMEM, VMEM],
+        attend_back_kernel, 6, outs, operands, scratch + wires(60, 12),
+        in_specs=[ANY, ANY] + [VMEM] * 10 + [ANY, VMEM, VMEM],
+        out_specs=[VMEM] * 7,
         limit=62,
     )
 
 
 def tail_kernel(
-    parts, normed, compressed, tokens, grad_middle, first_weight, gain_in, gain_q, gain_mid_grad, cosine, sine,
-    gu_total, gu_passed, gu_kept, up_grad, out_grad,
+    back, normed, compressed, tokens, grad_middle, first_weight, gain_in, gain_q, gain_mid_grad, cosine, sine,
+    gu_total, gu_passed, gu_kept, o_passed, o_kept, plane_set, query_grad,
     grad_tokens, down_out, key_out, value_out, gains_out, gate_out, up_out, q_up_out, out_out,
-    kept, from_c, s1, r1, s2, r2, back, kv_send, kv_recv, weight, mixed, normed_grad, gain_rows,
+    total, up_grad, normed_v, kv_send, kv_recv, mixed, normed_grad, gain_rows,
     blocks, acc, recv, core, gains, gains_recv,
-    gu_far, gu_own, gu_back, gu_wide, up_recv, up_passed, up_kept, up_far, up_own, up_back,
-    heads, o_recv, o_passed, o_kept, o_far,
+    gu_far, gu_back, gu_wide, up_recv, up_passed, up_kept, up_far, up_own, up_back,
+    o_far,
     send_sem, recv_sem, local_sem,
 ):
     y, x, h, l, c = coordinates()
     own = dict(zip("yxhlc", (y, x, h, l, c)))
     every = slice(None)
     wire = Wire(send_sem, recv_sem, local_sem)
-    load = wire.local(first_weight, weight)
-    greet([16, 4] + PLANE)
     rows = back.shape[0]
     rank_dim = compressed.shape[1]
     split = rank_dim + 2 * HEAD_DIM
-    buffers = (parts, back, kept, from_c, s1, r1, s2, r2)
-    of = lambda columns: [ref.at[(every,) * (len(ref.shape) - 1) + (columns,)] for ref in buffers]
-    far_columns = pl.ds(split, back.shape[1] - split)
-    far_give, far_arrive, far_steps, far_finish = plane_reduce(wire, *of(far_columns), routes(rows, 2, 1))
-    give, arrive, steps, finish = plane_reduce(wire, *of(pl.ds(0, split)), routes(rows, 4, 3))
-    each(far_give)
-    each(give)
-    each(far_arrive)
-    gu_h = fold_h(wire, gu_passed, gu_kept, gu_far, gu_own)
-    swapped = wire.send(out_grad.at[:, 1 - c], heads.at[:, c], 1)
-    stayed = wire.local(out_grad.at[:, c], heads.at[:, c])
-    each(arrive)
-    stayed.wait()
-    swapped.wait_recv()
-    o_sums = fold_y(wire, lambda yy, hh: heads.at[yy, hh], o_recv, o_passed, o_kept)
-    up_sums = [
-        fold_y(wire, lambda yy, hh, k=k: up_grad.at[yy, k, hh], up_recv.at[k], up_passed.at[k], up_kept.at[k])
-        for k in range(2)
-    ]
-    do(far_steps)
-    far_finish()
+    load_normed = wire.local(plane_set.at[:, :, :, :, pl.ds(0, rank_dim)], normed_v)
     kv_send[...] = back[:, split:].astype(bf16)
+    greet([16, 4] + PLANE)
     far = wire.send(kv_send, kv_recv, 4)
-    do(steps)
-    finish()
+    gu_first = wire.local(gu_total, gu_wide.at[0])
+    gu_first.wait()
+    piece_rows = gu_back.shape[2]
+    gu_piece = lambda k: gu_wide.at[k // 4, pl.ds(pl.multiple_of((k % 4) * piece_rows, piece_rows), piece_rows)]
+    gu_begin, gu_rest, gu_done = hand_back_halves(wire, gu_piece, gu_back.at[0])
+    gu_begin()
     inner, outer = norm_back(compressed[...], gain_q[...], back[:, :rank_dim])
     mixed[:, :rank_dim] = inner.astype(bf16)
     gain_rows[1:2, :rank_dim] = jnp.sum(outer, axis=0, keepdims=True)
     gain_rows[2:3, :] = gain_mid_grad[...]
-    gu_h()
-    piece_rows = gu_back.shape[2]
-    piece = lambda k: pl.ds(pl.multiple_of((k % 4) * piece_rows, piece_rows), piece_rows)
-
-    both = [wire.local(gu_total, gu_wide.at[0]), wire.local(gu_own, gu_wide.at[1])]
-    landed(both)
-    gu_done = hand_back(wire, lambda k: gu_wide.at[k // 4, piece(k)], gu_back.at[0])
     far.wait_recv()
+    gu_h = fold_h(wire, gu_passed, gu_kept, gu_far, gu_wide.at[1])
+    o_h = fold_h(wire, o_passed, o_kept, o_far, out_out)
     kv = back[:, rank_dim:split] + kv_recv[...].astype(f32)
-    mixed[:, rank_dim : rank_dim + HEAD_DIM] = turned(kv[:, :HEAD_DIM], cosine[...], sine[...], -1.0).astype(bf16)
+    mixed[:, rank_dim : rank_dim + HEAD_DIM] = turned(kv[:, :HEAD_DIM], cosine[:rows], sine[:rows], -1.0).astype(bf16)
     mixed[:, rank_dim + HEAD_DIM :] = kv[:, HEAD_DIM:].astype(bf16)
     size = normed.shape[1] // 8
     cores = []
@@ -1367,11 +1479,6 @@
         )
         blocks[at] = grad.astype(bf16).reshape(blocks.shape[3:])
         cores.append(wire.send(blocks.at[at + (every, 1 - c)], core.at[at], 1))
-    do(o_sums)
-    o_h = fold_h(wire, o_passed, o_kept, o_far, out_out)
-    for k in range(2):
-        do(up_sums[k])
-    up_h = [fold_h(wire, up_passed.at[k], up_kept.at[k], up_far.at[k], up_own.at[k]) for k in range(2)]
     span = blocks.shape[5]
     width = blocks.shape[6]
     columns = thirds(width)
@@ -1412,8 +1519,21 @@
             over({bit: 1 - own[bit] if first_side else own[bit]}, body)
             if first_side:
                 pass_on(p, 0)
-    load.wait()
-    normed_grad[...] = lax.dot_general(mixed[...], weight[...], (((1,), (1,)), ((), ())), preferred_element_type=f32)
+    load_normed.wait()
+    up_size = up_grad.shape[3]
+    for k in range(8):
+        tokens_part = normed_v[:, :, :, :, k * up_size : (k + 1) * up_size].reshape(8 * rows, up_size)
+        up_grad[k // 4, k // 2 % 2, k % 2] = over_tokens(tokens_part, query_grad[...])
+    up_sums = [
+        fold_y(wire, lambda yy, hh, k=k: up_grad.at[yy, k, hh], up_recv.at[k], up_passed.at[k], up_kept.at[k])
+        for k in range(2)
+    ]
+    gu_h()
+    gu_rest()
+    wire.left(cores)
+    wire.local(first_weight, blocks).wait()
+    weight = blocks[...].reshape(-1, blocks.shape[6])
+    normed_grad[...] = lax.dot_general(mixed[...], weight, (((1,), (1,)), ((), ())), preferred_element_type=f32)
     gain_rows[0:1, :] = jnp.zeros((1, gain_rows.shape[1]), f32)
 
     def norm(r):
@@ -1459,7 +1579,7 @@
                 other = tuple(1 - own[k] if k == bit else v for k, v in zip("yxhl", at))
                 value = wide(acc, at + (every, columns[p])) + wide(recv, other + (every, columns[p]))
                 if last:
-                    back[:span, columns[p]] = value
+                    total[:, columns[p]] = value
                 else:
                     acc[at + (every, columns[p])] = value.astype(bf16)
 
@@ -1476,6 +1596,10 @@
             if gain_step < 5:
                 gain_sent = pass_gains(gain_order, gain_step)
         if step == 0:
+            for k in range(2):
+                do(up_sums[k])
+            up_h = [fold_h(wire, up_passed.at[k], up_kept.at[k], up_far.at[k], up_own.at[k]) for k in range(2)]
+        if step == 1:
             for k in range(2):
                 up_h[k]()
             up_rows = up_back.shape[1]
@@ -1496,7 +1620,7 @@
                     for q in range(4):
                         n = q // 2 * 16 + source // 4 * 8 + q % 2 * 4 + source % 4
                         target[:, n * unit : (n + 1) * unit] = half[:, q * unit : (q + 1) * unit]
-        if step == 1:
+        if step == 3:
             o_h()
             up_done()
             for head in range(q_up_out.shape[1] // HEAD_DIM):
@@ -1512,24 +1636,24 @@
         if gain_step < 5:
             gain_sent = pass_gains(gain_order, gain_step)
     gains_out[...] = gains[y, x, h, l, c]
-    down_out[...] = back[:span, :rank_dim]
-    key_out[...] = back[:span, rank_dim : rank_dim + HEAD_DIM]
-    value_out[...] = back[:span, rank_dim + HEAD_DIM : split]
+    down_out[...] = total[:, :rank_dim]
+    key_out[...] = total[:, rank_dim : rank_dim + HEAD_DIM]
+    value_out[...] = total[:, rank_dim + HEAD_DIM :]
     wire.close()
 
 
 def tail(
-    parts, normed, compressed, tokens, grad_middle, first_weight, gain_in, gain_q, gain_mid_grad, cosine, sine,
-    gu_total, gu_passed, gu_kept, up_grad, out_grad,
+    back, normed, compressed, tokens, grad_middle, first_weight, gain_in, gain_q, gain_mid_grad, cosine, sine,
+    gu_total, gu_passed, gu_kept, o_passed, o_kept, plane_set, query_grad,
 ):
     rows, width = tokens.shape
     rank_dim = compressed.shape[1]
-    near = first_weight.shape[1]
+    near = first_weight.shape[-1]
     span = width // 32
     gu = gu_total.shape
     units = gu[1] * 4
-    up = up_grad.shape[3:]
-    heads = out_grad.shape[2:]
+    up = (rank_dim // 8, query_grad.shape[1])
+    heads = o_passed.shape
     outs = [
         shaped((rows, width)),
         shaped((span, rank_dim), f32),
@@ -1542,11 +1666,12 @@
         shaped(heads, f32),
     ]
     sums = (2, 2, 2, 2, span, near)
-    scratch = reduce_scratch(rows, width) + [
-        pltpu.VMEM((rows, width), f32),
+    scratch = [
+        pltpu.VMEM((span, near), f32),
+        pltpu.VMEM((2, 2, 2) + up, bf16),
+        pltpu.VMEM(plane_set.shape[:4] + (rank_dim,), bf16),
         pltpu.VMEM((rows, 2 * HEAD_DIM), bf16),
         pltpu.VMEM((rows, 2 * HEAD_DIM), bf16),
-        pltpu.VMEM(first_weight.shape, bf16),
         pltpu.VMEM((rows, near), bf16),
         pltpu.VMEM((rows, width), f32),
         pltpu.VMEM((8, width), f32),
@@ -1557,7 +1682,6 @@
         pltpu.VMEM((2, 2, 2, 2, 2, 1, 256), f32),
         pltpu.VMEM((2, 2, 2, 2, 2, 1, 256), f32),
         pltpu.VMEM(gu, bf16),
-        pltpu.VMEM(gu, bf16),
         pltpu.VMEM((1, 8, span, gu[1]), bf16),
         pltpu.VMEM((2,) + gu, bf16),
         pltpu.VMEM((2, 2) + up, bf16),
@@ -1566,29 +1690,44 @@
         pltpu.VMEM((2,) + up, bf16),
         pltpu.VMEM((2,) + up, bf16),
         pltpu.VMEM((8, up[0] // 4, up[1]), bf16),
-        pltpu.VMEM((2, 2) + heads, bf16),
-        pltpu.VMEM((2,) + heads, bf16),
-        pltpu.VMEM(heads, bf16),
-        pltpu.VMEM(heads, bf16),
         pltpu.VMEM(heads, bf16),
     ]
     operands = (
-        parts, normed, compressed, tokens, grad_middle, first_weight, gain_in, gain_q, gain_mid_grad, cosine, sine,
-        gu_total, gu_passed, gu_kept, up_grad, out_grad,
+        back, normed, compressed, tokens, grad_middle, first_weight, gain_in, gain_q, gain_mid_grad, cosine, sine,
+        gu_total, gu_passed, gu_kept, o_passed, o_kept, plane_set, query_grad,
     )
     return moving(
-        tail_kernel, 6, outs, operands, scratch + wires(100, 24),
-        in_specs=[ANY] + [VMEM] * 4 + [ANY] + [VMEM] * 5 + [ANY, ANY, VMEM, VMEM, ANY],
+        tail_kernel, 7, outs, operands, scratch + wires(100, 24),
+        in_specs=[VMEM] * 5 + [ANY] + [VMEM] * 5 + [ANY, ANY, VMEM, ANY, VMEM, ANY, VMEM],
         out_specs=[VMEM] * 9,
         limit=62,
     )
 
 
-def rope_table(places):
-    half = HEAD_DIM // 2
-    freqs = rope_base ** (-(2.0 * jnp.arange(half).astype(f32)) / HEAD_DIM)
-    angles = places.astype(f32)[:, None] * freqs[None, :]
-    return jnp.cos(angles), jnp.sin(angles)
+def finish_kernel(*refs):
+    count = (len(refs) - 2) // 3
+    loads = [pltpu.make_async_copy(refs[k], refs[2 * count + k], refs[-2].at[k]) for k in range(count)]
+    for load in loads:
+        load.start()
+    stores = []
+    for k in range(count):
+        loads[k].wait()
+        stores.append(pltpu.make_async_copy(refs[2 * count + k], refs[count + k], refs[-1].at[k]))
+        stores[-1].start()
+    landed(stores)
+
+
+def finish(arrays):
+    count = len(arrays)
+    return pl.pallas_call(
+        finish_kernel,
+        out_shape=[shaped(v.shape, v.dtype) for v in arrays],
+        in_specs=[ANY] * count,
+        out_specs=[ANY] * count,
+        scratch_shapes=[pltpu.VMEM(v.shape, v.dtype) for v in arrays] + [pltpu.SemaphoreType.DMA((count,))] * 2,
+        compiler_params=pltpu.CompilerParams(vmem_limit_bytes=62 * 1024 * 1024),
+        name="finish",
+    )(*arrays)
 
 
 def plane_local(
@@ -1609,51 +1748,42 @@
 ):
     rows, width = tokens.shape
     rank_dim = q_down.shape[1]
-    seq = lax.axis_index("seq")
-    h, l, c = seq // 4, (seq // 2) % 2, seq % 2
     span, q_span = norm_in_gain.shape[0], q_gain.shape[0]
 
     gains = jnp.concatenate([norm_in_gain, norm_mid_gain, q_gain, jnp.zeros((256 - 2 * span - q_span,), f32)])
     gains = lax.reduce_precision(gains, 8, 7).reshape(1, 256)
-    first_weight, up_query, gu_pieces, wo_own, wo_far, wd_own, in_gain, mid_gain, query_gain, places = head(
+    (
+        first_weight, up_query, gu_pieces, wo_own, wo_far, wd_own, in_gain, mid_gain, query_gain,
+        first_index, query_index, key_index, cosine, sine,
+    ) = head(
         q_down, key_proj, value_proj, gains, q_up, w_gate, w_up, out_proj, w_down, positions.reshape(1, rows)
     )
-    first_weight = first_weight.reshape(width, rank_dim + 2 * HEAD_DIM)
     up_query = up_query.reshape(rank_dim, 2 * HEAD_DIM)
 
-    blocks = jnp.arange(4, dtype=jnp.int32) ^ (l * 2 + c)
-    in_half = (blocks[:, None] * rows + jnp.arange(rows, dtype=jnp.int32)[None, :]).reshape(-1)
-    own_index = h * (4 * rows) + in_half
-    query_index = jnp.concatenate([own_index, own_index]).reshape(1, 8 * rows)
-    first_index = query_index - places
-    key_index = jnp.concatenate([own_index, (1 - h) * (4 * rows) + in_half]).reshape(8 * rows, 1)
-    cosine, sine = rope_table(places.reshape(-1))
-
     plane_set, out_weight, gu_set, wd_far, normed, compressed = pack(
-        tokens, in_gain, query_gain, first_weight, cosine[:rows], sine[:rows], wo_own, wo_far, gu_pieces, wd_own
+        tokens, in_gain, query_gain, first_weight.reshape(width, -1), cosine, sine, wo_own, wo_far, gu_pieces, wd_own
     )
     out_weight = out_weight.reshape(2 * HEAD_DIM, width)
     queries, attended, lse, middle, plane_mid, plane_cotangent, gu_zero, gu_one, down_weight = attend(
         plane_set, up_query, out_weight, cosine, sine, key_index, query_index, first_index, tokens, mid_gain, cotangent,
         gu_set, wd_own, wd_far,
     )
-    plane_mid = plane_mid.reshape(8 * rows, width)
-    plane_cotangent = plane_cotangent.reshape(8 * rows, width)
-    hidden, gu_grads, mid_parts, final_parts = feed(plane_mid, plane_cotangent, gu_zero, gu_one, down_weight)
-
-    by_plane = lambda parts: parts.reshape(2, 2, 2, rows, -1)
-    grad_middle, mid_gain_grad, plane_branch, grad_down, gu_passed, gu_kept, gu_one_grad = branch_step(
-        by_plane(mid_parts), middle, cotangent, mid_gain, plane_mid, hidden, gu_grads, plane_cotangent
-    )
-    query_grad, back_parts, output, gu_total, gu_passed, gu_kept = attend_back(
+    hidden, gu_grads, final_parts, normed_grad = feed(plane_mid, plane_cotangent, gu_zero, gu_one, down_weight)
+    flat = lambda blocks: blocks.reshape(8 * rows, -1)
+    grad_middle, mid_gain_grad, plane_branch, output, grad_down, gu_passed, gu_kept, gu_one_grad = branch_step(
+        normed_grad, final_parts.reshape(2, 2, 2, rows, width), middle, cotangent, mid_gain, flat(plane_mid), hidden,
+        gu_grads, flat(plane_cotangent),
+    )
+    query_grad, back, gu_total, gu_passed, gu_kept, o_passed, o_kept = attend_back(
         plane_set, plane_branch, queries, attended, lse, up_query, out_weight, cosine, sine,
-        key_index, query_index, first_index, by_plane(final_parts), middle, gu_passed, gu_kept, gu_one_grad,
-    )
-    out_grad = over_tokens(attended, plane_branch.reshape(8 * rows, width)).reshape(2, 2, -1, width)
-    up_grad = over_tokens(plane_set.reshape(8 * rows, -1)[:, :rank_dim], query_grad).reshape(2, 2, 2, -1, 2 * HEAD_DIM)
+        key_index, query_index, first_index, gu_passed, gu_kept, gu_one_grad,
+    )
     grad_tokens, grad_q_down, grad_key, grad_value, grad_gains, grad_gate, grad_up, grad_q_up, grad_out = tail(
-        back_parts, normed, compressed, tokens, grad_middle, first_weight, in_gain, query_gain, mid_gain_grad,
-        cosine[:rows], sine[:rows], gu_total, gu_passed, gu_kept, up_grad, out_grad,
+        back, normed, compressed, tokens, grad_middle, first_weight, in_gain, query_gain, mid_gain_grad,
+        cosine, sine, gu_total, gu_passed, gu_kept, o_passed, o_kept, plane_set, query_grad,
+    )
+    output, grad_tokens, grad_q_down, grad_q_up, grad_key, grad_value, grad_out, grad_gate, grad_up, grad_down = finish(
+        (output, grad_tokens, grad_q_down, grad_q_up, grad_key, grad_value, grad_out, grad_gate, grad_up, grad_down)
     )
     return (
         output,

time: 586 us -> 569 us (0.971)
  Pallas kernels: 546 us -> 561 us
  local copies, waits for them, and re-layouts: 15.6 us -> 1.18 us
  matrix products: 12.2 us -> 0 us
    pallas_call x6 -> x7, Pallas kernels: 509 us -> 555 us  [moving(): pl.pallas_call(kernel, out_shape=outs, in_specs=in_specs or [ANY] * len(o...]
    pallas_call x1, Pallas kernels: 37.1 us -> 6.37 us  [finish(): pl.pallas_call(finish_kernel, out_shape=[shaped(v.shape, v.dtype) for v i...]
    dot_general x2 -> x0, matrix products: 12.2 us -> none  [over_tokens(): lax.dot_general(left, right, (((0,), (0,)), ((), ())), preferred_element_...]
    unnamed x38 -> x2, local copies, waits for them, and re-layouts: 9.62 us -> 0.01 us
where the time goes in v4:
time: 569 us; the launch traced here: 564 us
  Pallas kernels  561 us (99%)
    pallas_call x7, Pallas kernels, moving(): pl.pallas_call(kernel, out_shape=outs, in_specs=in_specs or [ANY] * len(o...  555 us

profile of v4, /device:TPU:0, one launch (start us, length us, event | category | flops | bytes accessed | tf_op | source)
XLA Modules:
  0.0 564.4 jit_solution(8352547568567231953)
XLA Ops:
  0.7 0.1 pad.3.clone
  0.7 1.3 maximum_reduce-precision_fusion.gains
  2.1 66.2 %head_kernel.1 = (bf16[2,2,2,2,2,64,1536]{6,5,4,3,2,1,0:T(8,128)(2,1)}, bf16[2,2,2,128,512]{4,3,2,1,0:T(8,128)(2,1)}, bf16[8,64,1408]{2,1,0:T(8,128)(2,1)}, bf16...) custom-call(f32[64,1024]{1,0:T(8,128)} %q_down.1, ...), custom_call_target="tpu_custom_call" | custom-call | bytes 100000000 | tf_op jit(solution)/shard_map/head_kernel/pallas_call | solution.py:437
  68.2 69.7 %pack_kernel.1 = (bf16[2,2,2,192,2048]{4,3,2,1,0:T(8,128)(2,1)}, bf16[2,2,128,2048]{3,2,1,0:T(8,128)(2,1)}, bf16[2,256,1408]{2,1,0:T(8,128)(2,1)}, bf16[176,2048...) custom-call(bf16[192,2048]{1,0:T(8,128)(2,1)} %tokens.5, f32[1,2048]{1,0:T(1,128)} %get-tuple-element.80.gain_in, ...), custom_call_target="tpu_custom_call" | custom-call | bytes 100000000 | tf_op jit(solution)/shard_map/pack_kernel/pallas_call | solution.py:437
  138.0 114.3 %attend_kernel.1 = (bf16[1536,512]{1,0:T(8,128)(2,1)}, bf16[1536,512]{1,0:T(8,128)(2,1)}, f32[2,1,1536]{2,1,0:T(1,128)}, f32[192,2048]{1,0:T(8,128)}, bf16[2,2,2...) custom-call(bf16[2,2,2,192,2048]{4,3,2,1,0:T(8,128)(2,1)} %get-tuple, ...), custom_call_target="tpu_custom_call" | custom-call | bytes 100000000 | tf_op jit(solution)/shard_map/attend_kernel/pallas_call | solution.py:437
  252.3 56.4 %feed_kernel.1 = (bf16[1536,704]{1,0:T(8,128)(2,1)}, bf16[1536,1408]{1,0:T(8,128)(2,1)}, bf16[1536,2048]{1,0:T(8,128)(2,1)}, f32[192,2048]{1,0:T(8,128)}) custom-call(bf16[2,2,2,192,2048]{4,3,2,1,0:T(8,128)(2,1)} %get-tuple-element.98.mid, bf16[2,2,2,192,2048]{4,3,2,1,0:T(8,128)(2,1)} %get-tuple-element.99.cotangents, ...), custom_call_target="tpu_custom_call" | custom-call | bytes 100000000 | tf_op jit(solution)/shard_map/feed_kernel/pallas_call | solution.py:437
  308.7 79.1 %branch_kernel.1 = (f32[192,2048]{1,0:T(8,128)}, f32[1,2048]{1,0:T(1,128)}, bf16[2,2,2,192,2048]{4,3,2,1,0:T(8,128)(2,1)}, bf16[192,2048]{1,0:T(8,128)(2,1)}, f3...) custom-call(f32[192,2048]{1,0:T(8,128)} %get-tuple-element.103.norme, ...), custom_call_target="tpu_custom_call" | custom-call | bytes 100000000 | tf_op jit(solution)/shard_map/branch_kernel/pallas_call | solution.py:437
  387.9 66.7 %attend_back_kernel.1 = (bf16[1536,512]{1,0:T(8,128)(2,1)}, f32[192,2048]{1,0:T(8,128)}, bf16[256,1408]{1,0:T(8,128)(2,1)}, bf16[256,1408]{1,0:T(8,128)(2,1)}, b...) custom-call(bf16[2,2,2,192,2048]{4,3,2,1,0:T(8,128)(2,1)} %get-tuple-element.89.plane_set, ...), custom_call_target="tpu_custom_call" | custom-call | bytes 100000000 | tf_op jit(solution)/shard_map/attend_back_kernel/pallas_call | solution.py:437
  454.6 102.1 %tail_kernel.1 = (bf16[192,2048]{1,0:T(8,128)(2,1)}, f32[64,1024]{1,0:T(8,128)}, f32[64,256]{1,0:T(8,128)}, f32[64,256]{1,0:T(8,128)}, f32[1,256]{1,0:T(1,128)},...) custom-call(f32[192,2048]{1,0:T(8,128)} %get-tuple-element.116.back, ...), custom_call_target="tpu_custom_call" | custom-call | bytes 100000000 | tf_op jit(solution)/shard_map/tail_kernel/pallas_call | solution.py:437
  556.7 0.0 copy-start
  556.7 6.4 %finish.1 = (bf16[192,2048]{1,0:T(8,128)(2,1)}, bf16[192,2048]{1,0:T(8,128)(2,1)}, f32[64,1024]{1,0:T(8,128)}, f32[32,4096]{1,0:T(8,128)}, f32[64,256]{1,0:T(8,1...) custom-call(bf16[192,2048]{1,0:T(8,128)(2,1)} %get-tuple-element.108, ...), custom_call_target="tpu_custom_call" | custom-call | tf_op jit(solution)/shard_map/finish/pallas_call | solution.py:1722
  563.1 0.0 copy-done
  563.1 0.5 slice_bitcast_fusion.1
  563.6 0.6 slice_bitcast_fusion
  (1 shorter events, 0.0 us)
Async XLA Ops:
  556.7 6.4 %copy-start = (f32[1,256]{1,0:T(1,128)S(1)}, f32[1,256]{1,0:T(1,128)}, u32[]{:S(2)}) copy-start(f32[1,256]{1,0:T(1,128)} %get-tuple-element.138) | copy-start | bytes 3076

commit v5 on v4

--- a/solution.py
+++ b/solution.py
@@ -366,11 +366,16 @@
     return flip(lax.axis_index("dp"), mask // 8), flip(lax.axis_index("seq"), mask % 8)
 
 
+PENDING = []
+
+
 def greet(masks):
     barrier = pltpu.get_barrier_semaphore()
     for mask in masks:
         pl.semaphore_signal(barrier, inc=1, device_id=partner(mask), device_id_type=pl.DeviceIdType.MESH)
     pl.semaphore_wait(barrier, len(masks))
+    while PENDING:
+        PENDING.pop().wait()
 
 
 class Wire:
@@ -434,10 +439,27 @@
 
 
 def moving(kernel, number, outs, operands, scratch, in_specs=None, out_specs=None, limit=56):
+    in_specs = list(in_specs or [ANY] * len(operands))
+    early = [k for k, spec in enumerate(in_specs) if spec is VMEM and operands[k].size >= 1 << 14]
+    for k in early:
+        in_specs[k] = ANY
+
+    def whole(*refs):
+        refs, buffers, sems = list(refs[: -len(early) - 1]), refs[-len(early) - 1 : -1], refs[-1]
+        for n, (k, buffer) in enumerate(zip(early, buffers)):
+            copy = pltpu.make_async_copy(refs[k], buffer, sems.at[n])
+            copy.start()
+            PENDING.append(copy)
+            refs[k] = buffer
+        kernel(*refs)
+
+    if early:
+        buffers = [pltpu.VMEM(operands[k].shape, operands[k].dtype) for k in early]
+        scratch = list(scratch) + buffers + [pltpu.SemaphoreType.DMA((len(early),))]
     return pl.pallas_call(
-        kernel,
+        whole if early else kernel,
         out_shape=outs,
-        in_specs=in_specs or [ANY] * len(operands),
+        in_specs=in_specs,
         out_specs=out_specs or [ANY] * len(outs),
         scratch_shapes=scratch,
         compiler_params=pltpu.CompilerParams(
@@ -1114,6 +1136,22 @@
     return lambda: half(0, 1 - h, passed), lambda: half(1, h, kept)
 
 
+def fold_y_far(wire, source, recv, passed):
+    y, x, h, l, c = coordinates()
+    sent = wire.send(source(1 - y, 1 - h), recv, 16)
+
+    def finish():
+        sent.wait_recv()
+        mine = source(y, 1 - h)
+
+        def body(r):
+            passed[r] = (wide(mine, r) + wide(recv, r)).astype(passed.dtype)
+
+        each_rows(passed.shape[0], body)
+
+    return finish
+
+
 def fold_h(wire, passed, kept, recv, out):
     sent = wire.send(passed, recv, 4)
 
@@ -1178,9 +1216,9 @@
 
 def branch_kernel(
     normed_grad, final_parts, middle, cotangent, gain, mid, hidden, gu_grads, cotangents,
-    grad_middle, gain_grad, plane_branch, output, down_out, gu_passed, gu_kept, gu_one,
-    kept, from_c, s1, r1, s2, r2, total, branch, wd_grad, wd_recv, wd_passed, wd_kept, wd_far, gu_zero, gu_recv,
-    hidden_v, gu_v, tokens_v, load_sem, send_sem, recv_sem, local_sem,
+    grad_middle, gain_grad, plane_branch, output, down_out, gu_passed, gu_zero_out, gu_one_out,
+    kept, from_c, s1, r1, s2, r2, total, branch, wd_grad, wd_recv, wd_passed, wd_kept, wd_far, gu_recv,
+    hidden_v, gu_v, tokens_v, gu_zero, gu_one, load_sem, store_sem, send_sem, recv_sem, local_sem,
 ):
     wire = Wire(send_sem, recv_sem, local_sem)
     loads = [
@@ -1222,15 +1260,22 @@
         start = (yy * 4 + xx * 2 + hh) * gu_rows
         return over_tokens(tokens_v[:, start : start + gu_rows], gu_v[...])
 
+    stores = [
+        pltpu.make_async_copy(source.at[k // 2, k % 2], target.at[k // 2, k % 2], store_sem.at[side, k])
+        for side, (source, target) in enumerate(((gu_zero, gu_zero_out), (gu_one, gu_one_out)))
+        for k in range(4)
+    ]
     for k in range(4):
         gu_zero[k // 2, k % 2] = columns(k // 2, 0, k % 2)
+        stores[k].start()
         passing[k]()
-    gu_sums = fold_y(wire, lambda yy, hh: gu_zero.at[yy, hh], gu_recv, gu_passed, gu_kept)
+    gu_sum = fold_y_far(wire, lambda yy, hh: gu_zero.at[yy, hh], gu_recv, gu_passed)
     down_passed()
     down_h = fold_h(wire, wd_passed, wd_kept, wd_far, down_out)
     for k in range(4):
         steps[k]()
         gu_one[k // 2, k % 2] = columns(k // 2, 1, k % 2)
+        stores[4 + k].start()
     gathered()
     finish()
 
@@ -1239,8 +1284,9 @@
 
     each_rows(size, emit)
     down_kept()
-    do(gu_sums)
+    gu_sum()
     down_h()
+    landed(stores)
     wire.close()
 
 
@@ -1256,27 +1302,27 @@
         shaped((rows, width)),
         shaped(down, f32),
         shaped(gu),
-        shaped(gu),
+        shaped((2, 2) + gu),
         shaped((2, 2) + gu),
     ]
     scratch = reduce_scratch(rows, width) + [pltpu.VMEM((rows, width), f32), pltpu.VMEM((rows, width), bf16)]
     scratch += [pltpu.VMEM((2, 2) + down, bf16), pltpu.VMEM((2,) + down, bf16)] + [pltpu.VMEM(down, bf16)] * 3
-    scratch += [pltpu.VMEM((2, 2) + gu, bf16), pltpu.VMEM((2,) + gu, bf16)]
-    scratch += [pltpu.VMEM(v.shape, bf16) for v in (hidden, gu_grads, mid)]
+    scratch += [pltpu.VMEM(gu, bf16)]
+    scratch += [pltpu.VMEM(v.shape, bf16) for v in (hidden, gu_grads, mid)] + [pltpu.VMEM((2, 2) + gu, bf16)] * 2
     operands = (normed_grad, final_parts, middle, cotangent, gain, mid, hidden, gu_grads, cotangents)
     return moving(
-        branch_kernel, 5, outs, operands, scratch + [pltpu.SemaphoreType.DMA((4,))] + wires(60, 16),
+        branch_kernel, 5, outs, operands, scratch + [pltpu.SemaphoreType.DMA((4,)), pltpu.SemaphoreType.DMA((2, 4))] + wires(60, 16),
         in_specs=[VMEM, ANY, VMEM, VMEM, VMEM, ANY, ANY, ANY, ANY],
-        out_specs=[VMEM, VMEM, ANY, VMEM, VMEM, VMEM, VMEM, VMEM],
+        out_specs=[VMEM, VMEM, ANY, VMEM, VMEM, VMEM, ANY, ANY],
         limit=62,
     )
 
 
 def attend_back_kernel(
     plane_set, plane_branch, queries, attended, lse, wq, wo, cosine, sine, key_index, query_index, first_index,
-    gu_passed, gu_kept, gu_one,
-    query_grad, back, gu_out, gu_passed_next, gu_kept_next, o_passed, o_kept,
-    kv, branch, out_grad, heads, o_recv, staged, grad_keys, grad_values, from_c, s1, r1, s2, r2, gu_recv, gu_recv_y, mask,
+    gu_passed, gu_zero, gu_one,
+    query_grad, back, gu_out, gu_passed_next, gu_kept_next, heads,
+    kv, branch, out_grad, near_mine, near_recv, staged, grad_keys, grad_values, from_c, s1, r1, s2, r2, gu_recv, gu_recv_y, mask,
     load_sem, send_sem, recv_sem, local_sem,
 ):
     wire = Wire(send_sem, recv_sem, local_sem)
@@ -1290,7 +1336,10 @@
     for load in loads:
         load.start()
     greet(LINKS)
-    gu_h = fold_h(wire, gu_passed, gu_kept, gu_recv, gu_out)
+    y, x, h, l, c = coordinates()
+    far_sent = wire.send(gu_passed, gu_recv, 4)
+    near_load = wire.local(gu_zero.at[y, h], near_mine)
+    near_sent = wire.send(gu_zero.at[1 - y, h], near_recv, 16)
     gu_sums = fold_y(wire, lambda yy, hh: gu_one.at[yy, hh], gu_recv_y, gu_passed_next, gu_kept_next)
     buffers = (staged, back, staged.at[:, :, 0], from_c, s1, r1, s2, r2)
 
@@ -1361,7 +1410,6 @@
     kv_sum[1](ARRIVAL[1])
     normed_sum[1](ARRIVAL[1])
     landed(loads[2:])
-    y, x, h, l, c = coordinates()
     head_rows = out_grad.shape[2]
     for k in range(4):
         part = attended[:, k * head_rows : (k + 1) * head_rows]
@@ -1372,8 +1420,6 @@
     normed_sum[0](ARRIVAL[2])
     stayed.wait()
     swapped.wait_recv()
-    o_sums = fold_y(wire, lambda yy, hh: heads.at[yy, hh], o_recv, o_passed, o_kept)
-    gu_h()
     one(3)
     kv_sum[0](ARRIVAL[2])
     kv_sum[0](ARRIVAL[3])
@@ -1384,8 +1430,14 @@
     normed_sum[1](ARRIVAL[3])
     do(kv_sum[2])
     do(normed_sum[2])
+    near_load.wait()
+    arrived([near_sent, far_sent])
+
+    def total(r):
+        gu_out[r] = (wide(near_mine, r) + wide(near_recv, r) + wide(gu_recv, r)).astype(bf16)
+
+    each_rows(gu_out.shape[0], total)
     do(gu_sums)
-    do(o_sums)
     kv_sum[3]()
     normed_sum[3]()
     wire.close()
@@ -1393,7 +1445,7 @@
 
 def attend_back(
     plane_set, plane_branch, queries, attended, lse, wq, wo, cosine, sine, key_index, query_index, first_index,
-    gu_passed, gu_kept, gu_one,
+    gu_passed, gu_zero, gu_one,
 ):
     rows = plane_set.shape[3]
     tokens = 8 * rows
@@ -1406,15 +1458,14 @@
         shaped(gu),
         shaped(gu),
         shaped(gu),
-        shaped(heads),
-        shaped(heads),
+        shaped((2, 2) + heads),
     ]
     scratch = [
         pltpu.VMEM((2, 2, 2, rows, 4 * HEAD_DIM), bf16),
         pltpu.VMEM((2, 2, 2, rows, wo.shape[1]), bf16),
         pltpu.VMEM((2, 2) + heads, bf16),
-        pltpu.VMEM((2, 2) + heads, bf16),
-        pltpu.VMEM((2,) + heads, bf16),
+        pltpu.VMEM(gu, bf16),
+        pltpu.VMEM(gu, bf16),
         pltpu.VMEM((2, 2, 2, rows, width), bf16),
         pltpu.VMEM((8 * rows, HEAD_DIM), f32),
         pltpu.VMEM((8 * rows, HEAD_DIM), f32),
@@ -1423,24 +1474,24 @@
     scratch += [pltpu.VMEM((2,) + gu, bf16), pltpu.VMEM((tokens, 2 * rows), f32), pltpu.SemaphoreType.DMA((5,))]
     operands = (
         plane_set, plane_branch, queries, attended, lse, wq, wo, cosine, sine, key_index, query_index, first_index,
-        gu_passed, gu_kept, gu_one,
+        gu_passed, gu_zero, gu_one,
     )
     return moving(
         attend_back_kernel, 6, outs, operands, scratch + wires(60, 12),
-        in_specs=[ANY, ANY] + [VMEM] * 10 + [ANY, VMEM, VMEM],
-        out_specs=[VMEM] * 7,
+        in_specs=[ANY, ANY] + [VMEM] * 10 + [ANY, ANY, VMEM],
+        out_specs=[VMEM] * 6,
         limit=62,
     )
 
 
 def tail_kernel(
     back, normed, compressed, tokens, grad_middle, first_weight, gain_in, gain_q, gain_mid_grad, cosine, sine,
-    gu_total, gu_passed, gu_kept, o_passed, o_kept, plane_set, query_grad,
+    gu_total, gu_passed, gu_kept, heads, plane_set, query_grad,
     grad_tokens, down_out, key_out, value_out, gains_out, gate_out, up_out, q_up_out, out_out,
     total, up_grad, normed_v, kv_send, kv_recv, mixed, normed_grad, gain_rows,
     blocks, acc, recv, core, gains, gains_recv,
     gu_far, gu_back, gu_wide, up_recv, up_passed, up_kept, up_far, up_own, up_back,
-    o_far,
+    o_recv, o_passed, o_kept, o_far,
     send_sem, recv_sem, local_sem,
 ):
     y, x, h, l, c = coordinates()
@@ -1451,8 +1502,8 @@
     rank_dim = compressed.shape[1]
     split = rank_dim + 2 * HEAD_DIM
     load_normed = wire.local(plane_set.at[:, :, :, :, pl.ds(0, rank_dim)], normed_v)
+    greet([16, 4] + PLANE)
     kv_send[...] = back[:, split:].astype(bf16)
-    greet([16, 4] + PLANE)
     far = wire.send(kv_send, kv_recv, 4)
     gu_first = wire.local(gu_total, gu_wide.at[0])
     gu_first.wait()
@@ -1460,13 +1511,13 @@
     gu_piece = lambda k: gu_wide.at[k // 4, pl.ds(pl.multiple_of((k % 4) * piece_rows, piece_rows), piece_rows)]
     gu_begin, gu_rest, gu_done = hand_back_halves(wire, gu_piece, gu_back.at[0])
     gu_begin()
+    o_sums = fold_y(wire, lambda yy, hh: heads.at[yy, hh], o_recv, o_passed, o_kept)
     inner, outer = norm_back(compressed[...], gain_q[...], back[:, :rank_dim])
     mixed[:, :rank_dim] = inner.astype(bf16)
     gain_rows[1:2, :rank_dim] = jnp.sum(outer, axis=0, keepdims=True)
     gain_rows[2:3, :] = gain_mid_grad[...]
     far.wait_recv()
     gu_h = fold_h(wire, gu_passed, gu_kept, gu_far, gu_wide.at[1])
-    o_h = fold_h(wire, o_passed, o_kept, o_far, out_out)
     kv = back[:, rank_dim:split] + kv_recv[...].astype(f32)
     mixed[:, rank_dim : rank_dim + HEAD_DIM] = turned(kv[:, :HEAD_DIM], cosine[:rows], sine[:rows], -1.0).astype(bf16)
     mixed[:, rank_dim + HEAD_DIM :] = kv[:, HEAD_DIM:].astype(bf16)
@@ -1528,8 +1579,6 @@
         fold_y(wire, lambda yy, hh, k=k: up_grad.at[yy, k, hh], up_recv.at[k], up_passed.at[k], up_kept.at[k])
         for k in range(2)
     ]
-    gu_h()
-    gu_rest()
     wire.left(cores)
     wire.local(first_weight, blocks).wait()
     weight = blocks[...].reshape(-1, blocks.shape[6])
@@ -1565,6 +1614,10 @@
         mine = place({**fixed, bit: own[bit]})
         gains[mine] = gains[mine] + gains_recv[place({**fixed, bit: 1 - own[bit]})]
 
+    gu_h()
+    gu_rest()
+    do(o_sums)
+    o_h = fold_h(wire, o_passed, o_kept, o_far, out_out)
     gain_order = "cyxlh"
     gain_sent = pass_gains(gain_order, 0)
     gain_step = 0
@@ -1644,7 +1697,7 @@
 
 def tail(
     back, normed, compressed, tokens, grad_middle, first_weight, gain_in, gain_q, gain_mid_grad, cosine, sine,
-    gu_total, gu_passed, gu_kept, o_passed, o_kept, plane_set, query_grad,
+    gu_total, gu_passed, gu_kept, heads, plane_set, query_grad,
 ):
     rows, width = tokens.shape
     rank_dim = compressed.shape[1]
@@ -1653,7 +1706,7 @@
     gu = gu_total.shape
     units = gu[1] * 4
     up = (rank_dim // 8, query_grad.shape[1])
-    heads = o_passed.shape
+    out_size = heads.shape[2:]
     outs = [
         shaped((rows, width)),
         shaped((span, rank_dim), f32),
@@ -1663,7 +1716,7 @@
         shaped((span, units), f32),
         shaped((span, units), f32),
         shaped((up[0] // 4, 8 * up[1]), f32),
-        shaped(heads, f32),
+        shaped(out_size, f32),
     ]
     sums = (2, 2, 2, 2, span, near)
     scratch = [
@@ -1690,15 +1743,18 @@
         pltpu.VMEM((2,) + up, bf16),
         pltpu.VMEM((2,) + up, bf16),
         pltpu.VMEM((8, up[0] // 4, up[1]), bf16),
-        pltpu.VMEM(heads, bf16),
+        pltpu.VMEM((2,) + out_size, bf16),
+        pltpu.VMEM(out_size, bf16),
+        pltpu.VMEM(out_size, bf16),
+        pltpu.VMEM(out_size, bf16),
     ]
     operands = (
         back, normed, compressed, tokens, grad_middle, first_weight, gain_in, gain_q, gain_mid_grad, cosine, sine,
-        gu_total, gu_passed, gu_kept, o_passed, o_kept, plane_set, query_grad,
+        gu_total, gu_passed, gu_kept, heads, plane_set, query_grad,
     )
     return moving(
         tail_kernel, 7, outs, operands, scratch + wires(100, 24),
-        in_specs=[VMEM] * 5 + [ANY] + [VMEM] * 5 + [ANY, ANY, VMEM, ANY, VMEM, ANY, VMEM],
+        in_specs=[VMEM] * 5 + [ANY] + [VMEM] * 5 + [ANY, ANY, VMEM, VMEM, ANY, VMEM],
         out_specs=[VMEM] * 9,
         limit=62,
     )
@@ -1770,17 +1826,17 @@
     )
     hidden, gu_grads, final_parts, normed_grad = feed(plane_mid, plane_cotangent, gu_zero, gu_one, down_weight)
     flat = lambda blocks: blocks.reshape(8 * rows, -1)
-    grad_middle, mid_gain_grad, plane_branch, output, grad_down, gu_passed, gu_kept, gu_one_grad = branch_step(
+    grad_middle, mid_gain_grad, plane_branch, output, grad_down, gu_passed, gu_zero_grad, gu_one_grad = branch_step(
         normed_grad, final_parts.reshape(2, 2, 2, rows, width), middle, cotangent, mid_gain, flat(plane_mid), hidden,
         gu_grads, flat(plane_cotangent),
     )
-    query_grad, back, gu_total, gu_passed, gu_kept, o_passed, o_kept = attend_back(
+    query_grad, back, gu_total, gu_passed, gu_kept, out_grad = attend_back(
         plane_set, plane_branch, queries, attended, lse, up_query, out_weight, cosine, sine,
-        key_index, query_index, first_index, gu_passed, gu_kept, gu_one_grad,
+        key_index, query_index, first_index, gu_passed, gu_zero_grad, gu_one_grad,
     )
     grad_tokens, grad_q_down, grad_key, grad_value, grad_gains, grad_gate, grad_up, grad_q_up, grad_out = tail(
         back, normed, compressed, tokens, grad_middle, first_weight, in_gain, query_gain, mid_gain_grad,
-        cosine, sine, gu_total, gu_passed, gu_kept, o_passed, o_kept, plane_set, query_grad,
+        cosine, sine, gu_total, gu_passed, gu_kept, out_grad, plane_set, query_grad,
     )
     output, grad_tokens, grad_q_down, grad_q_up, grad_key, grad_value, grad_out, grad_gate, grad_up, grad_down = finish(
         (output, grad_tokens, grad_q_down, grad_q_up, grad_key, grad_value, grad_out, grad_gate, grad_up, grad_down)

time: 569 us -> 558 us (0.981)
  Pallas kernels: 561 us -> 549 us
    pallas_call x7, Pallas kernels: 555 us -> 543 us  [moving(): pl.pallas_call(whole if early else kernel, out_shape=outs, in_specs=in_sp...]
where the time goes in v5:
time: 558 us; the launch traced here: 553 us
  Pallas kernels  549 us (98%)
    pallas_call x7, Pallas kernels, moving(): pl.pallas_call(whole if early else kernel, out_shape=outs, in_specs=in_sp...  543 us

profile of v5, /device:TPU:0, one launch (start us, length us, event | category | flops | bytes accessed | tf_op | source)
XLA Modules:
  0.0 552.9 jit_solution(4612940674378892667)
XLA Ops:
  0.7 0.1 pad.3.clone
  0.7 1.3 maximum_reduce-precision_fusion.refs_3_
  2.1 63.1 %head_kernel.1 = (bf16[2,2,2,2,2,64,1536]{6,5,4,3,2,1,0:T(8,128)(2,1)}, bf16[2,2,2,128,512]{4,3,2,1,0:T(8,128)(2,1)}, bf16[8,64,1408]{2,1,0:T(8,128)(2,1)}, bf16...) custom-call(f32[64,1024]{1,0:T(8,128)} %refs_0_.2, ...), custom_call_target="tpu_custom_call" | custom-call | bytes 100000000 | tf_op jit(solution)/shard_map/head_kernel/pallas_call | solution.py:459
  65.1 67.6 %pack_kernel.1 = (bf16[2,2,2,192,2048]{4,3,2,1,0:T(8,128)(2,1)}, bf16[2,2,128,2048]{3,2,1,0:T(8,128)(2,1)}, bf16[2,256,1408]{2,1,0:T(8,128)(2,1)}, bf16[176,2048...) custom-call(bf16[192,2048]{1,0:T(8,128)(2,1)} %refs_3_.3, ...), custom_call_target="tpu_custom_call" | custom-call | bytes 100000000 | tf_op jit(solution)/shard_map/pack_kernel/pallas_call | solution.py:459
  132.8 115.7 %attend_kernel.1 = (bf16[1536,512]{1,0:T(8,128)(2,1)}, bf16[1536,512]{1,0:T(8,128)(2,1)}, f32[2,1,1536]{2,1,0:T(1,128)}, f32[192,2048]{1,0:T(8,128)}, bf16[2,2,2...) custom-call(bf16[2,2,2,192,2048]{4,3,2,1,0:T(8,128)(2,1)} %get-tuple, ...), custom_call_target="tpu_custom_call" | custom-call | bytes 100000000 | tf_op jit(solution)/shard_map/attend_kernel/pallas_call | solution.py:459
  248.5 56.8 %feed_kernel.1 = (bf16[1536,704]{1,0:T(8,128)(2,1)}, bf16[1536,1408]{1,0:T(8,128)(2,1)}, bf16[1536,2048]{1,0:T(8,128)(2,1)}, f32[192,2048]{1,0:T(8,128)}) custom-call(bf16[2,2,2,192,2048]{4,3,2,1,0:T(8,128)(2,1)} %get-tuple-element.97.mid, bf16[2,2,2,192,2048]{4,3,2,1,0:T(8,128)(2,1)} %get-tuple-element.98.cotangents, ...), custom_call_target="tpu_custom_call" | custom-call | bytes 100000000 | tf_op jit(solution)/shard_map/feed_kernel/pallas_call | solution.py:459
  305.4 76.3 %branch_kernel.1 = (f32[192,2048]{1,0:T(8,128)}, f32[1,2048]{1,0:T(1,128)}, bf16[2,2,2,192,2048]{4,3,2,1,0:T(8,128)(2,1)}, bf16[192,2048]{1,0:T(8,128)(2,1)}, f3...) custom-call(f32[192,2048]{1,0:T(8,128)} %get-tuple-element.102.refs_, ...), custom_call_target="tpu_custom_call" | custom-call | bytes 100000000 | tf_op jit(solution)/shard_map/branch_kernel/pallas_call | solution.py:459
  381.6 66.4 %attend_back_kernel.1 = (bf16[1536,512]{1,0:T(8,128)(2,1)}, f32[192,2048]{1,0:T(8,128)}, bf16[256,1408]{1,0:T(8,128)(2,1)}, bf16[256,1408]{1,0:T(8,128)(2,1)}, b...) custom-call(bf16[2,2,2,192,2048]{4,3,2,1,0:T(8,128)(2,1)} %get-tuple-element.88.refs_0_.refs_15_, ...), custom_call_target="tpu_custom_call" | custom-call | bytes 100000000 | tf_op jit(solution)/shard_map/attend_back_kernel/pallas_call | solution.py:459
  448.0 97.1 %tail_kernel.1 = (bf16[192,2048]{1,0:T(8,128)(2,1)}, f32[64,1024]{1,0:T(8,128)}, f32[64,256]{1,0:T(8,128)}, f32[64,256]{1,0:T(8,128)}, f32[1,256]{1,0:T(1,128)},...) custom-call(f32[192,2048]{1,0:T(8,128)} %get-tuple-element.115.refs_0_, ...), custom_call_target="tpu_custom_call" | custom-call | bytes 100000000 | tf_op jit(solution)/shard_map/tail_kernel/pallas_call | solution.py:459
  545.1 0.0 copy-start
  545.1 6.4 %finish.1 = (bf16[192,2048]{1,0:T(8,128)(2,1)}, bf16[192,2048]{1,0:T(8,128)(2,1)}, f32[64,1024]{1,0:T(8,128)}, f32[32,4096]{1,0:T(8,128)}, f32[64,256]{1,0:T(8,1...) custom-call(bf16[192,2048]{1,0:T(8,128)(2,1)} %get-tuple-element.107, ...), custom_call_target="tpu_custom_call" | custom-call | tf_op jit(solution)/shard_map/finish/pallas_call | solution.py:1778
  551.5 0.0 copy-done
  551.5 0.5 slice_bitcast_fusion.1
  552.0 0.6 slice_bitcast_fusion
  (1 shorter events, 0.0 us)
Async XLA Ops:
  545.1 6.4 %copy-start = (f32[1,256]{1,0:T(1,128)S(1)}, f32[1,256]{1,0:T(1,128)}, u32[]{:S(2)}) copy-start(f32[1,256]{1,0:T(1,128)} %get-tuple-element.136) | copy-start | bytes 3076

commit v6 on v5

--- a/solution.py
+++ b/solution.py
@@ -713,13 +713,6 @@
             wo_sent = wire.send(wo_out, wo_far, 4)
         if k == 3:
             five = [step(order[:3], columns, 1) for order, columns in orders]
-    up_h.wait_recv()
-    up_y += [wire.send(upq_out.at[y, :, 1 - h], upq_out.at[y, :, 1 - h], 16)]
-    gain.wait_recv()
-    gain = step("hlxy", None, 1)
-    for (order, columns), copy in zip(orders, sent):
-        copy.wait_recv()
-        five.append(last(order[:3], order[3], columns))
     place_mine.wait()
     arrived(place)
     rows = places.shape[1]
@@ -742,6 +735,13 @@
     index = jnp.concatenate(index, axis=1)
     query_index[...] = index
     first_index[...] = index - jnp.concatenate([places_out[j] for j in range(8)], axis=1)
+    up_h.wait_recv()
+    up_y += [wire.send(upq_out.at[y, :, 1 - h], upq_out.at[y, :, 1 - h], 16)]
+    gain.wait_recv()
+    gain = step("hlxy", None, 1)
+    for (order, columns), copy in zip(orders, sent):
+        copy.wait_recv()
+        five.append(last(order[:3], order[3], columns))
     gain.wait_recv()
     span, q_span = in_gain.shape[1] // 32, q_gain.shape[1] // 32
     for n in range(32):
@@ -901,7 +901,7 @@
     greet(LINKS)
     places = [lambda yy, hh: gu_zero.at[yy, hh], lambda yy, hh: gu_one.at[yy, hh]]
     passing, gathered = plane_gather(
-        wire, cotangent, cotangents, cotangents.at[0, 0, 0], routes(cotangent.shape[0], 4, 1)
+        wire, cotangent, cotangents, cotangents.at[0, 0, 0], routes(cotangent.shape[0], 4, 0)
     )
     far_sent = wire.send(gu_set.at[0], gu_far, 4)
     gu_done = [over_y(wire, ref, lambda yy, hh: wd_out.at[yy, hh], k) for k, ref in enumerate((wd_own, wd_far))]
@@ -936,7 +936,7 @@
         staged[g, i] = jnp.dot(merged, wo[...], preferred_element_type=f32).astype(bf16).reshape(2, rows, -1)
 
     give, arrive, steps, finish = plane_reduce(
-        wire, staged, middle, staged.at[:, :, 0], from_c, s1, r1, s2, r2, routes(rows, 4, 3), load=False
+        wire, staged, middle, staged.at[:, :, 0], from_c, s1, r1, s2, r2, routes(rows, 4, 4), load=False
     )
     for number, k in enumerate(ARRIVAL):
         one(*k)

time: 558 us -> 552 us (0.989)
  Pallas kernels: 549 us -> 543 us
    pallas_call x7, Pallas kernels: 543 us -> 537 us  [moving(): pl.pallas_call(whole if early else kernel, out_shape=outs, in_specs=in_sp...]
where the time goes in v6:
time: 552 us; the launch traced here: 547 us
  Pallas kernels  543 us (98%)
    pallas_call x7, Pallas kernels, moving(): pl.pallas_call(whole if early else kernel, out_shape=outs, in_specs=in_sp...  537 us

profile of v6, /device:TPU:0, one launch (start us, length us, event | category | flops | bytes accessed | tf_op | source)
XLA Modules:
  0.0 546.8 jit_solution(17304230552087436020)
XLA Ops:
  0.7 0.1 pad.3.clone
  0.7 1.3 maximum_reduce-precision_fusion.refs_3_
  2.1 62.3 %head_kernel.1 = (bf16[2,2,2,2,2,64,1536]{6,5,4,3,2,1,0:T(8,128)(2,1)}, bf16[2,2,2,128,512]{4,3,2,1,0:T(8,128)(2,1)}, bf16[8,64,1408]{2,1,0:T(8,128)(2,1)}, bf16...) custom-call(f32[64,1024]{1,0:T(8,128)} %refs_0_.2, ...), custom_call_target="tpu_custom_call" | custom-call | bytes 100000000 | tf_op jit(solution)/shard_map/head_kernel/pallas_call | solution.py:459
  64.3 68.4 %pack_kernel.1 = (bf16[2,2,2,192,2048]{4,3,2,1,0:T(8,128)(2,1)}, bf16[2,2,128,2048]{3,2,1,0:T(8,128)(2,1)}, bf16[2,256,1408]{2,1,0:T(8,128)(2,1)}, bf16[176,2048...) custom-call(bf16[192,2048]{1,0:T(8,128)(2,1)} %refs_3_.3, ...), custom_call_target="tpu_custom_call" | custom-call | bytes 100000000 | tf_op jit(solution)/shard_map/pack_kernel/pallas_call | solution.py:459
  132.8 113.0 %attend_kernel.1 = (bf16[1536,512]{1,0:T(8,128)(2,1)}, bf16[1536,512]{1,0:T(8,128)(2,1)}, f32[2,1,1536]{2,1,0:T(1,128)}, f32[192,2048]{1,0:T(8,128)}, bf16[2,2,2...) custom-call(bf16[2,2,2,192,2048]{4,3,2,1,0:T(8,128)(2,1)} %get-tuple, ...), custom_call_target="tpu_custom_call" | custom-call | bytes 100000000 | tf_op jit(solution)/shard_map/attend_kernel/pallas_call | solution.py:459
  245.8 56.6 %feed_kernel.1 = (bf16[1536,704]{1,0:T(8,128)(2,1)}, bf16[1536,1408]{1,0:T(8,128)(2,1)}, bf16[1536,2048]{1,0:T(8,128)(2,1)}, f32[192,2048]{1,0:T(8,128)}) custom-call(bf16[2,2,2,192,2048]{4,3,2,1,0:T(8,128)(2,1)} %get-tuple-element.97.mid, bf16[2,2,2,192,2048]{4,3,2,1,0:T(8,128)(2,1)} %get-tuple-element.98.cotangents, ...), custom_call_target="tpu_custom_call" | custom-call | bytes 100000000 | tf_op jit(solution)/shard_map/feed_kernel/pallas_call | solution.py:459
  302.4 75.8 %branch_kernel.1 = (f32[192,2048]{1,0:T(8,128)}, f32[1,2048]{1,0:T(1,128)}, bf16[2,2,2,192,2048]{4,3,2,1,0:T(8,128)(2,1)}, bf16[192,2048]{1,0:T(8,128)(2,1)}, f3...) custom-call(f32[192,2048]{1,0:T(8,128)} %get-tuple-element.102.refs_, ...), custom_call_target="tpu_custom_call" | custom-call | bytes 100000000 | tf_op jit(solution)/shard_map/branch_kernel/pallas_call | solution.py:459
  378.2 64.6 %attend_back_kernel.1 = (bf16[1536,512]{1,0:T(8,128)(2,1)}, f32[192,2048]{1,0:T(8,128)}, bf16[256,1408]{1,0:T(8,128)(2,1)}, bf16[256,1408]{1,0:T(8,128)(2,1)}, b...) custom-call(bf16[2,2,2,192,2048]{4,3,2,1,0:T(8,128)(2,1)} %get-tuple-element.88.refs_0_.refs_15_, ...), custom_call_target="tpu_custom_call" | custom-call | bytes 100000000 | tf_op jit(solution)/shard_map/attend_back_kernel/pallas_call | solution.py:459
  442.9 96.2 %tail_kernel.1 = (bf16[192,2048]{1,0:T(8,128)(2,1)}, f32[64,1024]{1,0:T(8,128)}, f32[64,256]{1,0:T(8,128)}, f32[64,256]{1,0:T(8,128)}, f32[1,256]{1,0:T(1,128)},...) custom-call(f32[192,2048]{1,0:T(8,128)} %get-tuple-element.115.refs_0_, ...), custom_call_target="tpu_custom_call" | custom-call | bytes 100000000 | tf_op jit(solution)/shard_map/tail_kernel/pallas_call | solution.py:459
  539.1 0.0 copy-start
  539.1 6.4 %finish.1 = (bf16[192,2048]{1,0:T(8,128)(2,1)}, bf16[192,2048]{1,0:T(8,128)(2,1)}, f32[64,1024]{1,0:T(8,128)}, f32[32,4096]{1,0:T(8,128)}, f32[64,256]{1,0:T(8,1...) custom-call(bf16[192,2048]{1,0:T(8,128)(2,1)} %get-tuple-element.107, ...), custom_call_target="tpu_custom_call" | custom-call | tf_op jit(solution)/shard_map/finish/pallas_call | solution.py:1778
  545.4 0.0 copy-done
  545.4 0.5 slice_bitcast_fusion.1
  546.0 0.6 slice_bitcast_fusion
  (1 shorter events, 0.0 us)
Async XLA Ops:
  539.1 6.4 %copy-start = (f32[1,256]{1,0:T(1,128)S(1)}, f32[1,256]{1,0:T(1,128)}, u32[]{:S(2)}) copy-start(f32[1,256]{1,0:T(1,128)} %get-tuple-element.136) | copy-start | bytes 3076
